TPU v7x, 128 devices: a whole 4x4x4 slice. The times are simulated.
128 devices in a mesh: plane: 16 (over x, z), height: 8 (over y, core).
Axes of the slice: x: 4, y: 4, z: 4, core: 2. Of those that a mesh axis runs over, the one named last changes fastest.
Arguments:
- points: bfloat16 [262144, 128], P(('plane', 'height')), may hold values from -6 to 6
- point_brick: int32 [262144, 1], P(('plane', 'height')), may hold values from 0 to 127; in each aligned block of 2048 rows (0 to 2047, 2048 to 4095, ...) at most 32 rows name the same one
- point_voxel: int32 [262144], P(('plane', 'height')), may hold values from 0 to 1023
- send_rows: int32 [16, 8, 4, 64], P('plane', 'height'), may hold values from 0 to 1023
- pair_in: int32 [16, 8, 26, 256], P('plane', 'height'), may hold values from 0 to 1280, as said below
- pair_out: int32 [16, 8, 26, 256], P('plane', 'height'), may hold values from 0 to 1024, as said below
- bev_cell: int32 [16, 8, 1024], P('plane', 'height'), may hold values from 0 to 4095
- conv_weight: bfloat16 [27, 128, 256], replicated, may hold values from -0.1875 to 0.1875
- head_weight: bfloat16 [9, 256, 128], replicated, may hold values from -0.125 to 0.125
- head_cot: bfloat16 [1024, 64, 128], P('plane'), may hold values from -0.0234375 to 0.0234375
Outputs:
- head_out: bfloat16 [1024, 64, 128], P(('plane', 'height'))
- conv_grad: float32 [27, 128, 256], replicated
- head_grad: float32 [9, 256, 128], replicated
Inputs may be any that keep to these rules, and one draw needn't show every extreme that they name: `point_brick`: in the rows of one device no brick appears more than 32 times. `pair_in`: the value 1024 + 4 * 64 names the zero row and marks a padding pair. `pair_out`: the value 1024 marks a padding pair whose result is dropped.
All inputs are finite; a program needn't handle non-finite values.
Results may differ from a plain program's by a relative error of at most 0.017.
Values may be sent and summed in bfloat16 or wider, within the bound.
No kernel may reach another device: no remote copies, remote signals or barrier semaphores. Data moves between devices by JAX's collectives and lax.ppermute only.
A program may use at most 128 MiB of HBM per device.

v0:
```python
import jax
import jax.numpy as jnp
from jax import lax
from jax.sharding import PartitionSpec as P


def from_behind(shard, axis, by):
    peers = lax.axis_size(axis)
    pairs = [(i, i + by) for i in range(peers) if 0 <= i + by < peers]
    return lax.ppermute(shard, axis, pairs)


def with_halo(block, sides, width):
    for axis, dim in sides:
        count = lax.axis_size(axis)
        forward = [(i, i + 1) for i in range(count - 1)]
        backward = [(target, source) for source, target in forward]
        low = lax.ppermute(
            lax.slice_in_dim(block, block.shape[dim] - width, None, axis=dim), axis, forward
        )
        high = lax.ppermute(lax.slice_in_dim(block, 0, width, axis=dim), axis, backward)
        block = jnp.concatenate([low, block, high], axis=dim)
    return block


def window_patches(padded, height_rows, width_cols, flipped):
    pieces = []
    for row_off in range(3):
        for col_off in range(3):
            first_row = 2 - row_off if flipped else row_off
            first_col = 2 - col_off if flipped else col_off
            pieces.append(
                padded[first_row : first_row + height_rows, first_col : first_col + width_cols]
            )
    return jnp.concatenate(pieces, axis=-1)


def silu_slope(pre_act):
    sigma = jax.nn.sigmoid(pre_act)
    return sigma * (1.0 + pre_act * (1.0 - sigma))


def plane_side(rim_rows, offset):
    return from_behind(rim_rows, "plane", offset)


def height_side(rim_rows, offset):
    return from_behind(rim_rows, "height", offset)


def match_table(wanted, table_size):
    return (wanted[:, None] == jnp.arange(table_size, dtype=jnp.int32)[None, :]).astype(
        jnp.bfloat16
    )


def sum_into(one_hot, values):
    return lax.dot_general(
        one_hot, values, (((0,), (0,)), ((), ())), preferred_element_type=jnp.float32
    )


def slot_fill(points, point_voxel, slot_ids, slot_total, voxels):
    width_rows = min(512, slot_total)
    first_slots = jnp.arange(slot_total // width_rows, dtype=jnp.int32) * width_rows

    def fill_step(carried, first_slot):
        wanted = first_slot + jnp.arange(width_rows, dtype=jnp.int32)
        matches = slot_ids[:, None] == wanted[None, :]
        filled_rows = sum_into(matches.astype(jnp.bfloat16), points).astype(jnp.bfloat16)
        voxel_sum = jnp.sum(jnp.where(matches, point_voxel[:, None], 0), axis=0)
        filled_voxel = jnp.where(jnp.any(matches, axis=0), voxel_sum, voxels)
        return (carried, (filled_rows, filled_voxel))

    unused, (send_feat, send_vox) = lax.scan(fill_step, jnp.zeros((), jnp.int32), first_slots)
    return (send_feat.reshape(slot_total, points.shape[1]), send_vox.reshape(slot_total))


def pool_points(feature_rows, voxel_ids, voxels):
    total_rows = feature_rows.shape[0]
    width_rows = min(512, total_rows)
    count_blocks = total_rows // width_rows
    channels = feature_rows.shape[1]

    def pool_step(running, members):
        block_feat, block_voxel = members
        return (running + sum_into(match_table(block_voxel, voxels), block_feat), None)

    pooled, unused = lax.scan(
        pool_step,
        jnp.zeros((voxels, channels), jnp.float32),
        (
            feature_rows.reshape(count_blocks, width_rows, channels),
            voxel_ids.reshape(count_blocks, width_rows),
        ),
    )
    return pooled


def column_sums(activated, bev_cells, cell_total):
    voxels = activated.shape[0]
    width_rows = min(512, voxels)
    count_blocks = voxels // width_rows
    channels = activated.shape[1]

    def column_step(running, members):
        block_act, block_cells = members
        return (running + sum_into(match_table(block_cells, cell_total), block_act), None)

    summed, unused = lax.scan(
        column_step,
        jnp.zeros((cell_total, channels), jnp.float32),
        (
            activated.reshape(count_blocks, width_rows, channels),
            bev_cells.reshape(count_blocks, width_rows),
        ),
    )
    return summed


def upstream_rows(grad_flat, bev_cells):
    cell_total = grad_flat.shape[0]
    voxels = bev_cells.shape[0]
    width_rows = min(512, voxels)
    count_blocks = voxels // width_rows

    def lookup_step(carried, block_cells):
        picked = jnp.dot(
            match_table(block_cells, cell_total), grad_flat, preferred_element_type=jnp.float32
        ).astype(jnp.bfloat16)
        return (carried, picked)

    unused, picked_rows = lax.scan(
        lookup_step, jnp.zeros((), jnp.int32), bev_cells.reshape(count_blocks, width_rows)
    )
    return picked_rows.reshape(voxels, grad_flat.shape[1])


def local(
    points,
    point_brick,
    point_voxel,
    send_rows,
    pair_in,
    pair_out,
    bev_cell,
    conv_weight,
    head_weight,
    head_cot,
):
    channels = points.shape[1]
    voxels = bev_cell.shape[2]
    plane_count = lax.axis_size("plane")
    layer_count = lax.axis_size("height")
    brick_count = plane_count * layer_count
    capacity = 2 * points.shape[0] // brick_count
    target = point_brick[:, 0]
    one_hot = (target[:, None] == jnp.arange(brick_count, dtype=jnp.int32)[None, :]).astype(
        jnp.int32
    )
    ranking = jnp.sum((jnp.cumsum(one_hot, axis=0) - 1) * one_hot, axis=1)
    slot_ids = target * capacity + ranking
    send_feat, send_vox = slot_fill(points, point_voxel, slot_ids, brick_count * capacity, voxels)
    got_feat, got_vox = (
        lax.all_to_all(
            send_feat.reshape(brick_count, capacity, channels),
            ("plane", "height"),
            split_axis=0,
            concat_axis=0,
            tiled=True,
        ),
        lax.all_to_all(
            send_vox.reshape(brick_count, capacity),
            ("plane", "height"),
            split_axis=0,
            concat_axis=0,
            tiled=True,
        ),
    )
    pooled = pool_points(got_feat.reshape(-1, channels), got_vox.reshape(-1), voxels).astype(
        jnp.bfloat16
    )
    rim_count = send_rows.shape[3]
    outgoing = jnp.dot(
        match_table(send_rows[0, 0].reshape(-1), voxels), pooled, preferred_element_type=jnp.float32
    ).astype(jnp.bfloat16)
    outgoing = outgoing.reshape(4, rim_count, channels)
    from_left = plane_side(outgoing[1], 1)
    from_right = plane_side(outgoing[0], -1)
    from_below = height_side(outgoing[3], 1)
    from_above = height_side(outgoing[2], -1)
    ext_table = jnp.concatenate(
        [
            pooled,
            from_left,
            from_right,
            from_below,
            from_above,
            jnp.zeros((1, channels), jnp.bfloat16),
        ],
        axis=0,
    )
    ext_count = ext_table.shape[0]
    pair_src = pair_in[0, 0]
    pair_dst = pair_out[0, 0]
    width_out = conv_weight.shape[2]

    def forward_offset(running, members):
        offset_src, offset_dst, offset_weight = members
        picked = jnp.dot(
            match_table(offset_src, ext_count), ext_table, preferred_element_type=jnp.float32
        ).astype(jnp.bfloat16)
        offset_term = jnp.dot(picked, offset_weight, preferred_element_type=jnp.float32)
        high_part = offset_term.astype(jnp.bfloat16)
        low_part = (offset_term - high_part.astype(jnp.float32)).astype(jnp.bfloat16)
        dst_table = match_table(offset_dst, voxels)
        running = running + sum_into(dst_table, high_part) + sum_into(dst_table, low_part)
        return (running, picked)

    summed, gathered = lax.scan(
        forward_offset,
        jnp.zeros((voxels, width_out), jnp.float32),
        (pair_src, pair_dst, conv_weight[:26]),
    )
    pre_act = summed + jnp.dot(pooled, conv_weight[26], preferred_element_type=jnp.float32)
    activated = jax.nn.silu(pre_act).astype(jnp.bfloat16)
    bev_cells = bev_cell[0, 0]
    side_x = head_cot.shape[0]
    side_y = head_cot.shape[1]
    head_width = head_cot.shape[2]
    column_part = column_sums(activated, bev_cells, side_x * side_y)
    column_part = column_part.reshape(side_x, side_y, width_out)
    share_rows = side_x // layer_count
    layer_index = lax.axis_index("height")
    flat_weight = head_weight.reshape(-1, head_width)
    back_weight = jnp.transpose(head_weight, (0, 2, 1)).reshape(-1, width_out)
    own_cot = lax.dynamic_slice_in_dim(head_cot, layer_index * share_rows, share_rows, 0)
    column_tile = lax.psum(column_part.astype(jnp.bfloat16), "height")
    joined = with_halo(jnp.concatenate([column_tile, head_cot], axis=-1), (("plane", 0),), 1)
    joined = jnp.pad(joined, ((0, 0), (1, 1), (0, 0)))
    patches = window_patches(joined[..., :width_out], side_x, side_y, False)
    full_out = jnp.dot(
        patches.reshape(-1, 9 * width_out), flat_weight, preferred_element_type=jnp.float32
    )
    full_out = full_out.astype(jnp.bfloat16).reshape(side_x, side_y, head_width)
    head_out = lax.dynamic_slice_in_dim(full_out, layer_index * share_rows, share_rows, 0)
    own_patches = lax.dynamic_slice_in_dim(patches, layer_index * share_rows, share_rows, 0)
    flipped = window_patches(joined[..., width_out:], side_x, side_y, True)
    bev_grad = jnp.dot(
        flipped.reshape(-1, 9 * head_width), back_weight, preferred_element_type=jnp.float32
    ).astype(jnp.bfloat16)
    head_local = lax.dot_general(
        own_patches.reshape(-1, 9 * width_out),
        own_cot.reshape(-1, head_width),
        (((0,), (0,)), ((), ())),
        preferred_element_type=jnp.float32,
    )
    upstream = upstream_rows(bev_grad, bev_cells)
    pre_grad = (upstream.astype(jnp.float32) * silu_slope(pre_act)).astype(jnp.bfloat16)

    def backward_offset(carried, members):
        picked, offset_dst = members
        dst_grad = jnp.dot(
            match_table(offset_dst, voxels), pre_grad, preferred_element_type=jnp.float32
        ).astype(jnp.bfloat16)
        return (carried, sum_into(picked, dst_grad))

    unused, off_grad = lax.scan(backward_offset, jnp.zeros((), jnp.int32), (gathered, pair_dst))
    centre_grad = sum_into(pooled, pre_grad)
    conv_local = jnp.concatenate([off_grad, centre_grad[None]], axis=0)
    conv_grad, head_grad = lax.psum(
        (conv_local, head_local.reshape(9, width_out, head_width)), ("plane", "height")
    )
    return (head_out, conv_grad, head_grad)


def solution(mesh):
    in_specs = (
        P(("plane", "height"), None),
        P(("plane", "height"), None),
        P(("plane", "height")),
        P("plane", "height", None, None),
        P("plane", "height", None, None),
        P("plane", "height", None, None),
        P("plane", "height", None),
        P(),
        P(),
        P("plane", None, None),
    )
    out_specs = (P(("plane", "height"), None, None), P(), P())
    return jax.shard_map(local, mesh=mesh, in_specs=in_specs, out_specs=out_specs, check_vma=False)
```

profile of v0, /device:TPU:2, one launch (start us, length us, event | category | flops | bytes accessed | tf_op | source)
XLA Modules:
  0.0 603.6 jit_solution(13334501322359457533)
XLA Ops:
  9.6 44.0 %while.67 = (s32[]{:T(128)}, bf16[8,512,128]{2,1,0:T(8,128)(2,1)}, s32[8,512]{1,0:T(8,128)S(1)}, s32[2048]{0:T(1024)S(1)}, s32[8]{0:T(128)S(1)}, /*index=5*/bf16...) while((s32[]{:T(128)}, bf16[8,512,128]{2,1,0:T(8,128)(2,1)}, s32[8,512]{1,0:T(8,128)S(1)}, ...), condition=%wide.region_6.7_spmd, body=%wide.region_3.6_spmd.sunk | while | flops 274792448 | bytes 708209 | solution.py:75
  53.7 19.3 %all_to_all.14 = s32[128,1,32]{2,1,0:T(1,128)S(1)} all-to-all(s32[128,1,32]{2,1,0:T(1,128)S(1)} %bitcast.144), channel_id=1, replica_groups=mesh['plane'=16,'height'=8] {'plane','height'}, dimensions={0} | all-to-all | bytes 32768 | tf_op jit(solution)/shard_map/all_to_all | solution.py:172
  72.9 5.2 all-to-all-start.1
  79.7 17.2 %all-to-all-done.1 = bf16[128,32,128]{2,1,0:T(8,128)(2,1)S(1)} async-done(((bf16[128,32,128]{2,1,0:T(8,128)(2,1)}), bf16[128,32,128]{2,1,0:T(8,128)(2,1)S(1)}, u32[]{:S(2)}, u32[]{:S(2)}) %all-to-all-start.1) | async-done | bytes 1048608 | tf_op jit(solution)/shard_map/all_to_all | solution.py:165
  96.9 8.0 %while.70 = (s32[]{:T(128)}, f32[1024,128]{1,0:T(8,128)S(1)}, s32[8,512]{1,0:T(8,128)S(1)}, bf16[8,512,128]{2,1,0:T(8,128)(2,1)S(1)}, s32[]{:T(128)}, /*index=5*/s32[]{:T(128)}) while((s32[]{:T(128)}, f32[1024,128]{1,0:T(8,128)S(1)}, s32[8,512]{1,0:T(8,128)S(1)}, bf16[8,512,128]{2,1,0:T(8,128)(2,1)S(1)}, s32[]{:T(128)}, ...), condition=%wide.region_8.9_spmd.clone, body=%wide.region_7.8_spmd.clone.sunk | while | flops 135004160 | bytes 1185879 | solution.py:89
  110.3 5.2 collective-permute-start.1
  121.1 87.1 %while.71 = (s32[]{:T(128)}, f32[1024,256]{1,0:T(8,128)S(1)}, bf16[26,256,128]{2,1,0:T(8,128)(2,1)}, s32[26,256]{1,0:T(8,128)S(1)}, s32[26,256]{1,0:T(8,128)S(1)...) while((s32[]{:T(128)}, f32[1024,256]{1,0:T(8,128)S(1)}, ...), condition=%wide.region_10.11_spmd.clone, body=%wide.region_9.10_spmd.clone.sunk | while | flops 371163392 | bytes 5580399 | solution.py:220
  211.1 11.1 %while.72 = (s32[]{:T(128)}, f32[4096,256]{1,0:T(8,128)}, s32[2,512]{1,0:T(2,128)S(1)}, bf16[2,512,256]{2,1,0:T(8,128)(2,1)S(1)}, s32[]{:T(128)}, /*index=5*/s32[]{:T(128)}) while((s32[]{:T(128)}, f32[4096,256]{1,0:T(8,128)}, s32[2,512]{1,0:T(2,128)S(1)}, bf16[2,512,256]{2,1,0:T(8,128)(2,1)S(1)}, s32[]{:T(128)}, ...), condition=%wide.region_12.13_spmd.clone, body=%wide.region_11.12_spmd.clone.sunk | while | flops 1077936128 | bytes 8656983 | solution.py:110
  211.1 4.5 fusion.124
  215.5 6.6 %fusion.124 = f32[4096,256]{1,0:T(8,128)} fusion(f32[4096,256]{1,0:T(8,128)} %get-tuple-element.593, s32[512]{0:T(512)S(1)} %bitcast.143, pred[]{:T(512)S(6)} %compare.52, bf16[2,512,256]{2,1,0:T(8,128)(2,1)S(1)} %get-tuple-element.601, s32[]{:T(128)} %get-tuple-element.592), kind=kOutput, calls=%fused_computation.58.clone.1 | convolution fusion | flops 1077936128 | bytes 8652805 | tf_op jit(solution)/shard_map/while/body/eval_jaxpr/dot_general | solution.py:58
  222.2 3.7 convert_element_type.70
  226.2 64.9 %all-reduce.5.cloned.1.call-done = bf16[64,64,256]{2,1,0:T(8,128)(2,1)} async-done(((bf16[64,64,256]{2,1,0:T(8,128)(2,1)}), bf16[64,64,256]{2,1,0:T(8,128)(2,1)}) %all-reduce.5.cloned.1.call-update) | async-done | bytes 2097168 | tf_op jit(solution)/shard_map/psum | solution.py:238
  295.0 3.4 collective-permute-start.4
  298.4 4.5 collective-permute-start.5
  306.6 3.4 fusion.55
  316.4 4.0 convolution_convert_fusion.1
  320.4 7.7 %while.68 = (s32[]{:T(128)}, bf16[2,512,256]{2,1,0:T(8,128)(2,1)}, s32[2,512]{1,0:T(2,128)S(1)}, bf16[4096,256]{1,0:T(8,128)(2,1)}, s32[]{:T(128)}) while((s32[]{:T(128)}, bf16[2,512,256]{2,1,0:T(8,128)(2,1)}, s32[2,512]{1,0:T(2,128)S(1)}, bf16[4096,256]{1,0:T(8,128)(2,1)}, s32[]{:T(128)}) %tuple.141), condition=%wide.region_15.16_spmd, body=%wide.region_14.15_spmd.sunk | while | flops 1075970048 | bytes 2366017 | solution.py:133
  320.4 3.8 fusion.112
  324.3 3.8 fusion.112
  331.0 77.4 %while.69 = (s32[]{:T(128)}, f32[26,128,256]{2,1,0:T(8,128)}, bf16[26,256,128]{2,1,0:T(8,128)(2,1)}, s32[26,256]{1,0:T(8,128)}, bf16[1024,256]{1,0:T(8,128)(2,1)}, /*index=5*/s32[]{:T(128)}) while((s32[]{:T(128)}, f32[26,128,256]{2,1,0:T(8,128)}, bf16[26,256,128]{2,1,0:T(8,128)(2,1)}, s32[26,256]{1,0:T(8,128)}, ...), condition=%wide.region_17.18_spmd, body=%wide.region_16.17_spmd.sunk | while | flops 151322624 | bytes 725065 | solution.py:268
  432.1 4.2 pad_maximum_fusion
  438.1 9.1 %convolution_convert_fusion.2 = bf16[4096,128]{1,0:T(8,128)(2,1)S(1)} fusion(bf16[4096,2304]{1,0:T(8,128)(2,1)} %bitcast.138, bf16[2304,128]{1,0:T(8,128)(2,1)S(1)} %bitcast.140), kind=kOutput, calls=%fused_computation.68 | convolution fusion | flops 2416443392 | bytes 20512768 | tf_op jit(solution)/shard_map/dot_general | solution.py:242
  447.8 143.7 %all-reduce.7.cloned.1.call-done = (f32[27,128,256]{2,1,0:T(8,128)}, f32[9,256,128]{2,1,0:T(8,128)}) async-done(((f32[27,128,256]{2,1,0:T(8,128)}, f32[9,256,128]{2,1,0:T(8,128)}), (f32[27,128,256]{2,1,0:T(8,128)}, f32[9,256,128]{2,1,0:T(8,128)})) %all-reduce.7.cloned.1.call-update) | async-done | bytes 4718608 | tf_op jit(solution)/shard_map/psum | solution.py:271
  591.5 4.3 copy.105
  (378 shorter events, 276.4 us)
Async XLA Ops:
  7.2 2.4 copy-start.19
  7.2 2.4 copy-start.14
  9.6 68.6 %copy-start.18 = (s32[1,1,4,64]{3,2,1,0:T(4,128)S(1)}, s32[1,1,4,64]{3,2,1,0:T(4,128)}, u32[]{:S(2)}) copy-start(s32[1,1,4,64]{3,2,1,0:T(4,128)} %param.25) | copy-start | bytes 3076
  72.9 24.0 %all-to-all-start.1 = ((bf16[128,32,128]{2,1,0:T(8,128)(2,1)}), bf16[128,32,128]{2,1,0:T(8,128)(2,1)S(1)}, u32[]{:S(2)}, u32[]{:S(2)}) async-start(bf16[128,32,128]{2,1,0:T(8,128)(2,1)} %bitcast.14), calls=%async_computation.1 | async-start | bytes 2097152 | tf_op jit(solution)/shard_map/all_to_all | solution.py:165
  78.1 212.9 %all-reduce.5.cloned.1.call-start = ((), (), s32[]{:S(2)}) async-start(), calls=%async_computation.2 | async-start | bytes 4194304 | tf_op jit(solution)/shard_map/psum | solution.py:238
  104.9 4.7 copy-start.17
  104.9 16.2 %slice-start = ((bf16[27,128,256]{2,1,0:T(8,128)(2,1)}), bf16[26,128,256]{2,1,0:T(8,128)(2,1)S(1)}, s32[]{:S(2)}) async-start(bf16[27,128,256]{2,1,0:T(8,128)(2,1)} %param.29), calls=%async_computation.4 | async-start | bytes 3407872 | tf_op jit(solution)/shard_map/slice | solution.py:223
  106.1 12.0 %collective-permute-start = (bf16[64,128]{1,0:T(8,128)(2,1)S(1)}, bf16[64,128]{1,0:T(8,128)(2,1)S(1)}, u32[]{:S(2)}, u32[]{:S(2)}) collective-permute-start(bf16[64,128]{1,0:T(8,128)(2,1)S(1)} %get-tuple-element.309), channel_id=1, source_target_pairs={{0,8},{8,16},{16,24},{24,32},{32,40},{40,48},{48,56},{56,64},{64,7... | collective-permute-start | bytes 49160 | tf_op jit(solution)/shard_map/ppermute | solution.py:10
  110.3 8.4 %collective-permute-start.1 = (bf16[64,128]{1,0:T(8,128)(2,1)S(1)}, bf16[64,128]{1,0:T(8,128)(2,1)S(1)}, u32[]{:S(2)}, u32[]{:S(2)}) collective-permute-start(bf16[64,128]{1,0:T(8,128)(2,1)S(1)} %get-tuple-element.308), channel_id=1, source_target_pairs={{8,0},{16,8},{24,16},{32,24},{40,32},{48,40},{56,48},{64,56},{72,6... | collective-permute-start | bytes 49160 | tf_op jit(solution)/shard_map/ppermute | solution.py:10
  115.5 3.8 collective-permute-start.2
  116.8 3.1 collective-permute-start.3
  208.8 2.2 copy-start.2
  225.9 365.6 %all-reduce.7.cloned.1.call-start = ((), (), s32[]{:S(2)}) async-start(), calls=%async_computation.3 | async-start | bytes 9437184 | tf_op jit(solution)/shard_map/psum | solution.py:271
  295.0 11.7 %collective-permute-start.4 = (bf16[1,64,384]{2,1,0:T(8,128)(2,1)}, bf16[1,64,384]{2,1,0:T(8,128)(2,1)S(1)}, u32[]{:S(2)}, u32[]{:S(2)}) collective-permute-start(bf16[1,64,384]{2,1,0:T(8,128)(2,1)} %get-tuple-element.304), channel_id=1, source_target_pairs={{0,8},{8,16},{16,24},{24,32},{32,40},{40,48},{48,56},{56,64},{64,7... | collective-permute-start | bytes 147464 | tf_op jit(solution)/shard_map/ppermute | solution.py:18
  298.4 8.2 %collective-permute-start.5 = (bf16[1,64,384]{2,1,0:T(8,128)(2,1)}, bf16[1,64,384]{2,1,0:T(8,128)(2,1)S(1)}, u32[]{:S(2)}, u32[]{:S(2)}) collective-permute-start(bf16[1,64,384]{2,1,0:T(8,128)(2,1)} %get-tuple-element.305), channel_id=1, source_target_pairs={{8,0},{16,8},{24,16},{32,24},{40,32},{48,40},{56,48},{64,56},{72,6... | collective-permute-start | bytes 147464 | tf_op jit(solution)/shard_map/ppermute | solution.py:21
  306.6 8.7 %copy-start.12 = (bf16[1,64,384]{2,1,0:T(8,128)(2,1)}, bf16[1,64,384]{2,1,0:T(8,128)(2,1)S(1)}, u32[]{:S(2)}) copy-start(bf16[1,64,384]{2,1,0:T(8,128)(2,1)S(1)} %collective-permute-done.4) | copy-start | bytes 147460
  306.6 6.0 copy-start.10
  310.0 5.7 copy-start
  330.5 77.9 %copy-start.13 = (bf16[1,64,384]{2,1,0:T(8,128)(2,1)S(1)}, bf16[1,64,384]{2,1,0:T(8,128)(2,1)}, u32[]{:S(2)}) copy-start(bf16[1,64,384]{2,1,0:T(8,128)(2,1)} %copy-done.12) | copy-start | bytes 147460
  408.4 2.8 copy-start.1
  411.2 4.5 copy-start.3
  417.3 4.5 copy-start.11
  432.1 4.2 copy-start.9
  591.5 4.3 copy-start.6
  (6 other events, 7.4 us)
Sparse Core Ops, SparseCore 0:
  226.0 64.9 all-reduce.4
  438.2 153.2 all-reduce.6
where the time goes:
time: 608 us; the launch traced here: 604 us
  waiting for transfers between devices  226 us (37%)
  matrix products  207 us (34%)
  local copies, waits for them, and re-layouts  70 us (12%)
  other arithmetic  41.3 us (7%)
  starting transfers between devices  23.9 us (4%)
  blocking collectives  19.3 us (3%)
  between operations  14.5 us (2%)
    psum x1, waiting for transfers between devices, local(): lax.psum((conv_local, head_local.reshape(9, width_out, head_width)), ('pl...  144 us
    dot_general x97, matrix products, sum_into(): lax.dot_general(one_hot, values, (((0,), (0,)), ((), ())), preferred_elem...  125 us
    psum x1, waiting for transfers between devices, local(): column_tile = lax.psum(column_part.astype(jnp.bfloat16), 'height')  64.9 us
    dot_general x26, matrix products, forward_offset(): jnp.dot(match_table(offset_src, ext_count), ext_table, preferred_element_...  52.2 us
    unnamed x62, local copies, waits for them, and re-layouts  30.7 us
    all_to_all x1, blocking collectives, local(): lax.all_to_all(send_vox.reshape(brick_count, capacity), ('plane', 'height...  19.3 us
    dynamic_slice x52, local copies, waits for them, and re-layouts, local(): lax.scan(forward_offset, jnp.zeros((voxels, width_out), jnp.float32), (pa...  18.5 us
    all_to_all x1, waiting for transfers between devices, local(): lax.all_to_all(send_feat.reshape(brick_count, capacity, channels), ('plan...  17.2 us
  transfers between devices with their start and end apart: 9, of which 3 were waited for; matrix products, arithmetic and copies ran while one was open for 3% of the time, Pallas kernels for 0%

commit v1 on v0

v1 whole, which is shorter than its diff:
```python
import functools

import jax
import jax.numpy as jnp
from jax import lax
from jax.experimental import pallas as pl
from jax.experimental.pallas import tpu as pltpu
from jax.sharding import Mesh, PartitionSpec as P

BF = jnp.bfloat16
F32 = jnp.float32
I32 = jnp.int32
PLANE = ("x", "z")
HEIGHT = ("y", "c")
ALL = ("x", "z", "y", "c")
CAP = 32
ROWS = 40
OFFS = 26
VMEM = pl.BlockSpec(memory_space=pltpu.VMEM)
SMEM = pl.BlockSpec(memory_space=pltpu.SMEM)


def iota(shape, axis):
    return lax.broadcasted_iota(I32, shape, axis)


def hot(mask):
    return jnp.where(mask, 1.0, 0.0).astype(BF)


def dot(a, b):
    return jnp.dot(a, b, preferred_element_type=F32)


def dot_rows(a, b):
    return lax.dot_general(a, b, (((0,), (0,)), ((), ())), preferred_element_type=F32)


def dot_lanes(a, b):
    return lax.dot_general(a, b, (((1,), (1,)), ((), ())), preferred_element_type=F32)


def call(kernel, outs, args, specs=None, scratch=(), flops=0, limit=56):
    return pl.pallas_call(
        kernel,
        out_shape=outs,
        in_specs=[VMEM] * len(args) if specs is None else specs,
        out_specs=jax.tree.map(lambda _: VMEM, outs),
        scratch_shapes=list(scratch),
        compiler_params=pltpu.CompilerParams(vmem_limit_bytes=limit * 1024 * 1024),
        cost_estimate=pl.CostEstimate(flops=flops, bytes_accessed=4 << 20, transcendentals=0),
    )(*args)


def fill_kernel(brick_ref, voxel_ref, points_ref, out_ref, slot_ref):
    step = 256
    total = brick_ref.shape[1]
    upper = hot(iota((step, step), 0) <= iota((step, step), 1))
    run = jnp.zeros((128, 1), F32)
    high = jnp.zeros((128, 128), F32)
    low = jnp.zeros((128, 128), F32)
    for first in range(0, total, step):
        brick = brick_ref[:, first : first + step]
        voxel = voxel_ref[:, first : first + step]
        member = jnp.where(brick == iota((128, step), 0), 1.0, 0.0)
        counts = dot(member.astype(BF), upper) + run
        rank = (jnp.sum(member * counts, axis=0, keepdims=True) - 1.0).astype(I32)
        run = counts[:, step - 1 :]
        slot_ref[:, first : first + step] = brick * CAP + rank
        ranks = hot(rank == (iota((128, step), 0) & (CAP - 1)))
        top = (voxel >> 5).astype(F32)
        bottom = (voxel & 31).astype(F32)
        high = high + dot_lanes((member * top).astype(BF), ranks)
        low = low + dot_lanes((member * bottom).astype(BF), ranks)
    place = iota((128, ROWS - CAP, 128), 1)
    codes = jnp.where(place == 0, high[:, None, :], jnp.where(place == 1, low[:, None, :], 0.0))
    out_ref[:, CAP:ROWS, :] = codes.astype(BF)

    def step_fill(i, carry):
        wanted = iota((256, total), 0) + i * 256
        rows = dot(hot(slot_ref[...] == wanted), points_ref[...]).astype(BF)
        out_ref[pl.ds(i * 8, 8), 0:CAP, :] = rows.reshape(8, CAP, 128)
        return carry

    lax.fori_loop(0, 16, step_fill, 0)


def pool_kernel(got_ref, rim_ref, pooled_ref, rows_ref, acc_ref):
    voxels = pooled_ref.shape[0]

    def step_pool(i, carry):
        codes = got_ref[pl.ds(i * 8, 8), CAP:ROWS, :].astype(F32)
        ids = codes[:, 0, :] * 32.0 + codes[:, 1, :]
        wide = jnp.concatenate([ids, ids], axis=1)
        own = (iota((8, 256), 1) >> 5) == iota((8, 256), 0)
        row = jnp.sum(jnp.where(own, wide, 0.0), axis=0, keepdims=True).astype(I32)
        match = hot(row == iota((voxels, 256), 0))
        part = dot(match, got_ref[pl.ds(i * 8, 8), 0:CAP, :].reshape(256, 128))
        acc_ref[...] = jnp.where(i == 0, part, acc_ref[...] + part)
        return carry

    acc_ref[...] = jnp.zeros_like(acc_ref)
    lax.fori_loop(0, 16, step_pool, 0)
    pooled = acc_ref[...].astype(BF)
    pooled_ref[...] = pooled
    rows_ref[...] = dot(hot(rim_ref[...] == iota((256, voxels), 1)), pooled).astype(BF)


def gather_kernel(pooled_ref, src_ref, out_ref):
    voxels = pooled_ref.shape[0]
    for k in range(OFFS):
        match = hot(src_ref[:, k : k + 1] == iota((256, voxels), 1))
        out_ref[k * 256 : (k + 1) * 256, :] = dot(match, pooled_ref[...]).astype(BF)


def conv_kernel(
    core_ref,
    pooled_ref,
    picked_ref,
    left_ref,
    right_ref,
    below_ref,
    above_ref,
    src_ref,
    dst_ref,
    weight_ref,
    upstream_ref,
    window_ref,
    act_ref,
    keep_ref,
    send_ref,
    table_ref,
    pre_ref,
    grad_ref,
):
    voxels = pooled_ref.shape[0]
    rim = jnp.concatenate(
        [left_ref[...], right_ref[...], below_ref[...], above_ref[...]], axis=0
    )
    for k in range(OFFS):
        match = hot(src_ref[:, k : k + 1] == iota((256, 256), 1) + voxels)
        rows = picked_ref[k * 256 : (k + 1) * 256, :].astype(F32) + dot(match, rim)
        place = hot(dst_ref[k : k + 1, :] == iota((voxels, 256), 0))
        table_ref[:, k * 128 : (k + 1) * 128] = dot(place, rows.astype(BF)).astype(BF)
    table_ref[:, OFFS * 128 :] = pooled_ref[...]
    for m in range(0, voxels, 256):
        pre = dot(table_ref[m : m + 256, :], weight_ref[...])
        sigma = 1.0 / (1.0 + jnp.exp(-pre))
        act_ref[m : m + 256, :] = (pre * sigma).astype(BF)
        slope = sigma * (1.0 + pre * (1.0 - sigma))
        grad_ref[m : m + 256, :] = (upstream_ref[m : m + 256, :].astype(F32) * slope).astype(BF)
    first = core_ref[0] == 0
    for k in range(OFFS + 1):
        full = dot_rows(table_ref[:, k * 128 : (k + 1) * 128], grad_ref[...]).astype(F32)
        lo, hi = full[:, :128], full[:, 128:]
        keep_ref[k * 128 : (k + 1) * 128, :] = jnp.where(first, lo, hi).astype(BF)
        send_ref[k * 128 : (k + 1) * 128, :] = jnp.where(first, hi, lo).astype(BF)
    base = (OFFS + 1) * 128
    for k in range(9):
        full = dot_rows(act_ref[...], window_ref[:, k * 128 : (k + 1) * 128])
        lo, hi = full[:128], full[128:]
        at = base + k * 128
        keep_ref[at : at + 128, :] = jnp.where(first, lo, hi).astype(BF)
        send_ref[at : at + 128, :] = jnp.where(first, hi, lo).astype(BF)


def column_kernel(core_ref, cell_ref, act_ref, keep_ref, send_ref):
    core = core_ref[0]

    def step_column(i, carry):
        y, part = i // 2, i % 2
        for out_ref, which in ((keep_ref, core), (send_ref, 1 - core)):
            start = (y * 2 + which) * 512 + part * 256
            match = hot(cell_ref[...] == iota((256, cell_ref.shape[1]), 0) + start)
            out_ref[pl.ds(i * 256, 256), :] = dot(match, act_ref[...]).astype(BF)
        return carry

    lax.fori_loop(0, 8, step_column, 0)


def shifts(rows):
    total = rows.shape[0]
    y = iota(rows.shape, 0) & 63
    wide = rows.astype(F32)
    lower = jnp.where(y == 0, 0.0, pltpu.roll(wide, 1, 0))
    upper = jnp.where(y == 63, 0.0, pltpu.roll(wide, total - 1, 0))
    return [lower.astype(BF), rows, upper.astype(BF)]


def window_kernel(low_ref, cot_ref, high_ref, cell_ref, back_ref, window_ref, up_ref, moved_ref, patch_ref):
    cells = cot_ref.shape[0]
    for at, ref in ((0, low_ref), (64, cot_ref), (64 + cells, high_ref)):
        size = ref.shape[0]
        block = min(size, 512)
        for m in range(0, size, block):
            for b, moved in enumerate(shifts(ref[m : m + block, :])):
                moved_ref[b, at + m : at + m + block, :] = moved
    for a in range(3):
        for b in range(3):
            k = 3 * a + b
            patch_ref[:, k * 128 : (k + 1) * 128] = moved_ref[2 - b, (2 - a) * 64 : (2 - a) * 64 + cells, :]

    def step_window(i, carry):
        match = hot(cell_ref[pl.ds(i * 256, 256), :] == iota((256, cells), 1))
        for first in (0, 256, 512, 768, 1024):
            last = min(first + 256, 1152)
            window_ref[pl.ds(i * 256, 256), first:last] = dot(match, patch_ref[:, first:last]).astype(BF)
        up_ref[pl.ds(i * 256, 256), :] = dot(window_ref[pl.ds(i * 256, 256), :], back_ref[...]).astype(BF)
        return carry

    lax.fori_loop(0, 4, step_window, 0)


def head_kernel(low_ref, own_ref, high_ref, weight_ref, out_ref, moved_ref):
    size = own_ref.shape[0]
    for at, ref in ((0, low_ref), (64, own_ref), (64 + size, high_ref)):
        for b, moved in enumerate(shifts(ref[...])):
            moved_ref[b, at : at + ref.shape[0], :] = moved
    total = jnp.zeros(out_ref.shape, F32)
    for a in range(3):
        for b in range(3):
            total = total + dot(moved_ref[b, a * 64 : a * 64 + size, :], weight_ref[3 * a + b])
    out_ref[...] = total.astype(BF)


def chain(block, axes, by):
    count = lax.axis_size(axes)
    return lax.ppermute(
        block, axes, [(i, i + by) for i in range(count) if 0 <= i + by < count]
    )


def swap(block):
    return lax.ppermute(block, "c", [(0, 1), (1, 0)])


def exchange(block, axes):
    return lax.all_to_all(block, axes, split_axis=0, concat_axis=0, tiled=True)


def local(
    points,
    point_brick,
    point_voxel,
    send_rows,
    pair_in,
    pair_out,
    bev_cell,
    conv_weight,
    head_weight,
    head_cot,
):
    shape = jax.ShapeDtypeStruct
    voxels = bev_cell.shape[2]
    total = points.shape[0]
    core = lax.axis_index("c").astype(I32).reshape(1)

    ready = call(
        fill_kernel,
        shape((128, ROWS, 128), BF),
        (point_brick.reshape(1, total), point_voxel.reshape(1, total), points),
        scratch=[pltpu.VMEM((1, total), I32)],
        flops=3 << 30,
    )
    got = exchange(ready, ALL)

    cot = head_cot.reshape(-1, 128)
    cells = cot.shape[0]
    cot_low = chain(cot[cells - 64 :], PLANE, 1)
    cot_high = chain(cot[:64], PLANE, -1)
    back_weight = jnp.transpose(head_weight, (0, 2, 1)).reshape(9 * 128, 256)
    window, upstream = call(
        window_kernel,
        [shape((voxels, 9 * 128), BF), shape((voxels, 256), BF)],
        (cot_low, cot, cot_high, bev_cell.reshape(voxels, 1), back_weight),
        scratch=[pltpu.VMEM((3, cells + 128, 128), BF), pltpu.VMEM((cells, 9 * 128), BF)],
        flops=10 << 30,
    )

    pooled, outgoing = call(
        pool_kernel,
        [shape((voxels, 128), BF), shape((256, 128), BF)],
        (got, send_rows.reshape(256, 1)),
        scratch=[pltpu.VMEM((voxels, 128), F32)],
        flops=2 << 30,
    )
    from_left = chain(outgoing[64:128], PLANE, 1)
    from_right = chain(outgoing[0:64], PLANE, -1)
    from_below = chain(outgoing[192:256], HEIGHT, 1)
    from_above = chain(outgoing[128:192], HEIGHT, -1)
    sources = jnp.transpose(pair_in[0, 0])
    picked = call(
        gather_kernel, shape((OFFS * 256, 128), BF), (pooled, sources), flops=3 << 30
    )
    table_width = (OFFS + 1) * 128
    grad_rows = table_width + 9 * 128
    act, keep, send = call(
        conv_kernel,
        [shape((voxels, 256), BF), shape((grad_rows, 128), BF), shape((grad_rows, 128), BF)],
        (
            core,
            pooled,
            picked,
            from_left,
            from_right,
            from_below,
            from_above,
            sources,
            pair_out[0, 0],
            conv_weight.reshape(table_width, 256),
            upstream,
            window,
        ),
        specs=[SMEM] + [VMEM] * 11,
        scratch=[
            pltpu.VMEM((voxels, table_width), BF),
            pltpu.VMEM((8, 128), F32),
            pltpu.VMEM((voxels, 256), BF),
        ],
        flops=8 << 30,
    )

    both = (keep.astype(F32) + swap(send).astype(F32)).astype(BF)
    shares = exchange(both.reshape(64, grad_rows // 64, 128), ("x", "z", "y"))
    share = jnp.sum(shares.astype(F32), axis=0).astype(BF)
    mine = exchange(
        jnp.broadcast_to(share[None], (64,) + share.shape), ("x", "z", "y")
    ).reshape(36, 128, 128)

    column_keep, column_send = call(
        column_kernel,
        [shape((2048, 256), BF), shape((2048, 256), BF)],
        (core, bev_cell.reshape(1, voxels), act),
        specs=[SMEM, VMEM, VMEM],
        flops=3 << 30,
    )
    column = (column_keep.astype(F32) + swap(column_send).astype(F32)).astype(BF)
    column = exchange(column.reshape(4, 512, 256), "y")
    bev = jnp.sum(column.astype(F32), axis=0).astype(BF)
    bev_low = chain(bev[448:], ALL, 1)
    bev_high = chain(bev[:64], ALL, -1)
    head_out = call(
        head_kernel,
        shape((512, 128), BF),
        (bev_low, bev, bev_high, head_weight),
        scratch=[pltpu.VMEM((3, 640, 256), BF)],
        flops=1 << 30,
    )

    theirs = swap(mine)
    first = core[0] == 0
    lo = jnp.where(first, mine, theirs).astype(F32)
    hi = jnp.where(first, theirs, mine).astype(F32)
    conv_grad = jnp.concatenate([lo[:27], hi[:27]], axis=2)
    head_grad = jnp.concatenate([lo[27:], hi[27:]], axis=1)
    return (head_out.reshape(8, 64, 128), conv_grad, head_grad)


def solution(mesh):
    grid = Mesh(mesh.devices.reshape(4, 4, 4, 2), ALL)
    in_specs = (
        P(ALL, None),
        P(ALL, None),
        P(ALL),
        P(PLANE, HEIGHT, None, None),
        P(PLANE, HEIGHT, None, None),
        P(PLANE, HEIGHT, None, None),
        P(PLANE, HEIGHT, None),
        P(),
        P(),
        P(PLANE, None, None),
    )
    out_specs = (P(ALL, None, None), P(), P())
    return jax.shard_map(local, mesh=grid, in_specs=in_specs, out_specs=out_specs, check_vma=False)
```

time: 608 us -> 204 us (0.34)
  matrix products: 207 us -> 0 us
  waiting for transfers between devices: 226 us -> 28.7 us
  Pallas kernels: 0 us -> 68.5 us
  local copies, waits for them, and re-layouts: 70 us -> 11.1 us
  other arithmetic: 41.3 us -> 7.65 us
  blocking collectives: 19.3 us -> 46.9 us
  starting transfers between devices: 23.9 us -> 39.7 us
  between operations: 14.5 us -> 0.87 us
    psum x2 -> x0, waiting for transfers between devices: 209 us -> none  [the longest x1 144 us: local(): lax.psum((conv_local, head_local.reshape(9, width_out, head_width)), ('pl...]
    dot_general x156 -> x0, matrix products: 207 us -> none  [the longest x97 125 us: sum_into(): lax.dot_general(one_hot, values, (((0,), (0,)), ((), ())), preferred_elem...]
    pallas_call x0 -> x7, Pallas kernels: none -> 68.5 us  [call(): pl.pallas_call(kernel, out_shape=outs, in_specs=[VMEM] * len(args) if spe...]
    dynamic_slice x75 -> x0, local copies, waits for them, and re-layouts: 28.7 us -> none  [the longest x52 18.5 us: local(): lax.scan(forward_offset, jnp.zeros((voxels, width_out), jnp.float32), (pa...]
    all_to_all x1 -> x2, blocking collectives: 19.3 us -> 46.9 us  [exchange(): return lax.all_to_all(block, axes, split_axis=0, concat_axis=0, tiled=True)]
    unnamed x62 -> x30, local copies, waits for them, and re-layouts: 30.7 us -> 4.3 us
    ppermute x6 -> x11, waiting for transfers between devices: 0.02 us -> 16.7 us  [the longest x8 14 us: chain(): lax.ppermute(block, axes, [(i, i + by) for i in range(count) if 0 <= i +...]
    all_to_all x1 -> x2, starting transfers between devices: 5.18 us -> 16.6 us  [exchange(): return lax.all_to_all(block, axes, split_axis=0, concat_axis=0, tiled=True)]
  transfers between devices with their start and end apart: 9 -> 13, of which waited for: 3 -> 5; matrix products, arithmetic and copies ran while one was open for 3% -> 4% of each run, Pallas kernels for 0% -> 16%
where the time goes in v1:
time: 204 us; the launch traced here: 203 us
  Pallas kernels  68.5 us (34%)
  blocking collectives  46.9 us (23%)
  starting transfers between devices  39.7 us (19%)
  waiting for transfers between devices  28.7 us (14%)
  local copies, waits for them, and re-layouts  11.1 us (5%)
  other arithmetic  7.65 us (4%)
    pallas_call x7, Pallas kernels, call(): pl.pallas_call(kernel, out_shape=outs, in_specs=[VMEM] * len(args) if spe...  68.5 us
    all_to_all x2, blocking collectives, exchange(): return lax.all_to_all(block, axes, split_axis=0, concat_axis=0, tiled=True)  46.9 us
    ppermute x8, starting transfers between devices, chain(): lax.ppermute(block, axes, [(i, i + by) for i in range(count) if 0 <= i +...  22.6 us
    all_to_all x2, starting transfers between devices, exchange(): return lax.all_to_all(block, axes, split_axis=0, concat_axis=0, tiled=True)  16.6 us
    ppermute x8, waiting for transfers between devices, chain(): lax.ppermute(block, axes, [(i, i + by) for i in range(count) if 0 <= i +...  14 us
    all_to_all x2, waiting for transfers between devices, exchange(): return lax.all_to_all(block, axes, split_axis=0, concat_axis=0, tiled=True)  12.1 us
    unnamed x30, local copies, waits for them, and re-layouts  4.3 us
  transfers between devices with their start and end apart: 13, of which 5 were waited for; matrix products, arithmetic and copies ran while one was open for 4% of the time, Pallas kernels for 16%

profile of v1, /device:TPU:2, one launch (start us, length us, event | category | flops | bytes accessed | tf_op | source)
XLA Modules:
  0.0 203.5 jit_solution(5737618597050004034)
XLA Ops:
  0.6 10.9 %shard_map.121 = bf16[128,40,128]{2,1,0:T(8,128)(2,1)} custom-call(s32[1,2048]{1,0:T(1,128)} %bitcast.36, s32[1,2048]{1,0:T(1,128)} %bitcast.37, bf16[2048,128]{1,0:T(8,128)(2,1)} %points_ref.1), custom_call_target="tpu_custom_call" | custom-call | flops 3221225472 | bytes 4194304 | tf_op jit(solution)/shard_map/pallas_call | solution.py:44
  11.6 10.5 %all-to-all-start = ((bf16[128,40,128]{2,1,0:T(8,128)(2,1)}), bf16[128,40,128]{2,1,0:T(8,128)(2,1)S(1)}, u32[]{:S(2)}, u32[]{:S(2)}) async-start(bf16[128,40,128]{2,1,0:T(8,128)(2,1)} %shard_map.121), calls=%async_computation | async-start | bytes 2621440 | tf_op jit(solution)/shard_map/all_to_all | solution.py:238
  22.9 5.2 %collective-permute-start.5 = (bf16[64,128]{1,0:T(8,128)(2,1)S(1)}, bf16[64,128]{1,0:T(8,128)(2,1)S(1)}, u32[]{:S(2)}, u32[]{:S(2)}) collective-permute-start(bf16[64,128]{1,0:T(8,128)(2,1)S(1)} %get-tuple-element.23), channel_id=1, source_target_pairs={{8,0},{16,8},{24,16},{32,24},{40,32},{48,40},{56,48},{64,56},{72,6... | collective-permute-start | bytes 49160 | tf_op jit(solution)/shard_map/ppermute | solution.py:228
  28.1 1.9 collective-permute-start.4
  34.3 3.2 %collective-permute-done.5.high_ref = bf16[64,128]{1,0:T(8,128)(2,1)S(1)} collective-permute-done((bf16[64,128]{1,0:T(8,128)(2,1)S(1)}, bf16[64,128]{1,0:T(8,128)(2,1)S(1)}, u32[]{:S(2)}, u32[]{:S(2)}) %collective-permute-start.5) | collective-permute-done | bytes 16416 | tf_op jit(solution)/shard_map/ppermute | solution.py:228
  37.6 3.3 %collective-permute-done.4.low_ref = bf16[64,128]{1,0:T(8,128)(2,1)S(1)} collective-permute-done((bf16[64,128]{1,0:T(8,128)(2,1)S(1)}, bf16[64,128]{1,0:T(8,128)(2,1)S(1)}, u32[]{:S(2)}, u32[]{:S(2)}) %collective-permute-start.4) | collective-permute-done | bytes 16416 | tf_op jit(solution)/shard_map/ppermute | solution.py:228
  41.4 18.4 %shard_map.124 = (bf16[1024,1152]{1,0:T(8,128)(2,1)}, bf16[1024,256]{1,0:T(8,128)(2,1)}) custom-call(bf16[64,128]{1,0:T(8,128)(2,1)} %copy-done.13, bf16[4096,128]{1,0:T(8,128)(2,1)} %bitcast.34, bf16[64,128]{1,0:T(8,128)(2,1)} %copy-done.12, s32[1024,1]{1,0:T(8,128)} %copy.18.cell_ref, bf16[1152,256]{1,0:T(8,128)(2,1)} %bitcast.28), custom_call_target="tpu_custom_call" | custom-call | flops 10737418240 | bytes 4194304 | tf_op jit(solution)/shard_map/pallas_call | solution.py:44
  60.9 7.2 %shard_map.122 = (bf16[1024,128]{1,0:T(8,128)(2,1)}, bf16[256,128]{1,0:T(8,128)(2,1)}) custom-call(bf16[128,40,128]{2,1,0:T(8,128)(2,1)} %copy-done, s32[256,1]{1,0:T(8,128)} %reshape.61.rim_ref), custom_call_target="tpu_custom_call" | custom-call | flops 2147483648 | bytes 4194304 | tf_op jit(solution)/shard_map/pallas_call | solution.py:44
  70.2 3.0 %collective-permute-start.2 = (bf16[64,128]{1,0:T(8,128)(2,1)S(1)}, bf16[64,128]{1,0:T(8,128)(2,1)S(1)}, u32[]{:S(2)}, u32[]{:S(2)}) collective-permute-start(bf16[64,128]{1,0:T(8,128)(2,1)S(1)} %get-tuple-element.28), channel_id=1, source_target_pairs={{0,1},{1,2},{2,3},{3,4},{4,5},{5,6},{6,7},{8,9},{9,10},{10,11},{11... | collective-permute-start | bytes 49160 | tf_op jit(solution)/shard_map/ppermute | solution.py:228
  73.3 2.4 %collective-permute-start.1 = (bf16[64,128]{1,0:T(8,128)(2,1)S(1)}, bf16[64,128]{1,0:T(8,128)(2,1)S(1)}, u32[]{:S(2)}, u32[]{:S(2)}) collective-permute-start(bf16[64,128]{1,0:T(8,128)(2,1)S(1)} %get-tuple-element.29), channel_id=1, source_target_pairs={{8,0},{16,8},{24,16},{32,24},{40,32},{48,40},{56,48},{64,56},{72,6... | collective-permute-start | bytes 49160 | tf_op jit(solution)/shard_map/ppermute | solution.py:228
  75.6 3.7 %collective-permute-start = (bf16[64,128]{1,0:T(8,128)(2,1)S(1)}, bf16[64,128]{1,0:T(8,128)(2,1)S(1)}, u32[]{:S(2)}, u32[]{:S(2)}) collective-permute-start(bf16[64,128]{1,0:T(8,128)(2,1)S(1)} %get-tuple-element.30), channel_id=1, source_target_pairs={{0,8},{8,16},{16,24},{24,32},{32,40},{40,48},{48,56},{56,64},{64,7... | collective-permute-start | bytes 49160 | tf_op jit(solution)/shard_map/ppermute | solution.py:228
  79.3 6.0 %shard_map.123.picked_ref = bf16[6656,128]{1,0:T(8,128)(2,1)} custom-call(bf16[1024,128]{1,0:T(8,128)(2,1)} %get-tuple-element.12.pooled_ref, s32[256,26]{1,0:T(8,128)} %bitcast.29), custom_call_target="tpu_custom_call" | custom-call | flops 3221225472 | bytes 4194304 | tf_op jit(solution)/shard_map/pallas_call | solution.py:44
  85.9 17.4 %shard_map.125 = (bf16[1024,256]{1,0:T(8,128)(2,1)}, bf16[4608,128]{1,0:T(8,128)(2,1)}, bf16[4608,128]{1,0:T(8,128)(2,1)}) custom-call(s32[1]{0:T(128)} %bitcast.core_ref, bf16[1024,128]{1,0:T(8,128)(2,1)} %get-tuple-element.12.pooled_ref, bf16[6656,128]{1,0:T(8,128)(2,1)} %shard_map.123.picked_ref, bf16[64,128]{1,0:T(8,128)(2,1)} %copy-done.11, ...), custom_call_target="tpu_custom_call" | custom-call | flops 8589934592 | bytes 4194304 | tf_op jit(solution)/shard_map/pallas_call | solution.py:44
  103.9 2.7 %collective-permute-done.9 = bf16[4608,128]{1,0:T(8,128)(2,1)S(1)} collective-permute-done((bf16[4608,128]{1,0:T(8,128)(2,1)}, bf16[4608,128]{1,0:T(8,128)(2,1)S(1)}, u32[]{:S(2)}, u32[]{:S(2)}) %collective-permute-start.9) | collective-permute-done | bytes 1179680 | tf_op jit(solution)/shard_map/ppermute | solution.py:234
  108.1 28.3 %all_to_all.20 = bf16[64,72,128]{2,1,0:T(8,128)(2,1)S(1)} all-to-all(bf16[64,72,128]{2,1,0:T(8,128)(2,1)S(1)} %bitcast.25), channel_id=1, replica_groups=mesh['x'=4,'z'=4,'y'=4,'c'=2] {'x','z','y'}, dimensions={0} | all-to-all | bytes 2359296 | tf_op jit(solution)/shard_map/all_to_all | solution.py:238
  137.8 6.1 %all-to-all-start.3 = ((bf16[64,72,128]{2,1,0:T(8,128)(2,1)}), bf16[64,72,128]{2,1,0:T(8,128)(2,1)S(1)}, u32[]{:S(2)}, u32[]{:S(2)}) async-start(bf16[64,72,128]{2,1,0:T(8,128)(2,1)} %broadcast_in_dim.2), calls=%async_computation.3 | async-start | bytes 2359296 | tf_op jit(solution)/shard_map/all_to_all | solution.py:238
  143.8 5.9 %shard_map.126 = (bf16[2048,256]{1,0:T(8,128)(2,1)}, bf16[2048,256]{1,0:T(8,128)(2,1)}) custom-call(s32[1]{0:T(128)} %bitcast.core_ref, s32[1,1024]{1,0:T(1,128)} %bitcast.32, bf16[1024,256]{1,0:T(8,128)(2,1)} %get-tuple-element.16.act_ref), custom_call_target="tpu_custom_call" | custom-call | flops 3221225472 | bytes 4194304 | tf_op jit(solution)/shard_map/pallas_call | solution.py:44
  149.7 12.1 %all-to-all-done.3 = bf16[64,72,128]{2,1,0:T(8,128)(2,1)S(1)} async-done(((bf16[64,72,128]{2,1,0:T(8,128)(2,1)}), bf16[64,72,128]{2,1,0:T(8,128)(2,1)S(1)}, u32[]{:S(2)}, u32[]{:S(2)}) %all-to-all-start.3) | async-done | bytes 1179680 | tf_op jit(solution)/shard_map/all_to_all | solution.py:238
  163.3 18.6 %all_to_all.21 = bf16[4,512,256]{2,1,0:T(8,128)(2,1)S(1)} all-to-all(bf16[4,512,256]{2,1,0:T(8,128)(2,1)S(1)} %bitcast.26), channel_id=1, replica_groups=mesh['x'=4,'z'=4,'y'=4,'c'=2] {'y'}, dimensions={0} | all-to-all | bytes 2097152 | tf_op jit(solution)/shard_map/all_to_all | solution.py:238
  183.6 3.2 %collective-permute-start.8 = (bf16[64,256]{1,0:T(8,128)(2,1)S(1)}, bf16[64,256]{1,0:T(8,128)(2,1)S(1)}, u32[]{:S(2)}, u32[]{:S(2)}) collective-permute-start(bf16[64,256]{1,0:T(8,128)(2,1)S(1)} %get-tuple-element.25), channel_id=1, source_target_pairs={{1,0},{2,1},{3,2},{4,3},{5,4},{6,5},{7,6},{8,7},{9,8},{10,9},{11,1... | collective-permute-start | bytes 98312 | tf_op jit(solution)/shard_map/ppermute | solution.py:228
  186.8 1.9 collective-permute-start.7
  188.7 7.5 %collective-permute-done.7.low_ref = bf16[64,256]{1,0:T(8,128)(2,1)S(1)} collective-permute-done((bf16[64,256]{1,0:T(8,128)(2,1)S(1)}, bf16[64,256]{1,0:T(8,128)(2,1)S(1)}, u32[]{:S(2)}, u32[]{:S(2)}) %collective-permute-start.7) | collective-permute-done | bytes 32800 | tf_op jit(solution)/shard_map/ppermute | solution.py:228
  196.8 2.6 %shard_map.127 = bf16[512,128]{1,0:T(8,128)(2,1)} custom-call(bf16[64,256]{1,0:T(8,128)(2,1)} %copy-done.7, bf16[512,256]{1,0:T(8,128)(2,1)} %reduce_sum.24.own_ref, bf16[64,256]{1,0:T(8,128)(2,1)} %copy-done.6, bf16[9,256,128]{2,1,0:T(8,128)(2,1)} %weight_ref.1), custom_call_target="tpu_custom_call" | custom-call | flops 1073741824 | bytes 4194304 | tf_op jit(solution)/shard_map/pallas_call | solution.py:44
  200.3 2.1 %pad_maximum_fusion = f32[27,128,256]{2,1,0:T(8,128)} fusion(f32[27,128,128]{2,1,0:T(8,128)S(1)} %slice.59, f32[27,128,128]{2,1,0:T(8,128)S(1)} %slice.58), kind=kLoop, calls=%fused_computation | loop fusion | flops 884736 | bytes 7077888 | tf_op jit(solution)/shard_map/concatenate | solution.py:354
  (59 shorter events, 18.5 us)
Async XLA Ops:
  11.6 18.5 %copy-start.3 = (s32[1,1,26,256]{3,1,2,0:T(1,128)S(1)}, s32[1,1,26,256]{3,1,2,0:T(1,128)}, u32[]{:S(2)}) copy-start(s32[1,1,26,256]{3,1,2,0:T(1,128)} %param.15) | copy-start | bytes 79876
  11.6 19.1 %copy-start.5 = (s32[1,1,4,64]{3,2,1,0:T(4,128)S(1)}, s32[1,1,4,64]{3,2,1,0:T(4,128)}, u32[]{:S(2)}) copy-start(s32[1,1,4,64]{3,2,1,0:T(4,128)} %param.13) | copy-start | bytes 3076
  11.6 19.9 %copy-start.2 = (s32[1,1,26,256]{3,1,2,0:T(1,128)S(1)}, s32[1,1,26,256]{3,1,2,0:T(1,128)}, u32[]{:S(2)}) copy-start(s32[1,1,26,256]{3,1,2,0:T(1,128)} %param.14) | copy-start | bytes 79876
  11.6 20.7 %copy-start.4 = (s32[1,1,1024]{2,1,0:T(1,128)S(1)}, s32[1,1,1024]{2,1,0:T(1,128)}, u32[]{:S(2)}) copy-start(s32[1,1,1024]{2,1,0:T(1,128)} %param.16) | copy-start | bytes 12292
  11.6 21.7 %copy-start.1 = (bf16[9,256,128]{2,1,0:T(8,128)(2,1)S(1)}, bf16[9,256,128]{2,1,0:T(8,128)(2,1)}, u32[]{:S(2)}) copy-start(bf16[9,256,128]{2,1,0:T(8,128)(2,1)} %weight_ref.1) | copy-start | bytes 1769476
  11.6 48.3 %all-to-all-start = ((bf16[128,40,128]{2,1,0:T(8,128)(2,1)}), bf16[128,40,128]{2,1,0:T(8,128)(2,1)S(1)}, u32[]{:S(2)}, u32[]{:S(2)}) async-start(bf16[128,40,128]{2,1,0:T(8,128)(2,1)} %shard_map.121), calls=%async_computation | async-start | bytes 2621440 | tf_op jit(solution)/shard_map/all_to_all | solution.py:238
  22.9 14.7 %collective-permute-start.5 = (bf16[64,128]{1,0:T(8,128)(2,1)S(1)}, bf16[64,128]{1,0:T(8,128)(2,1)S(1)}, u32[]{:S(2)}, u32[]{:S(2)}) collective-permute-start(bf16[64,128]{1,0:T(8,128)(2,1)S(1)} %get-tuple-element.23), channel_id=1, source_target_pairs={{8,0},{16,8},{24,16},{32,24},{40,32},{48,40},{56,48},{64,56},{72,6... | collective-permute-start | bytes 49160 | tf_op jit(solution)/shard_map/ppermute | solution.py:228
  28.1 12.7 %collective-permute-start.4 = (bf16[64,128]{1,0:T(8,128)(2,1)S(1)}, bf16[64,128]{1,0:T(8,128)(2,1)S(1)}, u32[]{:S(2)}, u32[]{:S(2)}) collective-permute-start(bf16[64,128]{1,0:T(8,128)(2,1)S(1)} %get-tuple-element.24), channel_id=1, source_target_pairs={{0,8},{8,16},{16,24},{24,32},{32,40},{40,48},{48,56},{56,64},{64,7... | collective-permute-start | bytes 49160 | tf_op jit(solution)/shard_map/ppermute | solution.py:228
  37.6 3.3 %copy-start.12 = (bf16[64,128]{1,0:T(8,128)(2,1)}, bf16[64,128]{1,0:T(8,128)(2,1)S(1)}, u32[]{:S(2)}) copy-start(bf16[64,128]{1,0:T(8,128)(2,1)S(1)} %collective-permute-done.5.high_ref) | copy-start | bytes 49156
  59.9 1.1 copy-start
  68.9 16.4 %collective-permute-start.3 = (bf16[64,128]{1,0:T(8,128)(2,1)S(1)}, bf16[64,128]{1,0:T(8,128)(2,1)S(1)}, u32[]{:S(2)}, u32[]{:S(2)}) collective-permute-start(bf16[64,128]{1,0:T(8,128)(2,1)S(1)} %get-tuple-element.27), channel_id=1, source_target_pairs={{1,0},{2,1},{3,2},{4,3},{5,4},{6,5},{7,6},{9,8},{10,9},{11,10},{12... | collective-permute-start | bytes 49160 | tf_op jit(solution)/shard_map/ppermute | solution.py:228
  70.2 15.1 %collective-permute-start.2 = (bf16[64,128]{1,0:T(8,128)(2,1)S(1)}, bf16[64,128]{1,0:T(8,128)(2,1)S(1)}, u32[]{:S(2)}, u32[]{:S(2)}) collective-permute-start(bf16[64,128]{1,0:T(8,128)(2,1)S(1)} %get-tuple-element.28), channel_id=1, source_target_pairs={{0,1},{1,2},{2,3},{3,4},{4,5},{5,6},{6,7},{8,9},{9,10},{10,11},{11... | collective-permute-start | bytes 49160 | tf_op jit(solution)/shard_map/ppermute | solution.py:228
  73.3 12.0 %collective-permute-start.1 = (bf16[64,128]{1,0:T(8,128)(2,1)S(1)}, bf16[64,128]{1,0:T(8,128)(2,1)S(1)}, u32[]{:S(2)}, u32[]{:S(2)}) collective-permute-start(bf16[64,128]{1,0:T(8,128)(2,1)S(1)} %get-tuple-element.29), channel_id=1, source_target_pairs={{8,0},{16,8},{24,16},{32,24},{40,32},{48,40},{56,48},{64,56},{72,6... | collective-permute-start | bytes 49160 | tf_op jit(solution)/shard_map/ppermute | solution.py:228
  75.6 9.7 %collective-permute-start = (bf16[64,128]{1,0:T(8,128)(2,1)S(1)}, bf16[64,128]{1,0:T(8,128)(2,1)S(1)}, u32[]{:S(2)}, u32[]{:S(2)}) collective-permute-start(bf16[64,128]{1,0:T(8,128)(2,1)S(1)} %get-tuple-element.30), channel_id=1, source_target_pairs={{0,8},{8,16},{16,24},{24,32},{32,40},{40,48},{48,56},{56,64},{64,7... | collective-permute-start | bytes 49160 | tf_op jit(solution)/shard_map/ppermute | solution.py:228
  85.3 0.6 copy-start.8
  85.3 0.6 copy-start.11
  103.3 3.2 %collective-permute-start.9 = (bf16[4608,128]{1,0:T(8,128)(2,1)}, bf16[4608,128]{1,0:T(8,128)(2,1)S(1)}, u32[]{:S(2)}, u32[]{:S(2)}) collective-permute-start(bf16[4608,128]{1,0:T(8,128)(2,1)} %get-tuple-element.20), channel_id=1, source_target_pairs={{0,1},{1,0},{2,3},{3,2},{4,5},{5,4},{6,7},{7,6},{8,9},{9,8},{10,11... | collective-permute-start | bytes 3538952 | tf_op jit(solution)/shard_map/ppermute | solution.py:234
  137.8 24.0 %all-to-all-start.3 = ((bf16[64,72,128]{2,1,0:T(8,128)(2,1)}), bf16[64,72,128]{2,1,0:T(8,128)(2,1)S(1)}, u32[]{:S(2)}, u32[]{:S(2)}) async-start(bf16[64,72,128]{2,1,0:T(8,128)(2,1)} %broadcast_in_dim.2), calls=%async_computation.3 | async-start | bytes 2359296 | tf_op jit(solution)/shard_map/all_to_all | solution.py:238
  149.7 12.1 %collective-permute-start.6 = (bf16[2048,256]{1,0:T(8,128)(2,1)}, bf16[2048,256]{1,0:T(8,128)(2,1)S(1)}, u32[]{:S(2)}, u32[]{:S(2)}) collective-permute-start(bf16[2048,256]{1,0:T(8,128)(2,1)} %get-tuple-element.18), channel_id=1, source_target_pairs={{0,1},{1,0},{2,3},{3,2},{4,5},{5,4},{6,7},{7,6},{8,9},{9,8},{10,11... | collective-permute-start | bytes 3145736 | tf_op jit(solution)/shard_map/ppermute | solution.py:234
  161.8 37.7 %collective-permute-start.10 = (bf16[36,128,128]{2,1,0:T(8,128)(2,1)S(1)}, bf16[36,128,128]{2,1,0:T(8,128)(2,1)S(1)}, u32[]{:S(2)}, u32[]{:S(2)}) collective-permute-start(bf16[36,128,128]{2,1,0:T(8,128)(2,1)S(1)} %bitcast.23), channel_id=1, source_target_pairs={{0,1},{1,0},{2,3},{3,2},{4,5},{5,4},{6,7},{7,6},{8,9},{9,8},{10,11... | collective-permute-start | bytes 3538952 | tf_op jit(solution)/shard_map/ppermute | solution.py:234
  183.6 5.1 %collective-permute-start.8 = (bf16[64,256]{1,0:T(8,128)(2,1)S(1)}, bf16[64,256]{1,0:T(8,128)(2,1)S(1)}, u32[]{:S(2)}, u32[]{:S(2)}) collective-permute-start(bf16[64,256]{1,0:T(8,128)(2,1)S(1)} %get-tuple-element.25), channel_id=1, source_target_pairs={{1,0},{2,1},{3,2},{4,3},{5,4},{6,5},{7,6},{8,7},{9,8},{10,9},{11,1... | collective-permute-start | bytes 98312 | tf_op jit(solution)/shard_map/ppermute | solution.py:228
  186.8 9.5 %collective-permute-start.7 = (bf16[64,256]{1,0:T(8,128)(2,1)S(1)}, bf16[64,256]{1,0:T(8,128)(2,1)S(1)}, u32[]{:S(2)}, u32[]{:S(2)}) collective-permute-start(bf16[64,256]{1,0:T(8,128)(2,1)S(1)} %get-tuple-element.26), channel_id=1, source_target_pairs={{0,1},{1,2},{2,3},{3,4},{4,5},{5,6},{6,7},{7,8},{8,9},{9,10},{10,1... | collective-permute-start | bytes 98312 | tf_op jit(solution)/shard_map/ppermute | solution.py:228
  188.7 7.5 %copy-start.6 = (bf16[64,256]{1,0:T(8,128)(2,1)}, bf16[64,256]{1,0:T(8,128)(2,1)S(1)}, u32[]{:S(2)}) copy-start(bf16[64,256]{1,0:T(8,128)(2,1)S(1)} %collective-permute-done.8.high_ref) | copy-start | bytes 98308
  196.2 0.6 copy-start.7
  (3 other events, 1.8 us)

commit v2 on v1

v2 whole, which is shorter than its diff:
```python
import functools

import jax
import jax.numpy as jnp
from jax import lax
from jax.experimental import pallas as pl
from jax.experimental.pallas import tpu as pltpu
from jax.sharding import Mesh, PartitionSpec as P

BF = jnp.bfloat16
F32 = jnp.float32
I32 = jnp.int32
PLANE = ("x", "z")
HEIGHT = ("y", "c")
ALL = ("x", "z", "y", "c")
CAP = 32
ROWS = 40
OFFS = 26
VMEM = pl.BlockSpec(memory_space=pltpu.VMEM)
SMEM = pl.BlockSpec(memory_space=pltpu.SMEM)


def iota(shape, axis):
    return lax.broadcasted_iota(I32, shape, axis)


def hot(mask):
    return jnp.where(mask, 1.0, 0.0).astype(BF)


def dot(a, b):
    return jnp.dot(a, b, preferred_element_type=F32)


def dot_rows(a, b):
    return lax.dot_general(a, b, (((0,), (0,)), ((), ())), preferred_element_type=F32)


def dot_lanes(a, b):
    return lax.dot_general(a, b, (((1,), (1,)), ((), ())), preferred_element_type=F32)


def call(kernel, outs, args, specs=None, scratch=(), flops=0, limit=56):
    return pl.pallas_call(
        kernel,
        out_shape=outs,
        in_specs=[VMEM] * len(args) if specs is None else specs,
        out_specs=jax.tree.map(lambda _: VMEM, outs),
        scratch_shapes=list(scratch),
        compiler_params=pltpu.CompilerParams(vmem_limit_bytes=limit * 1024 * 1024),
        cost_estimate=pl.CostEstimate(flops=flops, bytes_accessed=4 << 20, transcendentals=0),
    )(*args)


def fill_kernel(brick_ref, voxel_ref, points_ref, out_ref, slot_ref):
    step = 256
    total = brick_ref.shape[1]
    upper = hot(iota((step, step), 0) <= iota((step, step), 1))
    spans = [slice(first, first + step) for first in range(0, total, step)]
    masks = [brick_ref[:, span] == iota((128, step), 0) for span in spans]
    counts = dot(jnp.concatenate([hot(mask) for mask in masks], axis=0), upper)
    before = jnp.zeros((128, 1), F32)
    ranks = []
    for i, span in enumerate(spans):
        count = counts[i * 128 : (i + 1) * 128]
        rank = jnp.sum(jnp.where(masks[i], count + (before - 1.0), 0.0), axis=0, keepdims=True)
        before = before + count[:, step - 1 :]
        slot_ref[:, span] = brick_ref[:, span] * CAP + rank.astype(I32)
        ranks.append(rank.astype(I32))
    rank = jnp.concatenate(ranks, axis=1)
    member = brick_ref[...] == iota((128, total), 0)
    voxel = voxel_ref[...]
    high = jnp.where(member, (voxel >> 5).astype(F32), 0.0).astype(BF)
    low = jnp.where(member, (voxel & 31).astype(F32), 0.0).astype(BF)
    by_rank = hot(rank == (iota((128, total), 0) & (CAP - 1)))
    codes = dot_lanes(jnp.concatenate([high, low], axis=0), by_rank)
    place = iota((128, ROWS - CAP, 128), 1)
    rows = jnp.where(place == 0, codes[:128][:, None, :], 0.0)
    rows = jnp.where(place == 1, codes[128:][:, None, :], rows)
    out_ref[:, CAP:ROWS, :] = rows.astype(BF)
    for m in range(0, 128 * CAP, 512):
        match = hot(slot_ref[...] == iota((512, total), 0) + m)
        rows = dot(match, points_ref[...]).astype(BF)
        out_ref[m // CAP : (m + 512) // CAP, 0:CAP, :] = rows.reshape(512 // CAP, CAP, 128)


def pool_kernel(got_ref, rim_ref, pooled_ref, rows_ref, acc_ref):
    voxels = pooled_ref.shape[0]
    own = (iota((8, 256), 1) >> 5) == iota((8, 256), 0)
    for i in range(16):
        codes = got_ref[i * 8 : i * 8 + 8, CAP:ROWS, :].astype(F32)
        ids = codes[:, 0, :] * 32.0 + codes[:, 1, :]
        wide = jnp.concatenate([ids, ids], axis=1)
        row = jnp.sum(jnp.where(own, wide, 0.0), axis=0, keepdims=True).astype(I32)
        match = hot(row == iota((voxels, 256), 0))
        part = dot(match, got_ref[i * 8 : i * 8 + 8, 0:CAP, :].reshape(256, 128))
        acc_ref[...] = part if i == 0 else acc_ref[...] + part
    pooled = acc_ref[...].astype(BF)
    pooled_ref[...] = pooled
    rows_ref[...] = dot(hot(rim_ref[...] == iota((256, voxels), 1)), pooled).astype(BF)


def gather_kernel(pooled_ref, src_ref, out_ref, match_ref):
    voxels = pooled_ref.shape[0]
    for first in range(0, OFFS, 4):
        last = min(first + 4, OFFS)
        for k in range(first, last):
            match_ref[(k - first) * 256 : (k - first + 1) * 256, :] = hot(
                src_ref[:, k : k + 1] == iota((256, voxels), 1)
            )
        size = (last - first) * 256
        out_ref[first * 256 : last * 256, :] = dot(match_ref[:size, :], pooled_ref[...]).astype(BF)


def conv_kernel(
    core_ref,
    pooled_ref,
    picked_ref,
    left_ref,
    right_ref,
    below_ref,
    above_ref,
    src_ref,
    dst_ref,
    weight_ref,
    upstream_ref,
    window_ref,
    act_ref,
    keep_ref,
    send_ref,
    rows_ref,
    table_ref,
    grad_ref,
):
    voxels = pooled_ref.shape[0]
    rim = jnp.concatenate([left_ref[...], right_ref[...], below_ref[...], above_ref[...]], axis=0)
    for k in range(OFFS):
        match = hot(src_ref[:, k : k + 1] == iota((256, 256), 1) + voxels)
        rows = picked_ref[k * 256 : (k + 1) * 256, :].astype(F32) + dot(match, rim)
        rows_ref[k * 256 : (k + 1) * 256, :] = rows.astype(BF)
    for k in range(OFFS):
        place = hot(dst_ref[k : k + 1, :] == iota((voxels, 256), 0))
        table_ref[:, k * 128 : (k + 1) * 128] = dot(place, rows_ref[k * 256 : (k + 1) * 256, :]).astype(BF)
    table_ref[:, OFFS * 128 :] = pooled_ref[...]
    for m in range(0, voxels, 512):
        pre = dot(table_ref[m : m + 512, :], weight_ref[...])
        sigma = 1.0 / (1.0 + jnp.exp(-pre))
        act_ref[m : m + 512, :] = (pre * sigma).astype(BF)
        slope = sigma * (1.0 + pre * (1.0 - sigma))
        grad = upstream_ref[m : m + 512, :].astype(F32) * slope
        grad_ref[:, m : m + 512] = grad.T.astype(BF)
    first = core_ref[0] == 0
    wide = 9 * 128
    for n in range(0, (OFFS + 1) * 128, wide):
        full = dot(grad_ref[...], table_ref[:, n : n + wide])
        for at in range(0, wide, 128):
            lo, hi = full[:128, at : at + 128], full[128:, at : at + 128]
            keep_ref[n + at : n + at + 128, :] = jnp.where(first, lo, hi).T.astype(BF)
            send_ref[n + at : n + at + 128, :] = jnp.where(first, hi, lo).T.astype(BF)
    base = (OFFS + 1) * 128
    full = dot_rows(act_ref[...], window_ref[...])
    for at in range(0, wide, 128):
        lo, hi = full[:128, at : at + 128], full[128:, at : at + 128]
        keep_ref[base + at : base + at + 128, :] = jnp.where(first, lo, hi).astype(BF)
        send_ref[base + at : base + at + 128, :] = jnp.where(first, hi, lo).astype(BF)


def column_kernel(core_ref, cell_ref, act_ref, keep_ref, send_ref):
    core, here = core_ref[0], core_ref[1]
    for d in range(4):
        y = (here + d) & 3
        for out_ref, which in ((send_ref, 1 - core), (keep_ref, core)):
            for m in range(0, 512, 256):
                start = (y * 2 + which) * 512 + m
                match = hot(cell_ref[...] - start == iota((256, cell_ref.shape[1]), 0))
                out_ref[d * 512 + m : d * 512 + m + 256, :] = dot(match, act_ref[...]).astype(BF)


def shifts(rows):
    total = rows.shape[0]
    y = iota(rows.shape, 0) & 63
    wide = rows.astype(F32)
    lower = jnp.where(y == 0, 0.0, pltpu.roll(wide, 1, 0))
    upper = jnp.where(y == 63, 0.0, pltpu.roll(wide, total - 1, 0))
    return [lower.astype(BF), rows, upper.astype(BF)]


def window_kernel(cell_ref, low_ref, cot_ref, high_ref, weight_ref, window_ref, up_ref, pad_ref, rows_ref):
    voxels = window_ref.shape[0]
    pad_ref[:, 0:8, :] = jnp.zeros((66, 8, 128), F32)
    pad_ref[:, 72:80, :] = jnp.zeros((66, 8, 128), F32)
    pad_ref[0, 8:72, :] = low_ref[...].astype(F32)
    pad_ref[1:65, 8:72, :] = cot_ref[...].reshape(64, 64, 128).astype(F32)
    pad_ref[65, 8:72, :] = high_ref[...].astype(F32)

    def step_window(v, carry):
        cell = cell_ref[v]
        x = cell >> 6
        y = (cell & 63) + 7
        for a in range(3):
            rows_ref[a, pl.ds(v * 4, 4), :] = pad_ref[x + (2 - a), pl.ds(y, 4), :]
        return carry

    lax.fori_loop(0, voxels, step_window, 0, unroll=16)
    up = jnp.zeros(up_ref.shape, F32)
    for a in range(3):
        for b in range(3):
            k = 3 * a + b
            rows = rows_ref[a, pl.ds(2 - b, voxels, stride=4), :].astype(BF)
            window_ref[:, k * 128 : (k + 1) * 128] = rows
            up = up + dot_lanes(rows, weight_ref[k])
    up_ref[...] = up.astype(BF)


def final_kernel(mine_ref, theirs_ref, mine_head_ref, theirs_head_ref, core_ref, conv_ref, head_ref):
    first = core_ref[0] == 0
    mine, theirs = mine_ref[...].astype(F32), theirs_ref[...].astype(F32)
    conv_ref[:, :, 0:128] = jnp.where(first, mine, theirs)
    conv_ref[:, :, 128:256] = jnp.where(first, theirs, mine)
    mine, theirs = mine_head_ref[...].astype(F32), theirs_head_ref[...].astype(F32)
    head_ref[:, 0:128, :] = jnp.where(first, mine, theirs)
    head_ref[:, 128:256, :] = jnp.where(first, theirs, mine)


def join(mine, theirs, core):
    block = lambda i: (i, 0, 0)
    head = lambda i: (i + OFFS + 1, 0, 0)
    return pl.pallas_call(
        final_kernel,
        grid=(9,),
        out_shape=[
            jax.ShapeDtypeStruct((OFFS + 1, 128, 256), F32),
            jax.ShapeDtypeStruct((9, 256, 128), F32),
        ],
        in_specs=[
            pl.BlockSpec((3, 128, 128), block),
            pl.BlockSpec((3, 128, 128), block),
            pl.BlockSpec((1, 128, 128), head),
            pl.BlockSpec((1, 128, 128), head),
            SMEM,
        ],
        out_specs=[pl.BlockSpec((3, 128, 256), block), pl.BlockSpec((1, 256, 128), block)],
    )(mine, theirs, mine, theirs, core)


def head_kernel(low_ref, own_ref, high_ref, weight_ref, out_ref, moved_ref):
    size = own_ref.shape[0]
    for at, ref in ((0, low_ref), (64, own_ref), (64 + size, high_ref)):
        for b, moved in enumerate(shifts(ref[...])):
            moved_ref[b, at : at + ref.shape[0], :] = moved
    total = jnp.zeros(out_ref.shape, F32)
    for a in range(3):
        for b in range(3):
            total = total + dot(moved_ref[b, a * 64 : a * 64 + size, :], weight_ref[3 * a + b])
    out_ref[...] = total.astype(BF)


def chain(block, axes, by):
    count = lax.axis_size(axes)
    return lax.ppermute(
        block, axes, [(i, i + by) for i in range(count) if 0 <= i + by < count]
    )


def swap(block):
    return lax.ppermute(block, "c", [(0, 1), (1, 0)])


def exchange(block, axes):
    return lax.all_to_all(block, axes, split_axis=0, concat_axis=0, tiled=True)


def local(
    points,
    point_brick,
    point_voxel,
    send_rows,
    pair_in,
    pair_out,
    bev_cell,
    conv_weight,
    head_weight,
    head_cot,
):
    shape = jax.ShapeDtypeStruct
    voxels = bev_cell.shape[2]
    total = points.shape[0]
    core = jnp.stack([lax.axis_index("c"), lax.axis_index("y")]).astype(I32)

    ready = call(
        fill_kernel,
        shape((128, ROWS, 128), BF),
        (point_brick.reshape(1, total), point_voxel.reshape(1, total), points),
        scratch=[pltpu.VMEM((1, total), I32)],
        flops=3 << 30,
    )
    cot = head_cot.reshape(-1, 128)
    cells = cot.shape[0]
    cot_low = chain(cot[cells - 64 :], PLANE, 1)
    cot_high = chain(cot[:64], PLANE, -1)
    ready, cot_low, cot_high = lax.optimization_barrier((ready, cot_low, cot_high))
    got = exchange(ready, ALL)

    window, upstream = call(
        window_kernel,
        [shape((voxels, 9 * 128), BF), shape((voxels, 256), BF)],
        (bev_cell.reshape(voxels), cot_low, cot, cot_high, head_weight),
        specs=[SMEM] + [VMEM] * 4,
        scratch=[pltpu.VMEM((66, 80, 128), F32), pltpu.VMEM((3, 4 * voxels, 128), F32)],
        flops=1 << 30,
    )

    pooled, outgoing = call(
        pool_kernel,
        [shape((voxels, 128), BF), shape((256, 128), BF)],
        (got, send_rows.reshape(256, 1)),
        scratch=[pltpu.VMEM((voxels, 128), F32)],
        flops=2 << 30,
    )
    from_left = chain(outgoing[64:128], PLANE, 1)
    from_right = chain(outgoing[0:64], PLANE, -1)
    from_below = chain(outgoing[192:256], HEIGHT, 1)
    from_above = chain(outgoing[128:192], HEIGHT, -1)
    sources = jnp.transpose(pair_in[0, 0])
    picked = call(
        gather_kernel,
        shape((OFFS * 256, 128), BF),
        (pooled, sources),
        scratch=[pltpu.VMEM((1024, voxels), BF)],
        flops=3 << 30,
    )
    table_width = (OFFS + 1) * 128
    grad_rows = table_width + 9 * 128
    act, keep, send = call(
        conv_kernel,
        [shape((voxels, 256), BF), shape((grad_rows, 128), BF), shape((grad_rows, 128), BF)],
        (
            core,
            pooled,
            picked,
            from_left,
            from_right,
            from_below,
            from_above,
            sources,
            pair_out[0, 0],
            conv_weight.reshape(table_width, 256),
            upstream,
            window,
        ),
        specs=[SMEM] + [VMEM] * 11,
        scratch=[
            pltpu.VMEM((OFFS * 256, 128), BF),
            pltpu.VMEM((voxels, table_width), BF),
            pltpu.VMEM((256, voxels), BF),
        ],
        flops=8 << 30,
    )

    both = (keep.astype(F32) + swap(send).astype(F32)).astype(BF)
    both, act = lax.optimization_barrier((both, act))
    shares = exchange(both.reshape(64, grad_rows // 64, 128), ("x", "z", "y"))
    column_keep, column_send = call(
        column_kernel,
        [shape((2048, 256), BF), shape((2048, 256), BF)],
        (core, bev_cell.reshape(1, voxels), act),
        specs=[SMEM, VMEM, VMEM],
        flops=3 << 30,
    )
    column = (column_keep.astype(F32) + swap(column_send).astype(F32)).astype(BF)
    bev = column[:512].astype(F32)
    for d in (1, 2, 3):
        sent = column[d * 512 : (d + 1) * 512]
        bev = bev + lax.ppermute(sent, "y", [(i, (i + d) % 4) for i in range(4)]).astype(F32)
    bev = bev.astype(BF)
    share = jnp.sum(shares.astype(F32), axis=0).astype(BF)
    share, bev = lax.optimization_barrier((share, bev))
    mine = exchange(
        jnp.broadcast_to(share[None], (64,) + share.shape), ("x", "z", "y")
    ).reshape(36, 128, 128)
    bev_low = chain(bev[448:], ALL, 1)
    bev_high = chain(bev[:64], ALL, -1)
    head_out = call(
        head_kernel,
        shape((512, 128), BF),
        (bev_low, bev, bev_high, head_weight),
        scratch=[pltpu.VMEM((3, 640, 256), BF)],
        flops=1 << 30,
    )

    mine, head_out = lax.optimization_barrier((mine, head_out))
    conv_grad, head_grad = join(mine, swap(mine), core)
    return (head_out.reshape(8, 64, 128), conv_grad, head_grad)


def solution(mesh):
    grid = Mesh(mesh.devices.reshape(4, 4, 4, 2), ALL)
    in_specs = (
        P(ALL, None),
        P(ALL, None),
        P(ALL),
        P(PLANE, HEIGHT, None, None),
        P(PLANE, HEIGHT, None, None),
        P(PLANE, HEIGHT, None, None),
        P(PLANE, HEIGHT, None),
        P(),
        P(),
        P(PLANE, None, None),
    )
    out_specs = (P(ALL, None, None), P(), P())
    return jax.shard_map(local, mesh=grid, in_specs=in_specs, out_specs=out_specs, check_vma=False)
```

time: 204 us -> 175 us (0.86)
  blocking collectives: 46.9 us -> 0 us
  starting transfers between devices: 39.7 us -> 57.3 us
  waiting for transfers between devices: 28.7 us -> 44.5 us
  Pallas kernels: 68.5 us -> 53.7 us
    all_to_all x2 -> x0, blocking collectives: 46.9 us -> none  [exchange(): return lax.all_to_all(block, axes, split_axis=0, concat_axis=0, tiled=True)]
    pallas_call x7, Pallas kernels: 68.5 us -> 47 us  [call(): pl.pallas_call(kernel, out_shape=outs, in_specs=[VMEM] * len(args) if spe...]
    all_to_all x2 -> x3, waiting for transfers between devices: 12.1 us -> 22.4 us  [exchange(): return lax.all_to_all(block, axes, split_axis=0, concat_axis=0, tiled=True)]
    all_to_all x2 -> x3, starting transfers between devices: 16.6 us -> 26.3 us  [exchange(): return lax.all_to_all(block, axes, split_axis=0, concat_axis=0, tiled=True)]
    ppermute x0 -> x3, waiting for transfers between devices: none -> 7.3 us  [local(): lax.ppermute(sent, 'y', [(i, (i + d) % 4) for i in range(4)]).astype(F32)]
    pallas_call x0 -> x1, Pallas kernels: none -> 6.74 us  [join(): pl.pallas_call(final_kernel, grid=(9,), out_shape=[jax.ShapeDtypeStruct((...]
    ppermute x0 -> x3, starting transfers between devices: none -> 4.99 us  [local(): lax.ppermute(sent, 'y', [(i, (i + d) % 4) for i in range(4)]).astype(F32)]
    ppermute x8, waiting for transfers between devices: 14 us -> 9.09 us  [chain(): lax.ppermute(block, axes, [(i, i + by) for i in range(count) if 0 <= i +...]
  transfers between devices with their start and end apart: 13 -> 17, of which waited for: 5 -> 8; matrix products, arithmetic and copies ran while one was open for 4% -> 3% of each run, Pallas kernels for 16% -> 13%
where the time goes in v2:
time: 175 us; the launch traced here: 173 us
  starting transfers between devices  57.3 us (33%)
  Pallas kernels  53.7 us (31%)
  waiting for transfers between devices  44.5 us (25%)
  local copies, waits for them, and re-layouts  10.6 us (6%)
  other arithmetic  5.65 us (3%)
    pallas_call x7, Pallas kernels, call(): pl.pallas_call(kernel, out_shape=outs, in_specs=[VMEM] * len(args) if spe...  47 us
    all_to_all x3, starting transfers between devices, exchange(): return lax.all_to_all(block, axes, split_axis=0, concat_axis=0, tiled=True)  26.3 us
    ppermute x8, starting transfers between devices, chain(): lax.ppermute(block, axes, [(i, i + by) for i in range(count) if 0 <= i +...  25.4 us
    all_to_all x3, waiting for transfers between devices, exchange(): return lax.all_to_all(block, axes, split_axis=0, concat_axis=0, tiled=True)  22.4 us
    ppermute x8, waiting for transfers between devices, chain(): lax.ppermute(block, axes, [(i, i + by) for i in range(count) if 0 <= i +...  9.09 us
    ppermute x3, waiting for transfers between devices, local(): lax.ppermute(sent, 'y', [(i, (i + d) % 4) for i in range(4)]).astype(F32)  7.3 us
    pallas_call x1, Pallas kernels, join(): pl.pallas_call(final_kernel, grid=(9,), out_shape=[jax.ShapeDtypeStruct((...  6.74 us
    unnamed x38, local copies, waits for them, and re-layouts  6.33 us
  transfers between devices with their start and end apart: 17, of which 8 were waited for; matrix products, arithmetic and copies ran while one was open for 3% of the time, Pallas kernels for 13%

profile of v2, /device:TPU:2, one launch (start us, length us, event | category | flops | bytes accessed | tf_op | source)
XLA Modules:
  0.0 172.5 jit_solution(14784116853119017648)
XLA Ops:
  1.4 5.9 %collective-permute-start.1 = (bf16[64,128]{1,0:T(8,128)(2,1)S(1)}, bf16[64,128]{1,0:T(8,128)(2,1)S(1)}, u32[]{:S(2)}, u32[]{:S(2)}) collective-permute-start(bf16[64,128]{1,0:T(8,128)(2,1)S(1)} %get-tuple-element.46), channel_id=1, source_target_pairs={{8,0},{16,8},{24,16},{32,24},{40,32},{48,40},{56,48},{64,56},{72,6... | collective-permute-start | bytes 49160 | tf_op jit(solution)/shard_map/ppermute | solution.py:260
  9.2 7.4 %shard_map.121 = bf16[128,40,128]{2,1,0:T(8,128)(2,1)} custom-call(s32[1,2048]{1,0:T(1,128)} %bitcast.29, s32[1,2048]{1,0:T(1,128)} %bitcast.30, bf16[2048,128]{1,0:T(8,128)(2,1)} %points_ref.1), custom_call_target="tpu_custom_call" | custom-call | flops 3221225472 | bytes 4194304 | tf_op jit(solution)/shard_map/pallas_call | solution.py:44
  17.3 10.6 %all-to-all-start = ((bf16[128,40,128]{2,1,0:T(8,128)(2,1)}), bf16[128,40,128]{2,1,0:T(8,128)(2,1)S(1)}, u32[]{:S(2)}, u32[]{:S(2)}) async-start(bf16[128,40,128]{2,1,0:T(8,128)(2,1)} %shard_map.121), calls=%async_computation | async-start | bytes 2621440 | tf_op jit(solution)/shard_map/all_to_all | solution.py:270
  30.8 7.2 %shard_map.124 = (bf16[1024,1152]{1,0:T(8,128)(2,1)}, bf16[1024,256]{1,0:T(8,128)(2,1)}) custom-call(s32[1024]{0:T(1024)} %bitcast.31, bf16[64,128]{1,0:T(8,128)(2,1)} %copy-done.15, bf16[4096,128]{1,0:T(8,128)(2,1)} %bitcast.27, bf16[64,128]{1,0:T(8,128)(2,1)} %copy-done.13, bf16[9,256,128]{2,1,0:T(8,128)(2,1)} %weight_ref.3), custom_call_target="tpu_custom_call" | custom-call | flops 1073741824 | bytes 4194304 | tf_op jit(solution)/shard_map/pallas_call | solution.py:44
  38.0 11.6 %all-to-all-done.got_ref = bf16[128,40,128]{2,1,0:T(8,128)(2,1)S(1)} async-done(((bf16[128,40,128]{2,1,0:T(8,128)(2,1)}), bf16[128,40,128]{2,1,0:T(8,128)(2,1)S(1)}, u32[]{:S(2)}, u32[]{:S(2)}) %all-to-all-start) | async-done | bytes 1310752 | tf_op jit(solution)/shard_map/all_to_all | solution.py:270
  50.6 4.6 %shard_map.122 = (bf16[1024,128]{1,0:T(8,128)(2,1)}, bf16[256,128]{1,0:T(8,128)(2,1)}) custom-call(bf16[128,40,128]{2,1,0:T(8,128)(2,1)} %copy-done.2, s32[256,1]{1,0:T(8,128)} %reshape.49.rim_ref), custom_call_target="tpu_custom_call" | custom-call | flops 2147483648 | bytes 4194304 | tf_op jit(solution)/shard_map/pallas_call | solution.py:44
  57.3 3.0 %collective-permute-start.4 = (bf16[64,128]{1,0:T(8,128)(2,1)S(1)}, bf16[64,128]{1,0:T(8,128)(2,1)S(1)}, u32[]{:S(2)}, u32[]{:S(2)}) collective-permute-start(bf16[64,128]{1,0:T(8,128)(2,1)S(1)} %get-tuple-element.51), channel_id=1, source_target_pairs={{0,1},{1,2},{2,3},{3,4},{4,5},{5,6},{6,7},{8,9},{9,10},{10,11},{11... | collective-permute-start | bytes 49160 | tf_op jit(solution)/shard_map/ppermute | solution.py:260
  60.3 3.1 %collective-permute-start.3 = (bf16[64,128]{1,0:T(8,128)(2,1)S(1)}, bf16[64,128]{1,0:T(8,128)(2,1)S(1)}, u32[]{:S(2)}, u32[]{:S(2)}) collective-permute-start(bf16[64,128]{1,0:T(8,128)(2,1)S(1)} %get-tuple-element.52), channel_id=1, source_target_pairs={{8,0},{16,8},{24,16},{32,24},{40,32},{48,40},{56,48},{64,56},{72,6... | collective-permute-start | bytes 49160 | tf_op jit(solution)/shard_map/ppermute | solution.py:260
  63.4 2.9 %collective-permute-start.2 = (bf16[64,128]{1,0:T(8,128)(2,1)S(1)}, bf16[64,128]{1,0:T(8,128)(2,1)S(1)}, u32[]{:S(2)}, u32[]{:S(2)}) collective-permute-start(bf16[64,128]{1,0:T(8,128)(2,1)S(1)} %get-tuple-element.53), channel_id=1, source_target_pairs={{0,8},{8,16},{16,24},{24,32},{32,40},{40,48},{48,56},{56,64},{64,7... | collective-permute-start | bytes 49160 | tf_op jit(solution)/shard_map/ppermute | solution.py:260
  66.4 5.9 %shard_map.123.picked_ref = bf16[6656,128]{1,0:T(8,128)(2,1)} custom-call(bf16[1024,128]{1,0:T(8,128)(2,1)} %get-tuple-element.24.pooled_ref, s32[256,26]{1,0:T(8,128)} %bitcast.24), custom_call_target="tpu_custom_call" | custom-call | flops 3221225472 | bytes 4194304 | tf_op jit(solution)/shard_map/pallas_call | solution.py:44
  73.0 14.7 %shard_map.125 = (bf16[1024,256]{1,0:T(8,128)(2,1)}, bf16[4608,128]{1,0:T(8,128)(2,1)}, bf16[4608,128]{1,0:T(8,128)(2,1)}) custom-call(s32[2]{0:T(128)} %pad_add_fusion.core_ref, bf16[1024,128]{1,0:T(8,128)(2,1)} %get-tuple-element.24.pooled_ref, bf16[6656,128]{1,0:T(8,128)(2,1)} %shard_map.123.picked_ref, bf16[64,128]{1,0:T(8,128)(2,1)} %copy-done.17, ...), custom_call_target="tpu_custom_call" | custom-call | flops 8589934592 | bytes 4194304 | tf_op jit(solution)/shard_map/pallas_call | solution.py:44
  88.0 2.8 %collective-permute-done.6 = bf16[4608,128]{1,0:T(8,128)(2,1)S(1)} collective-permute-done((bf16[4608,128]{1,0:T(8,128)(2,1)}, bf16[4608,128]{1,0:T(8,128)(2,1)S(1)}, u32[]{:S(2)}, u32[]{:S(2)}) %collective-permute-start.6) | collective-permute-done | bytes 1179680 | tf_op jit(solution)/shard_map/ppermute | solution.py:266
  90.8 2.6 %add_convert_fusion = bf16[4608,128]{1,0:T(8,128)(2,1)} fusion(bf16[4608,128]{1,0:T(8,128)(2,1)S(1)} %collective-permute-done.6, bf16[4608,128]{1,0:T(8,128)(2,1)} %get-tuple-element.30), kind=kLoop, calls=%fused_computation | loop fusion | flops 2359296 | bytes 3538944 | tf_op jit(solution)/shard_map/convert_element_type | solution.py:360
  93.4 4.4 %shard_map.126 = (bf16[2048,256]{1,0:T(8,128)(2,1)}, bf16[2048,256]{1,0:T(8,128)(2,1)}) custom-call(s32[2]{0:T(128)} %pad_add_fusion.core_ref, s32[1,1024]{1,0:T(1,128)} %bitcast.32, bf16[1024,256]{1,0:T(8,128)(2,1)} %get-tuple-element.34.act_ref), custom_call_target="tpu_custom_call" | custom-call | flops 3221225472 | bytes 4194304 | tf_op jit(solution)/shard_map/pallas_call | solution.py:44
  98.1 7.3 %all-to-all-start.1 = ((bf16[64,72,128]{2,1,0:T(8,128)(2,1)}), bf16[64,72,128]{2,1,0:T(8,128)(2,1)S(1)}, u32[]{:S(2)}, u32[]{:S(2)}) async-start(bf16[64,72,128]{2,1,0:T(8,128)(2,1)} %bitcast.11), calls=%async_computation.1 | async-start | bytes 2359296 | tf_op jit(solution)/shard_map/all_to_all | solution.py:270
  113.6 10.9 %all-to-all-done.1 = bf16[64,72,128]{2,1,0:T(8,128)(2,1)S(1)} async-done(((bf16[64,72,128]{2,1,0:T(8,128)(2,1)}), bf16[64,72,128]{2,1,0:T(8,128)(2,1)S(1)}, u32[]{:S(2)}, u32[]{:S(2)}) %all-to-all-start.1) | async-done | bytes 1179680 | tf_op jit(solution)/shard_map/all_to_all | solution.py:270
  127.1 5.4 %collective-permute-done.9 = bf16[512,256]{1,0:T(8,128)(2,1)S(1)} collective-permute-done((bf16[512,256]{1,0:T(8,128)(2,1)S(1)}, bf16[512,256]{1,0:T(8,128)(2,1)S(1)}, u32[]{:S(2)}, u32[]{:S(2)}) %collective-permute-start.9) | collective-permute-done | bytes 262176 | tf_op jit(solution)/shard_map/ppermute | solution.py:374
  133.9 8.4 %all-to-all-start.2 = ((bf16[64,72,128]{2,1,0:T(8,128)(2,1)}), bf16[64,72,128]{2,1,0:T(8,128)(2,1)S(1)}, u32[]{:S(2)}, u32[]{:S(2)}) async-start(bf16[64,72,128]{2,1,0:T(8,128)(2,1)} %broadcast_in_dim.2), calls=%async_computation.2 | async-start | bytes 2359296 | tf_op jit(solution)/shard_map/all_to_all | solution.py:270
  142.3 5.4 %collective-permute-start.12 = (bf16[64,256]{1,0:T(8,128)(2,1)S(1)}, bf16[64,256]{1,0:T(8,128)(2,1)S(1)}, u32[]{:S(2)}, u32[]{:S(2)}) collective-permute-start(bf16[64,256]{1,0:T(8,128)(2,1)S(1)} %get-tuple-element.48), channel_id=1, source_target_pairs={{1,0},{2,1},{3,2},{4,3},{5,4},{6,5},{7,6},{8,7},{9,8},{10,9},{11,1... | collective-permute-start | bytes 98312 | tf_op jit(solution)/shard_map/ppermute | solution.py:260
  149.6 5.0 %collective-permute-done.12.high_ref = bf16[64,256]{1,0:T(8,128)(2,1)S(1)} collective-permute-done((bf16[64,256]{1,0:T(8,128)(2,1)S(1)}, bf16[64,256]{1,0:T(8,128)(2,1)S(1)}, u32[]{:S(2)}, u32[]{:S(2)}) %collective-permute-start.12) | collective-permute-done | bytes 32800 | tf_op jit(solution)/shard_map/ppermute | solution.py:260
  154.6 4.1 %collective-permute-done.11.low_ref = bf16[64,256]{1,0:T(8,128)(2,1)S(1)} collective-permute-done((bf16[64,256]{1,0:T(8,128)(2,1)S(1)}, bf16[64,256]{1,0:T(8,128)(2,1)S(1)}, u32[]{:S(2)}, u32[]{:S(2)}) %collective-permute-start.11) | collective-permute-done | bytes 32800 | tf_op jit(solution)/shard_map/ppermute | solution.py:260
  159.3 2.6 %shard_map.127 = bf16[512,128]{1,0:T(8,128)(2,1)} custom-call(bf16[64,256]{1,0:T(8,128)(2,1)} %copy-done.11, bf16[512,256]{1,0:T(8,128)(2,1)} %copy-done.5, bf16[64,256]{1,0:T(8,128)(2,1)} %copy-done.10, bf16[9,256,128]{2,1,0:T(8,128)(2,1)} %weight_ref.3), custom_call_target="tpu_custom_call" | custom-call | flops 1073741824 | bytes 4194304 | tf_op jit(solution)/shard_map/pallas_call | solution.py:44
  161.9 2.8 %collective-permute-done.13.theirs_ref.theirs_head_ref = bf16[36,128,128]{2,1,0:T(8,128)(2,1)S(1)} collective-permute-done((bf16[36,128,128]{2,1,0:T(8,128)(2,1)S(1)}, bf16[36,128,128]{2,1,0:T(8,128)(2,1)S(1)}, u32[]{:S(2)}, u32[]{:S(2)}) %collective-permute-start.13) | collective-permute-done | bytes 1179680 | tf_op jit(solution)/shard_map/ppermute | solution.py:266
  165.8 6.7 %shard_map.128 = (f32[27,128,256]{2,1,0:T(8,128)}, f32[9,256,128]{2,1,0:T(8,128)}) custom-call(bf16[36,128,128]{2,1,0:T(8,128)(2,1)} %bitcast.22, bf16[36,128,128]{2,1,0:T(8,128)(2,1)} %copy-done.1, bf16[36,128,128]{2,1,0:T(8,128)(2,1)} %bitcast.23, bf16[36,128,128]{2,1,0:T(8,128)(2,1)} %copy-done.1, s32[2]{0:T(128)} %pad_add_fusion.core_ref), custom_call_target="tpu_custom_call" | custom-call | tf_op jit(solution)/shard_map/pallas_call | solution.py:228
  (67 shorter events, 26.1 us)
Async XLA Ops:
  1.4 15.3 %collective-permute-start.1 = (bf16[64,128]{1,0:T(8,128)(2,1)S(1)}, bf16[64,128]{1,0:T(8,128)(2,1)S(1)}, u32[]{:S(2)}, u32[]{:S(2)}) collective-permute-start(bf16[64,128]{1,0:T(8,128)(2,1)S(1)} %get-tuple-element.46), channel_id=1, source_target_pairs={{8,0},{16,8},{24,16},{32,24},{40,32},{48,40},{56,48},{64,56},{72,6... | collective-permute-start | bytes 49160 | tf_op jit(solution)/shard_map/ppermute | solution.py:260
  7.3 9.4 %collective-permute-start = (bf16[64,128]{1,0:T(8,128)(2,1)S(1)}, bf16[64,128]{1,0:T(8,128)(2,1)S(1)}, u32[]{:S(2)}, u32[]{:S(2)}) collective-permute-start(bf16[64,128]{1,0:T(8,128)(2,1)S(1)} %get-tuple-element.47), channel_id=1, source_target_pairs={{0,8},{8,16},{16,24},{24,32},{32,40},{40,48},{48,56},{56,64},{64,7... | collective-permute-start | bytes 49160 | tf_op jit(solution)/shard_map/ppermute | solution.py:260
  16.6 11.3 %copy-start.8 = (s32[1,1,26,256]{3,1,2,0:T(1,128)S(1)}, s32[1,1,26,256]{3,1,2,0:T(1,128)}, u32[]{:S(2)}) copy-start(s32[1,1,26,256]{3,1,2,0:T(1,128)} %param.15) | copy-start | bytes 79876
  16.6 11.9 %copy-start.9 = (s32[1,1,4,64]{3,2,1,0:T(4,128)S(1)}, s32[1,1,4,64]{3,2,1,0:T(4,128)}, u32[]{:S(2)}) copy-start(s32[1,1,4,64]{3,2,1,0:T(4,128)} %param.13) | copy-start | bytes 3076
  16.6 12.7 %copy-start.7 = (s32[1,1,26,256]{3,1,2,0:T(1,128)S(1)}, s32[1,1,26,256]{3,1,2,0:T(1,128)}, u32[]{:S(2)}) copy-start(s32[1,1,26,256]{3,1,2,0:T(1,128)} %param.14) | copy-start | bytes 79876
  17.3 32.3 %all-to-all-start = ((bf16[128,40,128]{2,1,0:T(8,128)(2,1)}), bf16[128,40,128]{2,1,0:T(8,128)(2,1)S(1)}, u32[]{:S(2)}, u32[]{:S(2)}) async-start(bf16[128,40,128]{2,1,0:T(8,128)(2,1)} %shard_map.121), calls=%async_computation | async-start | bytes 2621440 | tf_op jit(solution)/shard_map/all_to_all | solution.py:270
  56.0 16.3 %collective-permute-start.5 = (bf16[64,128]{1,0:T(8,128)(2,1)S(1)}, bf16[64,128]{1,0:T(8,128)(2,1)S(1)}, u32[]{:S(2)}, u32[]{:S(2)}) collective-permute-start(bf16[64,128]{1,0:T(8,128)(2,1)S(1)} %get-tuple-element.50), channel_id=1, source_target_pairs={{1,0},{2,1},{3,2},{4,3},{5,4},{6,5},{7,6},{9,8},{10,9},{11,10},{12... | collective-permute-start | bytes 49160 | tf_op jit(solution)/shard_map/ppermute | solution.py:260
  57.3 15.0 %collective-permute-start.4 = (bf16[64,128]{1,0:T(8,128)(2,1)S(1)}, bf16[64,128]{1,0:T(8,128)(2,1)S(1)}, u32[]{:S(2)}, u32[]{:S(2)}) collective-permute-start(bf16[64,128]{1,0:T(8,128)(2,1)S(1)} %get-tuple-element.51), channel_id=1, source_target_pairs={{0,1},{1,2},{2,3},{3,4},{4,5},{5,6},{6,7},{8,9},{9,10},{10,11},{11... | collective-permute-start | bytes 49160 | tf_op jit(solution)/shard_map/ppermute | solution.py:260
  60.3 12.0 %collective-permute-start.3 = (bf16[64,128]{1,0:T(8,128)(2,1)S(1)}, bf16[64,128]{1,0:T(8,128)(2,1)S(1)}, u32[]{:S(2)}, u32[]{:S(2)}) collective-permute-start(bf16[64,128]{1,0:T(8,128)(2,1)S(1)} %get-tuple-element.52), channel_id=1, source_target_pairs={{8,0},{16,8},{24,16},{32,24},{40,32},{48,40},{56,48},{64,56},{72,6... | collective-permute-start | bytes 49160 | tf_op jit(solution)/shard_map/ppermute | solution.py:260
  63.4 8.9 %collective-permute-start.2 = (bf16[64,128]{1,0:T(8,128)(2,1)S(1)}, bf16[64,128]{1,0:T(8,128)(2,1)S(1)}, u32[]{:S(2)}, u32[]{:S(2)}) collective-permute-start(bf16[64,128]{1,0:T(8,128)(2,1)S(1)} %get-tuple-element.53), channel_id=1, source_target_pairs={{0,8},{8,16},{16,24},{24,32},{32,40},{40,48},{48,56},{56,64},{64,7... | collective-permute-start | bytes 49160 | tf_op jit(solution)/shard_map/ppermute | solution.py:260
  87.7 3.1 %collective-permute-start.6 = (bf16[4608,128]{1,0:T(8,128)(2,1)}, bf16[4608,128]{1,0:T(8,128)(2,1)S(1)}, u32[]{:S(2)}, u32[]{:S(2)}) collective-permute-start(bf16[4608,128]{1,0:T(8,128)(2,1)} %get-tuple-element.31), channel_id=1, source_target_pairs={{0,1},{1,0},{2,3},{3,2},{4,5},{5,4},{6,7},{7,6},{8,9},{9,8},{10,11... | collective-permute-start | bytes 3538952 | tf_op jit(solution)/shard_map/ppermute | solution.py:266
  97.8 8.5 %copy-start.3 = (bf16[2048,256]{1,0:T(8,128)(2,1)S(1)}, bf16[2048,256]{1,0:T(8,128)(2,1)}, u32[]{:S(2)}) copy-start(bf16[2048,256]{1,0:T(8,128)(2,1)} %get-tuple-element.35) | copy-start | bytes 3145732
  97.8 7.5 %collective-permute-start.7 = (bf16[2048,256]{1,0:T(8,128)(2,1)}, bf16[2048,256]{1,0:T(8,128)(2,1)S(1)}, u32[]{:S(2)}, u32[]{:S(2)}) collective-permute-start(bf16[2048,256]{1,0:T(8,128)(2,1)} %get-tuple-element.36), channel_id=1, source_target_pairs={{0,1},{1,0},{2,3},{3,2},{4,5},{5,4},{6,7},{7,6},{8,9},{9,8},{10,11... | collective-permute-start | bytes 3145736 | tf_op jit(solution)/shard_map/ppermute | solution.py:266
  98.1 26.4 %all-to-all-start.1 = ((bf16[64,72,128]{2,1,0:T(8,128)(2,1)}), bf16[64,72,128]{2,1,0:T(8,128)(2,1)S(1)}, u32[]{:S(2)}, u32[]{:S(2)}) async-start(bf16[64,72,128]{2,1,0:T(8,128)(2,1)} %bitcast.11), calls=%async_computation.1 | async-start | bytes 2359296 | tf_op jit(solution)/shard_map/all_to_all | solution.py:270
  108.6 18.5 %collective-permute-start.8 = (bf16[512,256]{1,0:T(8,128)(2,1)}, bf16[512,256]{1,0:T(8,128)(2,1)S(1)}, u32[]{:S(2)}, u32[]{:S(2)}) collective-permute-start(bf16[512,256]{1,0:T(8,128)(2,1)} %get-tuple-element.43), channel_id=1, source_target_pairs={{0,2},{2,4},{4,6},{6,0},{1,3},{3,5},{5,7},{7,1},{8,10},{10,12},{12... | collective-permute-start | bytes 786440 | tf_op jit(solution)/shard_map/ppermute | solution.py:374
  110.0 17.1 %collective-permute-start.10 = (bf16[512,256]{1,0:T(8,128)(2,1)S(1)}, bf16[512,256]{1,0:T(8,128)(2,1)S(1)}, u32[]{:S(2)}, u32[]{:S(2)}) collective-permute-start(bf16[512,256]{1,0:T(8,128)(2,1)S(1)} %get-tuple-element.44), channel_id=1, source_target_pairs={{0,6},{2,0},{4,2},{6,4},{1,7},{3,1},{5,3},{7,5},{8,14},{10,8},{12,... | collective-permute-start | bytes 786440 | tf_op jit(solution)/shard_map/ppermute | solution.py:374
  111.8 20.7 %collective-permute-start.9 = (bf16[512,256]{1,0:T(8,128)(2,1)S(1)}, bf16[512,256]{1,0:T(8,128)(2,1)S(1)}, u32[]{:S(2)}, u32[]{:S(2)}) collective-permute-start(bf16[512,256]{1,0:T(8,128)(2,1)S(1)} %get-tuple-element.45), channel_id=1, source_target_pairs={{0,4},{2,6},{4,0},{6,2},{1,5},{3,7},{5,1},{7,3},{8,12},{10,14},{12... | collective-permute-start | bytes 786440 | tf_op jit(solution)/shard_map/ppermute | solution.py:374
  125.2 7.4 %copy-start.6 = (bf16[72,128]{1,0:T(8,128)(2,1)S(1)}, bf16[72,128]{1,0:T(8,128)(2,1)}, u32[]{:S(2)}) copy-start(bf16[72,128]{1,0:T(8,128)(2,1)} %reduce_sum.12) | copy-start | bytes 55300
  132.7 9.6 %copy-start.5 = (bf16[512,256]{1,0:T(8,128)(2,1)}, bf16[512,256]{1,0:T(8,128)(2,1)S(1)}, u32[]{:S(2)}) copy-start(bf16[512,256]{1,0:T(8,128)(2,1)S(1)} %add_convert_fusion.2.own_ref) | copy-start | bytes 786436
  133.9 28.1 %all-to-all-start.2 = ((bf16[64,72,128]{2,1,0:T(8,128)(2,1)}), bf16[64,72,128]{2,1,0:T(8,128)(2,1)S(1)}, u32[]{:S(2)}, u32[]{:S(2)}) async-start(bf16[64,72,128]{2,1,0:T(8,128)(2,1)} %broadcast_in_dim.2), calls=%async_computation.2 | async-start | bytes 2359296 | tf_op jit(solution)/shard_map/all_to_all | solution.py:270
  142.3 12.3 %collective-permute-start.12 = (bf16[64,256]{1,0:T(8,128)(2,1)S(1)}, bf16[64,256]{1,0:T(8,128)(2,1)S(1)}, u32[]{:S(2)}, u32[]{:S(2)}) collective-permute-start(bf16[64,256]{1,0:T(8,128)(2,1)S(1)} %get-tuple-element.48), channel_id=1, source_target_pairs={{1,0},{2,1},{3,2},{4,3},{5,4},{6,5},{7,6},{8,7},{9,8},{10,9},{11,1... | collective-permute-start | bytes 98312 | tf_op jit(solution)/shard_map/ppermute | solution.py:260
  147.7 11.0 %collective-permute-start.11 = (bf16[64,256]{1,0:T(8,128)(2,1)S(1)}, bf16[64,256]{1,0:T(8,128)(2,1)S(1)}, u32[]{:S(2)}, u32[]{:S(2)}) collective-permute-start(bf16[64,256]{1,0:T(8,128)(2,1)S(1)} %get-tuple-element.49), channel_id=1, source_target_pairs={{0,1},{1,2},{2,3},{3,4},{4,5},{5,6},{6,7},{7,8},{8,9},{9,10},{10,1... | collective-permute-start | bytes 98312 | tf_op jit(solution)/shard_map/ppermute | solution.py:260
  154.6 4.1 %copy-start.10 = (bf16[64,256]{1,0:T(8,128)(2,1)}, bf16[64,256]{1,0:T(8,128)(2,1)S(1)}, u32[]{:S(2)}) copy-start(bf16[64,256]{1,0:T(8,128)(2,1)S(1)} %collective-permute-done.12.high_ref) | copy-start | bytes 98308
  161.9 2.8 %collective-permute-start.13 = (bf16[36,128,128]{2,1,0:T(8,128)(2,1)S(1)}, bf16[36,128,128]{2,1,0:T(8,128)(2,1)S(1)}, u32[]{:S(2)}, u32[]{:S(2)}) collective-permute-start(bf16[36,128,128]{2,1,0:T(8,128)(2,1)S(1)} %bitcast.21), channel_id=1, source_target_pairs={{0,1},{1,0},{2,3},{3,2},{4,5},{5,4},{6,7},{7,6},{8,9},{9,8},{10,11... | collective-permute-start | bytes 3538952 | tf_op jit(solution)/shard_map/ppermute | solution.py:266
  (11 other events, 10.2 us)

commit v3 on v2

--- a/solution.py
+++ b/solution.py
@@ -18,6 +18,7 @@
 OFFS = 26
 VMEM = pl.BlockSpec(memory_space=pltpu.VMEM)
 SMEM = pl.BlockSpec(memory_space=pltpu.SMEM)
+ANY = pl.BlockSpec(memory_space=pl.ANY)
 
 
 def iota(shape, axis):
@@ -40,12 +41,12 @@
     return lax.dot_general(a, b, (((1,), (1,)), ((), ())), preferred_element_type=F32)
 
 
-def call(kernel, outs, args, specs=None, scratch=(), flops=0, limit=56):
+def call(kernel, outs, args, specs=None, scratch=(), flops=0, limit=56, out=VMEM):
     return pl.pallas_call(
         kernel,
         out_shape=outs,
         in_specs=[VMEM] * len(args) if specs is None else specs,
-        out_specs=jax.tree.map(lambda _: VMEM, outs),
+        out_specs=jax.tree.map(lambda _: out, outs),
         scratch_shapes=list(scratch),
         compiler_params=pltpu.CompilerParams(vmem_limit_bytes=limit * 1024 * 1024),
         cost_estimate=pl.CostEstimate(flops=flops, bytes_accessed=4 << 20, transcendentals=0),
@@ -100,48 +101,64 @@
     rows_ref[...] = dot(hot(rim_ref[...] == iota((256, voxels), 1)), pooled).astype(BF)
 
 
-def gather_kernel(pooled_ref, src_ref, out_ref, match_ref):
-    voxels = pooled_ref.shape[0]
-    for first in range(0, OFFS, 4):
-        last = min(first + 4, OFFS)
-        for k in range(first, last):
-            match_ref[(k - first) * 256 : (k - first + 1) * 256, :] = hot(
-                src_ref[:, k : k + 1] == iota((256, voxels), 1)
-            )
-        size = (last - first) * 256
-        out_ref[first * 256 : last * 256, :] = dot(match_ref[:size, :], pooled_ref[...]).astype(BF)
-
-
 def conv_kernel(
     core_ref,
     pooled_ref,
-    picked_ref,
     left_ref,
     right_ref,
-    below_ref,
-    above_ref,
+    swapped_ref,
+    paired_ref,
     src_ref,
     dst_ref,
+    weight_any,
+    upstream_any,
+    window_any,
+    act_any,
+    keep_any,
+    send_any,
+    wide_ref,
+    rows_ref,
+    table_ref,
+    grad_ref,
     weight_ref,
     upstream_ref,
     window_ref,
     act_ref,
     keep_ref,
     send_ref,
-    rows_ref,
-    table_ref,
-    grad_ref,
+    sems,
 ):
     voxels = pooled_ref.shape[0]
-    rim = jnp.concatenate([left_ref[...], right_ref[...], below_ref[...], above_ref[...]], axis=0)
+    loads = [
+        pltpu.make_async_copy(weight_any, weight_ref, sems.at[0]),
+        pltpu.make_async_copy(upstream_any, upstream_ref, sems.at[1]),
+        pltpu.make_async_copy(window_any, window_ref, sems.at[2]),
+    ]
+    for load in loads:
+        load.start()
+    first = core_ref[0] == 0
+    for g in range(4):
+        wide_ref[:, g * 128 : (g + 1) * 128] = pooled_ref[g * 256 : (g + 1) * 256, :]
+    swapped, paired = swapped_ref[...].astype(F32), paired_ref[...].astype(F32)
+    wide_ref[0:64, 512:640] = left_ref[...]
+    wide_ref[64:128, 512:640] = right_ref[...]
+    wide_ref[128:192, 512:640] = jnp.where(first, paired, swapped).astype(BF)
+    wide_ref[192:256, 512:640] = jnp.where(first, swapped, paired).astype(BF)
+    row = src_ref[...] & 255
+    group = src_ref[...] >> 8
     for k in range(OFFS):
-        match = hot(src_ref[:, k : k + 1] == iota((256, 256), 1) + voxels)
-        rows = picked_ref[k * 256 : (k + 1) * 256, :].astype(F32) + dot(match, rim)
-        rows_ref[k * 256 : (k + 1) * 256, :] = rows.astype(BF)
+        rows = dot(hot(row[:, k : k + 1] == iota((256, 256), 1)), wide_ref[...])
+        side = jnp.broadcast_to(group[:, k : k + 1], (256, 128))
+        picked = jnp.zeros((256, 128), F32)
+        for g in range(5):
+            picked = jnp.where(side == g, rows[:, g * 128 : (g + 1) * 128], picked)
+        rows_ref[k * 256 : (k + 1) * 256, :] = picked.astype(BF)
     for k in range(OFFS):
         place = hot(dst_ref[k : k + 1, :] == iota((voxels, 256), 0))
         table_ref[:, k * 128 : (k + 1) * 128] = dot(place, rows_ref[k * 256 : (k + 1) * 256, :]).astype(BF)
     table_ref[:, OFFS * 128 :] = pooled_ref[...]
+    loads[0].wait()
+    loads[1].wait()
     for m in range(0, voxels, 512):
         pre = dot(table_ref[m : m + 512, :], weight_ref[...])
         sigma = 1.0 / (1.0 + jnp.exp(-pre))
@@ -149,20 +166,37 @@
         slope = sigma * (1.0 + pre * (1.0 - sigma))
         grad = upstream_ref[m : m + 512, :].astype(F32) * slope
         grad_ref[:, m : m + 512] = grad.T.astype(BF)
-    first = core_ref[0] == 0
+    stores = [pltpu.make_async_copy(act_ref, act_any, sems.at[3])]
+    stores[0].start()
     wide = 9 * 128
-    for n in range(0, (OFFS + 1) * 128, wide):
-        full = dot(grad_ref[...], table_ref[:, n : n + wide])
+    for step in range(3):
+        full = dot(grad_ref[...], table_ref[:, step * wide : (step + 1) * wide])
         for at in range(0, wide, 128):
             lo, hi = full[:128, at : at + 128], full[128:, at : at + 128]
-            keep_ref[n + at : n + at + 128, :] = jnp.where(first, lo, hi).T.astype(BF)
-            send_ref[n + at : n + at + 128, :] = jnp.where(first, hi, lo).T.astype(BF)
+            to = step * wide + at
+            keep_ref[to : to + 128, :] = jnp.where(first, lo, hi).T.astype(BF)
+            send_ref[to : to + 128, :] = jnp.where(first, hi, lo).T.astype(BF)
+    loads[2].wait()
     base = (OFFS + 1) * 128
+    stores += [
+        pltpu.make_async_copy(send_ref.at[0:base], send_any.at[0:base], sems.at[4]),
+        pltpu.make_async_copy(keep_ref.at[0:base], keep_any.at[0:base], sems.at[5]),
+    ]
+    stores[1].start()
+    stores[2].start()
     full = dot_rows(act_ref[...], window_ref[...])
     for at in range(0, wide, 128):
         lo, hi = full[:128, at : at + 128], full[128:, at : at + 128]
         keep_ref[base + at : base + at + 128, :] = jnp.where(first, lo, hi).astype(BF)
         send_ref[base + at : base + at + 128, :] = jnp.where(first, hi, lo).astype(BF)
+    stores += [
+        pltpu.make_async_copy(send_ref.at[base : base + wide], send_any.at[base : base + wide], sems.at[6]),
+        pltpu.make_async_copy(keep_ref.at[base : base + wide], keep_any.at[base : base + wide], sems.at[7]),
+    ]
+    stores[3].start()
+    stores[4].start()
+    for store in stores:
+        store.wait()
 
 
 def column_kernel(core_ref, cell_ref, act_ref, keep_ref, send_ref):
@@ -212,35 +246,36 @@
     up_ref[...] = up.astype(BF)
 
 
-def final_kernel(mine_ref, theirs_ref, mine_head_ref, theirs_head_ref, core_ref, conv_ref, head_ref):
+def final_kernel(mine_ref, theirs_ref, core_ref, conv_any, head_any, conv_ref, head_ref, sems):
     first = core_ref[0] == 0
-    mine, theirs = mine_ref[...].astype(F32), theirs_ref[...].astype(F32)
-    conv_ref[:, :, 0:128] = jnp.where(first, mine, theirs)
-    conv_ref[:, :, 128:256] = jnp.where(first, theirs, mine)
-    mine, theirs = mine_head_ref[...].astype(F32), theirs_head_ref[...].astype(F32)
-    head_ref[:, 0:128, :] = jnp.where(first, mine, theirs)
-    head_ref[:, 128:256, :] = jnp.where(first, theirs, mine)
+    stores = []
+    for i in range(9):
+        for k in range(3 * i, 3 * i + 3):
+            mine, theirs = mine_ref[k].astype(F32), theirs_ref[k].astype(F32)
+            conv_ref[k, :, 0:128] = jnp.where(first, mine, theirs)
+            conv_ref[k, :, 128:256] = jnp.where(first, theirs, mine)
+        part = pl.ds(3 * i, 3)
+        stores.append(pltpu.make_async_copy(conv_ref.at[part], conv_any.at[part], sems.at[2 * i]))
+        stores[-1].start()
+        mine, theirs = mine_ref[OFFS + 1 + i].astype(F32), theirs_ref[OFFS + 1 + i].astype(F32)
+        head_ref[i, 0:128, :] = jnp.where(first, mine, theirs)
+        head_ref[i, 128:256, :] = jnp.where(first, theirs, mine)
+        stores.append(pltpu.make_async_copy(head_ref.at[i], head_any.at[i], sems.at[2 * i + 1]))
+        stores[-1].start()
+    for store in stores:
+        store.wait()
 
 
 def join(mine, theirs, core):
-    block = lambda i: (i, 0, 0)
-    head = lambda i: (i + OFFS + 1, 0, 0)
+    conv, head = (OFFS + 1, 128, 256), (9, 256, 128)
     return pl.pallas_call(
         final_kernel,
-        grid=(9,),
-        out_shape=[
-            jax.ShapeDtypeStruct((OFFS + 1, 128, 256), F32),
-            jax.ShapeDtypeStruct((9, 256, 128), F32),
-        ],
-        in_specs=[
-            pl.BlockSpec((3, 128, 128), block),
-            pl.BlockSpec((3, 128, 128), block),
-            pl.BlockSpec((1, 128, 128), head),
-            pl.BlockSpec((1, 128, 128), head),
-            SMEM,
-        ],
-        out_specs=[pl.BlockSpec((3, 128, 256), block), pl.BlockSpec((1, 256, 128), block)],
-    )(mine, theirs, mine, theirs, core)
+        out_shape=[jax.ShapeDtypeStruct(conv, F32), jax.ShapeDtypeStruct(head, F32)],
+        in_specs=[VMEM, VMEM, SMEM],
+        out_specs=[ANY, ANY],
+        scratch_shapes=[pltpu.VMEM(conv, F32), pltpu.VMEM(head, F32), pltpu.SemaphoreType.DMA((18,))],
+        compiler_params=pltpu.CompilerParams(vmem_limit_bytes=32 * 1024 * 1024),
+    )(mine, theirs, core)
 
 
 def head_kernel(low_ref, own_ref, high_ref, weight_ref, out_ref, moved_ref):
@@ -310,25 +345,24 @@
         flops=1 << 30,
     )
 
+    sides = send_rows[0, 0]
+    even = core[0] == 0
+    sides = jnp.concatenate(
+        [sides[:2], jnp.where(even, sides[3:], sides[2:3]), jnp.where(even, sides[2:3], sides[3:])]
+    )
     pooled, outgoing = call(
         pool_kernel,
         [shape((voxels, 128), BF), shape((256, 128), BF)],
-        (got, send_rows.reshape(256, 1)),
+        (got, sides.reshape(256, 1)),
         scratch=[pltpu.VMEM((voxels, 128), F32)],
         flops=2 << 30,
     )
+    layers = lax.axis_size(HEIGHT)
+    pairs = [(i, i + 1) for i in range(1, layers - 1, 2)]
     from_left = chain(outgoing[64:128], PLANE, 1)
     from_right = chain(outgoing[0:64], PLANE, -1)
-    from_below = chain(outgoing[192:256], HEIGHT, 1)
-    from_above = chain(outgoing[128:192], HEIGHT, -1)
-    sources = jnp.transpose(pair_in[0, 0])
-    picked = call(
-        gather_kernel,
-        shape((OFFS * 256, 128), BF),
-        (pooled, sources),
-        scratch=[pltpu.VMEM((1024, voxels), BF)],
-        flops=3 << 30,
-    )
+    paired = lax.ppermute(outgoing[192:256], HEIGHT, pairs + [(j, i) for i, j in pairs])
+    swapped = swap(outgoing[128:192])
     table_width = (OFFS + 1) * 128
     grad_rows = table_width + 9 * 128
     act, keep, send = call(
@@ -337,29 +371,36 @@
         (
             core,
             pooled,
-            picked,
             from_left,
             from_right,
-            from_below,
-            from_above,
-            sources,
+            swapped,
+            paired,
+            jnp.transpose(pair_in[0, 0]),
             pair_out[0, 0],
             conv_weight.reshape(table_width, 256),
             upstream,
             window,
         ),
-        specs=[SMEM] + [VMEM] * 11,
+        specs=[SMEM] + [VMEM] * 7 + [ANY] * 3,
+        out=ANY,
         scratch=[
+            pltpu.VMEM((256, 5 * 128), BF),
             pltpu.VMEM((OFFS * 256, 128), BF),
             pltpu.VMEM((voxels, table_width), BF),
             pltpu.VMEM((256, voxels), BF),
+            pltpu.VMEM((table_width, 256), BF),
+            pltpu.VMEM((voxels, 256), BF),
+            pltpu.VMEM((voxels, 9 * 128), BF),
+            pltpu.VMEM((voxels, 256), BF),
+            pltpu.VMEM((grad_rows, 128), BF),
+            pltpu.VMEM((grad_rows, 128), BF),
+            pltpu.SemaphoreType.DMA((8,)),
         ],
         flops=8 << 30,
-    )
-
-    both = (keep.astype(F32) + swap(send).astype(F32)).astype(BF)
-    both, act = lax.optimization_barrier((both, act))
-    shares = exchange(both.reshape(64, grad_rows // 64, 128), ("x", "z", "y"))
+        limit=40,
+    )
+
+    arrived = swap(send)
     column_keep, column_send = call(
         column_kernel,
         [shape((2048, 256), BF), shape((2048, 256), BF)],
@@ -367,13 +408,19 @@
         specs=[SMEM, VMEM, VMEM],
         flops=3 << 30,
     )
+    arrived, column_keep, column_send = lax.optimization_barrier((arrived, column_keep, column_send))
+    both = (keep.astype(F32) + arrived.astype(F32)).astype(BF)
+    shares = exchange(both.reshape(64, grad_rows // 64, 128), ("x", "z", "y"))
     column = (column_keep.astype(F32) + swap(column_send).astype(F32)).astype(BF)
+    ahead = [
+        lax.ppermute(column[d * 512 : (d + 1) * 512], "y", [(i, (i + d) % 4) for i in range(4)])
+        for d in (1, 2, 3)
+    ]
+    share = jnp.sum(shares.astype(F32), axis=0).astype(BF)
     bev = column[:512].astype(F32)
-    for d in (1, 2, 3):
-        sent = column[d * 512 : (d + 1) * 512]
-        bev = bev + lax.ppermute(sent, "y", [(i, (i + d) % 4) for i in range(4)]).astype(F32)
+    for part in ahead:
+        bev = bev + part.astype(F32)
     bev = bev.astype(BF)
-    share = jnp.sum(shares.astype(F32), axis=0).astype(BF)
     share, bev = lax.optimization_barrier((share, bev))
     mine = exchange(
         jnp.broadcast_to(share[None], (64,) + share.shape), ("x", "z", "y")

time: 175 us -> 168 us (0.960)
  Pallas kernels: 53.7 us -> 43.5 us
  waiting for transfers between devices: 44.5 us -> 51.2 us
  other arithmetic: 5.65 us -> 3.83 us
    all_to_all x3, waiting for transfers between devices: 22.4 us -> 32.2 us  [exchange(): return lax.all_to_all(block, axes, split_axis=0, concat_axis=0, tiled=True)]
    pallas_call x7 -> x6, Pallas kernels: 47 us -> 40.6 us  [call(): pl.pallas_call(kernel, out_shape=outs, in_specs=[VMEM] * len(args) if spe...]
    ppermute x8 -> x6, starting transfers between devices: 25.4 us -> 21 us  [chain(): lax.ppermute(block, axes, [(i, i + by) for i in range(count) if 0 <= i +...]
    pallas_call x1, Pallas kernels: 6.74 us -> 2.88 us  [join(): pl.pallas_call(final_kernel, out_shape=[jax.ShapeDtypeStruct(conv, F32),...]
    ppermute x3 -> x4, waiting for transfers between devices: 5.65 us -> 2.85 us  [swap(): return lax.ppermute(block, 'c', [(0, 1), (1, 0)])]
    ppermute x3 -> x4, starting transfers between devices: 4.99 us -> 5.64 us  [the longest x3 4.99 us: local(): lax.ppermute(column[d * 512:(d + 1) * 512], 'y', [(i, (i + d) % 4) for i...]
    ppermute x8 -> x6, waiting for transfers between devices: 9.09 us -> 8.84 us  [chain(): lax.ppermute(block, axes, [(i, i + by) for i in range(count) if 0 <= i +...]
    ppermute x3 -> x4, waiting for transfers between devices: 7.3 us -> 7.3 us  [the longest x3 7.3 us: local(): lax.ppermute(column[d * 512:(d + 1) * 512], 'y', [(i, (i + d) % 4) for i...]
  transfers between devices with their start and end apart: 17 -> 17, of which waited for: 8 -> 7; matrix products, arithmetic and copies ran while one was open for 3% -> 3% of each run, Pallas kernels for 13% -> 13%
where the time goes in v3:
time: 168 us; the launch traced here: 166 us
  starting transfers between devices  55.9 us (33%)
  waiting for transfers between devices  51.2 us (30%)
  Pallas kernels  43.5 us (26%)
  local copies, waits for them, and re-layouts  10.1 us (6%)
  other arithmetic  3.83 us (2%)
    pallas_call x6, Pallas kernels, call(): pl.pallas_call(kernel, out_shape=outs, in_specs=[VMEM] * len(args) if spe...  40.6 us
    all_to_all x3, waiting for transfers between devices, exchange(): return lax.all_to_all(block, axes, split_axis=0, concat_axis=0, tiled=True)  32.2 us
    all_to_all x3, starting transfers between devices, exchange(): return lax.all_to_all(block, axes, split_axis=0, concat_axis=0, tiled=True)  27.9 us
    ppermute x6, starting transfers between devices, chain(): lax.ppermute(block, axes, [(i, i + by) for i in range(count) if 0 <= i +...  21 us
    ppermute x6, waiting for transfers between devices, chain(): lax.ppermute(block, axes, [(i, i + by) for i in range(count) if 0 <= i +...  8.84 us
    ppermute x3, waiting for transfers between devices, local(): lax.ppermute(column[d * 512:(d + 1) * 512], 'y', [(i, (i + d) % 4) for i...  7.3 us
    unnamed x38, local copies, waits for them, and re-layouts  5.91 us
    ppermute x3, starting transfers between devices, local(): lax.ppermute(column[d * 512:(d + 1) * 512], 'y', [(i, (i + d) % 4) for i...  4.99 us
  transfers between devices with their start and end apart: 17, of which 7 were waited for; matrix products, arithmetic and copies ran while one was open for 3% of the time, Pallas kernels for 13%

profile of v3, /device:TPU:2, one launch (start us, length us, event | category | flops | bytes accessed | tf_op | source)
XLA Modules:
  0.0 165.7 jit_solution(7771419340564872620)
XLA Ops:
  1.4 5.9 %collective-permute-start.1 = (bf16[64,128]{1,0:T(8,128)(2,1)S(1)}, bf16[64,128]{1,0:T(8,128)(2,1)S(1)}, u32[]{:S(2)}, u32[]{:S(2)}) collective-permute-start(bf16[64,128]{1,0:T(8,128)(2,1)S(1)} %get-tuple-element.48), channel_id=1, source_target_pairs={{8,0},{16,8},{24,16},{32,24},{40,32},{48,40},{56,48},{64,56},{72,6... | collective-permute-start | bytes 49160 | tf_op jit(solution)/shard_map/ppermute | solution.py:295
  7.3 1.9 %collective-permute-start = (bf16[64,128]{1,0:T(8,128)(2,1)S(1)}, bf16[64,128]{1,0:T(8,128)(2,1)S(1)}, u32[]{:S(2)}, u32[]{:S(2)}) collective-permute-start(bf16[64,128]{1,0:T(8,128)(2,1)S(1)} %get-tuple-element.49), channel_id=1, source_target_pairs={{0,8},{8,16},{16,24},{24,32},{32,40},{40,48},{48,56},{56,64},{64,7... | collective-permute-start | bytes 49160 | tf_op jit(solution)/shard_map/ppermute | solution.py:295
  9.2 7.4 %shard_map.121 = bf16[128,40,128]{2,1,0:T(8,128)(2,1)} custom-call(s32[1,2048]{1,0:T(1,128)} %bitcast.33, s32[1,2048]{1,0:T(1,128)} %bitcast.34, bf16[2048,128]{1,0:T(8,128)(2,1)} %points_ref.1), custom_call_target="tpu_custom_call" | custom-call | flops 3221225472 | bytes 4194304 | tf_op jit(solution)/shard_map/pallas_call | solution.py:45
  17.2 10.6 %all-to-all-start = ((bf16[128,40,128]{2,1,0:T(8,128)(2,1)}), bf16[128,40,128]{2,1,0:T(8,128)(2,1)S(1)}, u32[]{:S(2)}, u32[]{:S(2)}) async-start(bf16[128,40,128]{2,1,0:T(8,128)(2,1)} %shard_map.121), calls=%async_computation | async-start | bytes 2621440 | tf_op jit(solution)/shard_map/all_to_all | solution.py:305
  29.0 20.5 %all-to-all-done.got_ref = bf16[128,40,128]{2,1,0:T(8,128)(2,1)S(1)} async-done(((bf16[128,40,128]{2,1,0:T(8,128)(2,1)}), bf16[128,40,128]{2,1,0:T(8,128)(2,1)S(1)}, u32[]{:S(2)}, u32[]{:S(2)}) %all-to-all-start) | async-done | bytes 1310752 | tf_op jit(solution)/shard_map/all_to_all | solution.py:305
  50.5 4.6 %shard_map.122 = (bf16[1024,128]{1,0:T(8,128)(2,1)}, bf16[256,128]{1,0:T(8,128)(2,1)}) custom-call(bf16[128,40,128]{2,1,0:T(8,128)(2,1)} %copy-done.7, s32[256,1]{1,0:T(8,128)} %reshape.96.rim_ref), custom_call_target="tpu_custom_call" | custom-call | flops 2147483648 | bytes 4194304 | tf_op jit(solution)/shard_map/pallas_call | solution.py:45
  57.4 3.9 %collective-permute-start.3 = (bf16[64,128]{1,0:T(8,128)(2,1)S(1)}, bf16[64,128]{1,0:T(8,128)(2,1)S(1)}, u32[]{:S(2)}, u32[]{:S(2)}) collective-permute-start(bf16[64,128]{1,0:T(8,128)(2,1)S(1)} %get-tuple-element.54), channel_id=1, source_target_pairs={{8,0},{16,8},{24,16},{32,24},{40,32},{48,40},{56,48},{64,56},{72,6... | collective-permute-start | bytes 49160 | tf_op jit(solution)/shard_map/ppermute | solution.py:295
  61.3 2.1 %collective-permute-start.2 = (bf16[64,128]{1,0:T(8,128)(2,1)S(1)}, bf16[64,128]{1,0:T(8,128)(2,1)S(1)}, u32[]{:S(2)}, u32[]{:S(2)}) collective-permute-start(bf16[64,128]{1,0:T(8,128)(2,1)S(1)} %get-tuple-element.55), channel_id=1, source_target_pairs={{0,8},{8,16},{16,24},{24,32},{32,40},{40,48},{48,56},{56,64},{64,7... | collective-permute-start | bytes 49160 | tf_op jit(solution)/shard_map/ppermute | solution.py:295
  63.4 7.3 %shard_map.123 = (bf16[1024,1152]{1,0:T(8,128)(2,1)}, bf16[1024,256]{1,0:T(8,128)(2,1)}) custom-call(s32[1024]{0:T(1024)} %bitcast.35, bf16[64,128]{1,0:T(8,128)(2,1)} %copy-done.17, bf16[4096,128]{1,0:T(8,128)(2,1)} %bitcast.32, bf16[64,128]{1,0:T(8,128)(2,1)} %copy-done.16, bf16[9,256,128]{2,1,0:T(8,128)(2,1)} %weight_ref.3), custom_call_target="tpu_custom_call" | custom-call | flops 1073741824 | bytes 4194304 | tf_op jit(solution)/shard_map/pallas_call | solution.py:45
  73.5 14.3 %shard_map.124 = (bf16[1024,256]{1,0:T(8,128)(2,1)S(1)}, bf16[4608,128]{1,0:T(8,128)(2,1)S(1)}, bf16[4608,128]{1,0:T(8,128)(2,1)S(1)}) custom-call(s32[2]{0:T(128)S(1)} %pad_add_fusion.1.core_ref, bf16[1024,128]{1,0:T(8,128)(2,1)S(1)} %copy-done.5, bf16[64,128]{1,0:T(8,128)(2,1)S(1)} %collective-permute-done.2.left_ref, ...), custom_call_target="tpu_custom_call" | custom-call | flops 8589934592 | bytes 4194304 | tf_op jit(solution)/shard_map/pallas_call | solution.py:45
  88.6 4.4 %shard_map.125 = (bf16[2048,256]{1,0:T(8,128)(2,1)}, bf16[2048,256]{1,0:T(8,128)(2,1)}) custom-call(s32[2]{0:T(128)} %copy-done, s32[1,1024]{1,0:T(1,128)} %bitcast.36, bf16[1024,256]{1,0:T(8,128)(2,1)} %copy-done.6), custom_call_target="tpu_custom_call" | custom-call | flops 3221225472 | bytes 4194304 | tf_op jit(solution)/shard_map/pallas_call | solution.py:45
  94.9 8.8 %all-to-all-start.1 = ((bf16[64,72,128]{2,1,0:T(8,128)(2,1)}), bf16[64,72,128]{2,1,0:T(8,128)(2,1)S(1)}, u32[]{:S(2)}, u32[]{:S(2)}) async-start(bf16[64,72,128]{2,1,0:T(8,128)(2,1)} %bitcast.15), calls=%async_computation.1 | async-start | bytes 2359296 | tf_op jit(solution)/shard_map/all_to_all | solution.py:305
  107.4 1.8 %collective-permute-start.10 = (bf16[512,256]{1,0:T(8,128)(2,1)S(1)}, bf16[512,256]{1,0:T(8,128)(2,1)S(1)}, u32[]{:S(2)}, u32[]{:S(2)}) collective-permute-start(bf16[512,256]{1,0:T(8,128)(2,1)S(1)} %get-tuple-element.46), channel_id=1, source_target_pairs={{0,6},{2,0},{4,2},{6,4},{1,7},{3,1},{5,3},{7,5},{8,14},{10,8},{12,... | collective-permute-start | bytes 786440 | tf_op jit(solution)/shard_map/ppermute | solution.py:416
  111.0 11.6 %all-to-all-done.1 = bf16[64,72,128]{2,1,0:T(8,128)(2,1)S(1)} async-done(((bf16[64,72,128]{2,1,0:T(8,128)(2,1)}), bf16[64,72,128]{2,1,0:T(8,128)(2,1)S(1)}, u32[]{:S(2)}, u32[]{:S(2)}) %all-to-all-start.1) | async-done | bytes 1179680 | tf_op jit(solution)/shard_map/all_to_all | solution.py:305
  123.4 1.9 %collective-permute-done.8 = bf16[512,256]{1,0:T(8,128)(2,1)S(1)} collective-permute-done((bf16[512,256]{1,0:T(8,128)(2,1)}, bf16[512,256]{1,0:T(8,128)(2,1)S(1)}, u32[]{:S(2)}, u32[]{:S(2)}) %collective-permute-start.8) | collective-permute-done | bytes 262176 | tf_op jit(solution)/shard_map/ppermute | solution.py:416
  125.3 5.4 %collective-permute-done.9 = bf16[512,256]{1,0:T(8,128)(2,1)S(1)} collective-permute-done((bf16[512,256]{1,0:T(8,128)(2,1)S(1)}, bf16[512,256]{1,0:T(8,128)(2,1)S(1)}, u32[]{:S(2)}, u32[]{:S(2)}) %collective-permute-start.9) | collective-permute-done | bytes 262176 | tf_op jit(solution)/shard_map/ppermute | solution.py:416
  132.0 8.4 %all-to-all-start.2 = ((bf16[64,72,128]{2,1,0:T(8,128)(2,1)}), bf16[64,72,128]{2,1,0:T(8,128)(2,1)S(1)}, u32[]{:S(2)}, u32[]{:S(2)}) async-start(bf16[64,72,128]{2,1,0:T(8,128)(2,1)} %broadcast_in_dim.2), calls=%async_computation.2 | async-start | bytes 2359296 | tf_op jit(solution)/shard_map/all_to_all | solution.py:305
  140.5 5.3 %collective-permute-start.12 = (bf16[64,256]{1,0:T(8,128)(2,1)S(1)}, bf16[64,256]{1,0:T(8,128)(2,1)S(1)}, u32[]{:S(2)}, u32[]{:S(2)}) collective-permute-start(bf16[64,256]{1,0:T(8,128)(2,1)S(1)} %get-tuple-element.50), channel_id=1, source_target_pairs={{1,0},{2,1},{3,2},{4,3},{5,4},{6,5},{7,6},{8,7},{9,8},{10,9},{11,1... | collective-permute-start | bytes 98312 | tf_op jit(solution)/shard_map/ppermute | solution.py:295
  145.7 1.9 %collective-permute-start.11 = (bf16[64,256]{1,0:T(8,128)(2,1)S(1)}, bf16[64,256]{1,0:T(8,128)(2,1)S(1)}, u32[]{:S(2)}, u32[]{:S(2)}) collective-permute-start(bf16[64,256]{1,0:T(8,128)(2,1)S(1)} %get-tuple-element.51), channel_id=1, source_target_pairs={{0,1},{1,2},{2,3},{3,4},{4,5},{5,6},{6,7},{7,8},{8,9},{9,10},{10,1... | collective-permute-start | bytes 98312 | tf_op jit(solution)/shard_map/ppermute | solution.py:295
  147.7 5.0 %collective-permute-done.12.high_ref = bf16[64,256]{1,0:T(8,128)(2,1)S(1)} collective-permute-done((bf16[64,256]{1,0:T(8,128)(2,1)S(1)}, bf16[64,256]{1,0:T(8,128)(2,1)S(1)}, u32[]{:S(2)}, u32[]{:S(2)}) %collective-permute-start.12) | collective-permute-done | bytes 32800 | tf_op jit(solution)/shard_map/ppermute | solution.py:295
  152.6 3.9 %collective-permute-done.11.low_ref = bf16[64,256]{1,0:T(8,128)(2,1)S(1)} collective-permute-done((bf16[64,256]{1,0:T(8,128)(2,1)S(1)}, bf16[64,256]{1,0:T(8,128)(2,1)S(1)}, u32[]{:S(2)}, u32[]{:S(2)}) %collective-permute-start.11) | collective-permute-done | bytes 32800 | tf_op jit(solution)/shard_map/ppermute | solution.py:295
  157.1 2.6 %shard_map.126 = bf16[512,128]{1,0:T(8,128)(2,1)} custom-call(bf16[64,256]{1,0:T(8,128)(2,1)} %copy-done.15, bf16[512,256]{1,0:T(8,128)(2,1)} %copy-done.9, bf16[64,256]{1,0:T(8,128)(2,1)} %copy-done.14, bf16[9,256,128]{2,1,0:T(8,128)(2,1)} %weight_ref.3), custom_call_target="tpu_custom_call" | custom-call | flops 1073741824 | bytes 4194304 | tf_op jit(solution)/shard_map/pallas_call | solution.py:45
  159.7 2.8 %collective-permute-done.13.theirs_ref = bf16[36,128,128]{2,1,0:T(8,128)(2,1)S(1)} collective-permute-done((bf16[36,128,128]{2,1,0:T(8,128)(2,1)S(1)}, bf16[36,128,128]{2,1,0:T(8,128)(2,1)S(1)}, u32[]{:S(2)}, u32[]{:S(2)}) %collective-permute-start.13) | collective-permute-done | bytes 1179680 | tf_op jit(solution)/shard_map/ppermute | solution.py:301
  162.6 2.9 %shard_map.127 = (f32[27,128,256]{2,1,0:T(8,128)}, f32[9,256,128]{2,1,0:T(8,128)}) custom-call(bf16[36,128,128]{2,1,0:T(8,128)(2,1)S(1)} %bitcast.28, bf16[36,128,128]{2,1,0:T(8,128)(2,1)S(1)} %collective-permute-done.13.theirs_ref, s32[2]{0:T(128)S(1)} %copy-done.1), custom_call_target="tpu_custom_call" | custom-call | tf_op jit(solution)/shard_map/pallas_call | solution.py:271
  (69 shorter events, 19.2 us)
Async XLA Ops:
  1.4 15.2 %collective-permute-start.1 = (bf16[64,128]{1,0:T(8,128)(2,1)S(1)}, bf16[64,128]{1,0:T(8,128)(2,1)S(1)}, u32[]{:S(2)}, u32[]{:S(2)}) collective-permute-start(bf16[64,128]{1,0:T(8,128)(2,1)S(1)} %get-tuple-element.48), channel_id=1, source_target_pairs={{8,0},{16,8},{24,16},{32,24},{40,32},{48,40},{56,48},{64,56},{72,6... | collective-permute-start | bytes 49160 | tf_op jit(solution)/shard_map/ppermute | solution.py:295
  7.3 9.3 %collective-permute-start = (bf16[64,128]{1,0:T(8,128)(2,1)S(1)}, bf16[64,128]{1,0:T(8,128)(2,1)S(1)}, u32[]{:S(2)}, u32[]{:S(2)}) collective-permute-start(bf16[64,128]{1,0:T(8,128)(2,1)S(1)} %get-tuple-element.49), channel_id=1, source_target_pairs={{0,8},{8,16},{16,24},{24,32},{32,40},{40,48},{48,56},{56,64},{64,7... | collective-permute-start | bytes 49160 | tf_op jit(solution)/shard_map/ppermute | solution.py:295
  16.6 11.3 %copy-start.12 = (s32[1,1,26,256]{3,1,2,0:T(1,128)S(1)}, s32[1,1,26,256]{3,1,2,0:T(1,128)}, u32[]{:S(2)}) copy-start(s32[1,1,26,256]{3,1,2,0:T(1,128)} %param.15) | copy-start | bytes 79876
  16.6 11.3 %copy-start.13 = (s32[1,1,4,64]{3,2,1,0:T(4,128)S(1)}, s32[1,1,4,64]{3,2,1,0:T(4,128)}, u32[]{:S(2)}) copy-start(s32[1,1,4,64]{3,2,1,0:T(4,128)} %param.13) | copy-start | bytes 3076
  16.6 12.2 %copy-start.11 = (s32[1,1,26,256]{3,1,2,0:T(1,128)S(1)}, s32[1,1,26,256]{3,1,2,0:T(1,128)}, u32[]{:S(2)}) copy-start(s32[1,1,26,256]{3,1,2,0:T(1,128)} %param.14) | copy-start | bytes 79876
  17.2 32.3 %all-to-all-start = ((bf16[128,40,128]{2,1,0:T(8,128)(2,1)}), bf16[128,40,128]{2,1,0:T(8,128)(2,1)S(1)}, u32[]{:S(2)}, u32[]{:S(2)}) async-start(bf16[128,40,128]{2,1,0:T(8,128)(2,1)} %shard_map.121), calls=%async_computation | async-start | bytes 2621440 | tf_op jit(solution)/shard_map/all_to_all | solution.py:305
  28.9 41.8 %copy-start = (s32[2]{0:T(128)}, s32[2]{0:T(128)S(1)}, u32[]{:S(2)}) copy-start(s32[2]{0:T(128)S(1)} %pad_add_fusion.1.core_ref) | copy-start | bytes 28
  55.9 14.8 %collective-permute-start.5 = (bf16[64,128]{1,0:T(8,128)(2,1)S(1)}, bf16[64,128]{1,0:T(8,128)(2,1)S(1)}, u32[]{:S(2)}, u32[]{:S(2)}) collective-permute-start(bf16[64,128]{1,0:T(8,128)(2,1)S(1)} %get-tuple-element.52), channel_id=1, source_target_pairs={{1,2},{3,4},{5,6},{2,1},{4,3},{6,5},{9,10},{11,12},{13,14},{10,9},... | collective-permute-start | bytes 49160 | tf_op jit(solution)/shard_map/ppermute | solution.py:364
  56.6 14.2 %collective-permute-start.4 = (bf16[64,128]{1,0:T(8,128)(2,1)S(1)}, bf16[64,128]{1,0:T(8,128)(2,1)S(1)}, u32[]{:S(2)}, u32[]{:S(2)}) collective-permute-start(bf16[64,128]{1,0:T(8,128)(2,1)S(1)} %get-tuple-element.53), channel_id=1, source_target_pairs={{0,1},{1,0},{2,3},{3,2},{4,5},{5,4},{6,7},{7,6},{8,9},{9,8},{10,11... | collective-permute-start | bytes 49160 | tf_op jit(solution)/shard_map/ppermute | solution.py:301
  57.4 13.4 %collective-permute-start.3 = (bf16[64,128]{1,0:T(8,128)(2,1)S(1)}, bf16[64,128]{1,0:T(8,128)(2,1)S(1)}, u32[]{:S(2)}, u32[]{:S(2)}) collective-permute-start(bf16[64,128]{1,0:T(8,128)(2,1)S(1)} %get-tuple-element.54), channel_id=1, source_target_pairs={{8,0},{16,8},{24,16},{32,24},{40,32},{48,40},{56,48},{64,56},{72,6... | collective-permute-start | bytes 49160 | tf_op jit(solution)/shard_map/ppermute | solution.py:295
  61.3 9.5 %collective-permute-start.2 = (bf16[64,128]{1,0:T(8,128)(2,1)S(1)}, bf16[64,128]{1,0:T(8,128)(2,1)S(1)}, u32[]{:S(2)}, u32[]{:S(2)}) collective-permute-start(bf16[64,128]{1,0:T(8,128)(2,1)S(1)} %get-tuple-element.55), channel_id=1, source_target_pairs={{0,8},{8,16},{16,24},{24,32},{32,40},{40,48},{48,56},{56,64},{64,7... | collective-permute-start | bytes 49160 | tf_op jit(solution)/shard_map/ppermute | solution.py:295
  88.6 4.5 %collective-permute-start.6 = (bf16[4608,128]{1,0:T(8,128)(2,1)S(1)}, bf16[4608,128]{1,0:T(8,128)(2,1)S(1)}, u32[]{:S(2)}, u32[]{:S(2)}) collective-permute-start(bf16[4608,128]{1,0:T(8,128)(2,1)S(1)} %get-tuple-element.32), channel_id=1, source_target_pairs={{0,1},{1,0},{2,3},{3,2},{4,5},{5,4},{6,7},{7,6},{8,9},{9,8},{10,11... | collective-permute-start | bytes 3538952 | tf_op jit(solution)/shard_map/ppermute | solution.py:301
  93.0 10.7 %collective-permute-start.7 = (bf16[2048,256]{1,0:T(8,128)(2,1)}, bf16[2048,256]{1,0:T(8,128)(2,1)}, u32[]{:S(2)}, u32[]{:S(2)}) collective-permute-start(bf16[2048,256]{1,0:T(8,128)(2,1)} %get-tuple-element.38), channel_id=1, source_target_pairs={{0,1},{1,0},{2,3},{3,2},{4,5},{5,4},{6,7},{7,6},{8,9},{9,8},{10,11... | collective-permute-start | bytes 3145736 | tf_op jit(solution)/shard_map/ppermute | solution.py:301
  94.9 8.9 %copy-start.8 = (bf16[2048,256]{1,0:T(8,128)(2,1)S(1)}, bf16[2048,256]{1,0:T(8,128)(2,1)}, u32[]{:S(2)}) copy-start(bf16[2048,256]{1,0:T(8,128)(2,1)} %get-tuple-element.37) | copy-start | bytes 3145732
  94.9 27.7 %all-to-all-start.1 = ((bf16[64,72,128]{2,1,0:T(8,128)(2,1)}), bf16[64,72,128]{2,1,0:T(8,128)(2,1)S(1)}, u32[]{:S(2)}, u32[]{:S(2)}) async-start(bf16[64,72,128]{2,1,0:T(8,128)(2,1)} %bitcast.15), calls=%async_computation.1 | async-start | bytes 2359296 | tf_op jit(solution)/shard_map/all_to_all | solution.py:305
  106.0 19.3 %collective-permute-start.8 = (bf16[512,256]{1,0:T(8,128)(2,1)}, bf16[512,256]{1,0:T(8,128)(2,1)S(1)}, u32[]{:S(2)}, u32[]{:S(2)}) collective-permute-start(bf16[512,256]{1,0:T(8,128)(2,1)} %get-tuple-element.45), channel_id=1, source_target_pairs={{0,2},{2,4},{4,6},{6,0},{1,3},{3,5},{5,7},{7,1},{8,10},{10,12},{12... | collective-permute-start | bytes 786440 | tf_op jit(solution)/shard_map/ppermute | solution.py:416
  107.4 17.9 %collective-permute-start.10 = (bf16[512,256]{1,0:T(8,128)(2,1)S(1)}, bf16[512,256]{1,0:T(8,128)(2,1)S(1)}, u32[]{:S(2)}, u32[]{:S(2)}) collective-permute-start(bf16[512,256]{1,0:T(8,128)(2,1)S(1)} %get-tuple-element.46), channel_id=1, source_target_pairs={{0,6},{2,0},{4,2},{6,4},{1,7},{3,1},{5,3},{7,5},{8,14},{10,8},{12,... | collective-permute-start | bytes 786440 | tf_op jit(solution)/shard_map/ppermute | solution.py:416
  109.2 21.5 %collective-permute-start.9 = (bf16[512,256]{1,0:T(8,128)(2,1)S(1)}, bf16[512,256]{1,0:T(8,128)(2,1)S(1)}, u32[]{:S(2)}, u32[]{:S(2)}) collective-permute-start(bf16[512,256]{1,0:T(8,128)(2,1)S(1)} %get-tuple-element.47), channel_id=1, source_target_pairs={{0,4},{2,6},{4,0},{6,2},{1,5},{3,7},{5,1},{7,3},{8,12},{10,14},{12... | collective-permute-start | bytes 786440 | tf_op jit(solution)/shard_map/ppermute | solution.py:416
  130.8 9.6 %copy-start.9 = (bf16[512,256]{1,0:T(8,128)(2,1)}, bf16[512,256]{1,0:T(8,128)(2,1)S(1)}, u32[]{:S(2)}) copy-start(bf16[512,256]{1,0:T(8,128)(2,1)S(1)} %add_convert_fusion.2.own_ref) | copy-start | bytes 786436
  132.0 27.7 %all-to-all-start.2 = ((bf16[64,72,128]{2,1,0:T(8,128)(2,1)}), bf16[64,72,128]{2,1,0:T(8,128)(2,1)S(1)}, u32[]{:S(2)}, u32[]{:S(2)}) async-start(bf16[64,72,128]{2,1,0:T(8,128)(2,1)} %broadcast_in_dim.2), calls=%async_computation.2 | async-start | bytes 2359296 | tf_op jit(solution)/shard_map/all_to_all | solution.py:305
  140.5 12.2 %collective-permute-start.12 = (bf16[64,256]{1,0:T(8,128)(2,1)S(1)}, bf16[64,256]{1,0:T(8,128)(2,1)S(1)}, u32[]{:S(2)}, u32[]{:S(2)}) collective-permute-start(bf16[64,256]{1,0:T(8,128)(2,1)S(1)} %get-tuple-element.50), channel_id=1, source_target_pairs={{1,0},{2,1},{3,2},{4,3},{5,4},{6,5},{7,6},{8,7},{9,8},{10,9},{11,1... | collective-permute-start | bytes 98312 | tf_op jit(solution)/shard_map/ppermute | solution.py:295
  145.7 16.9 %copy-start.1 = (s32[2]{0:T(128)S(1)}, s32[2]{0:T(128)}, u32[]{:S(2)}) copy-start(s32[2]{0:T(128)} %copy-done) | copy-start | bytes 28
  145.7 10.8 %collective-permute-start.11 = (bf16[64,256]{1,0:T(8,128)(2,1)S(1)}, bf16[64,256]{1,0:T(8,128)(2,1)S(1)}, u32[]{:S(2)}, u32[]{:S(2)}) collective-permute-start(bf16[64,256]{1,0:T(8,128)(2,1)S(1)} %get-tuple-element.51), channel_id=1, source_target_pairs={{0,1},{1,2},{2,3},{3,4},{4,5},{5,6},{6,7},{7,8},{8,9},{9,10},{10,1... | collective-permute-start | bytes 98312 | tf_op jit(solution)/shard_map/ppermute | solution.py:295
  159.7 2.8 %collective-permute-start.13 = (bf16[36,128,128]{2,1,0:T(8,128)(2,1)S(1)}, bf16[36,128,128]{2,1,0:T(8,128)(2,1)S(1)}, u32[]{:S(2)}, u32[]{:S(2)}) collective-permute-start(bf16[36,128,128]{2,1,0:T(8,128)(2,1)S(1)} %bitcast.27), channel_id=1, source_target_pairs={{0,1},{1,0},{2,3},{3,2},{4,5},{5,4},{6,7},{7,6},{8,9},{9,8},{10,11... | collective-permute-start | bytes 3538952 | tf_op jit(solution)/shard_map/ppermute | solution.py:301
  (11 other events, 32.4 us)

commit v4 on v3

--- a/solution.py
+++ b/solution.py
@@ -16,6 +16,7 @@
 CAP = 32
 ROWS = 40
 OFFS = 26
+EDGED = 576
 VMEM = pl.BlockSpec(memory_space=pltpu.VMEM)
 SMEM = pl.BlockSpec(memory_space=pltpu.SMEM)
 ANY = pl.BlockSpec(memory_space=pl.ANY)
@@ -199,24 +200,30 @@
         store.wait()
 
 
-def column_kernel(core_ref, cell_ref, act_ref, keep_ref, send_ref):
+def head_kernel(core_ref, cell_ref, act_ref, weight_ref, keep_ref, send_ref, wide_ref, total_ref):
     core, here = core_ref[0], core_ref[1]
+    for a in range(3):
+        for b in range(3):
+            wide_ref[b, :, a * 128 : (a + 1) * 128] = weight_ref[3 * a + b]
+    total_ref[...] = jnp.zeros_like(total_ref)
+    y = iota((512, 256), 0) & 63
+    for part in range(8):
+        match = hot(cell_ref[...] - part * 512 == iota((512, cell_ref.shape[1]), 0))
+        column = dot(match, act_ref[...])
+        lower = jnp.where(y == 0, 0.0, pltpu.roll(column, 1, 0)).astype(BF)
+        upper = jnp.where(y == 63, 0.0, pltpu.roll(column, 511, 0)).astype(BF)
+        rows = dot(lower, wide_ref[0]) + dot(column.astype(BF), wide_ref[1]) + dot(upper, wide_ref[2])
+        for a in range(3):
+            at = (part * 8 + 2 - a) * 64
+            total_ref[at : at + 512, :] += rows[:, a * 128 : (a + 1) * 128]
     for d in range(4):
-        y = (here + d) & 3
         for out_ref, which in ((send_ref, 1 - core), (keep_ref, core)):
-            for m in range(0, 512, 256):
-                start = (y * 2 + which) * 512 + m
-                match = hot(cell_ref[...] - start == iota((256, cell_ref.shape[1]), 0))
-                out_ref[d * 512 + m : d * 512 + m + 256, :] = dot(match, act_ref[...]).astype(BF)
-
-
-def shifts(rows):
-    total = rows.shape[0]
-    y = iota(rows.shape, 0) & 63
-    wide = rows.astype(F32)
-    lower = jnp.where(y == 0, 0.0, pltpu.roll(wide, 1, 0))
-    upper = jnp.where(y == 63, 0.0, pltpu.roll(wide, total - 1, 0))
-    return [lower.astype(BF), rows, upper.astype(BF)]
+            layer = ((here + d) & 3) * 2 + which
+            first = pl.multiple_of(layer * 512 + 64, 64)
+            out_ref[d * EDGED : d * EDGED + 512, :] = total_ref[pl.ds(first, 512), :].astype(BF)
+            beyond = jnp.where(layer == 7, total_ref[65 * 64 : 66 * 64, :], 0.0)
+            beyond = jnp.where(layer == 0, total_ref[0:64, :], beyond)
+            out_ref[d * EDGED + 512 : (d + 1) * EDGED, :] = beyond.astype(BF)
 
 
 def window_kernel(cell_ref, low_ref, cot_ref, high_ref, weight_ref, window_ref, up_ref, pad_ref, rows_ref):
@@ -278,18 +285,6 @@
     )(mine, theirs, core)
 
 
-def head_kernel(low_ref, own_ref, high_ref, weight_ref, out_ref, moved_ref):
-    size = own_ref.shape[0]
-    for at, ref in ((0, low_ref), (64, own_ref), (64 + size, high_ref)):
-        for b, moved in enumerate(shifts(ref[...])):
-            moved_ref[b, at : at + ref.shape[0], :] = moved
-    total = jnp.zeros(out_ref.shape, F32)
-    for a in range(3):
-        for b in range(3):
-            total = total + dot(moved_ref[b, a * 64 : a * 64 + size, :], weight_ref[3 * a + b])
-    out_ref[...] = total.astype(BF)
-
-
 def chain(block, axes, by):
     count = lax.axis_size(axes)
     return lax.ppermute(
@@ -333,7 +328,6 @@
     cells = cot.shape[0]
     cot_low = chain(cot[cells - 64 :], PLANE, 1)
     cot_high = chain(cot[:64], PLANE, -1)
-    ready, cot_low, cot_high = lax.optimization_barrier((ready, cot_low, cot_high))
     got = exchange(ready, ALL)
 
     window, upstream = call(
@@ -344,6 +338,8 @@
         scratch=[pltpu.VMEM((66, 80, 128), F32), pltpu.VMEM((3, 4 * voxels, 128), F32)],
         flops=1 << 30,
     )
+
+    got, window, upstream = lax.optimization_barrier((got, window, upstream))
 
     sides = send_rows[0, 0]
     even = core[0] == 0
@@ -397,44 +393,40 @@
             pltpu.SemaphoreType.DMA((8,)),
         ],
         flops=8 << 30,
-        limit=40,
-    )
-
-    arrived = swap(send)
-    column_keep, column_send = call(
-        column_kernel,
-        [shape((2048, 256), BF), shape((2048, 256), BF)],
-        (core, bev_cell.reshape(1, voxels), act),
-        specs=[SMEM, VMEM, VMEM],
-        flops=3 << 30,
-    )
-    arrived, column_keep, column_send = lax.optimization_barrier((arrived, column_keep, column_send))
-    both = (keep.astype(F32) + arrived.astype(F32)).astype(BF)
-    shares = exchange(both.reshape(64, grad_rows // 64, 128), ("x", "z", "y"))
-    column = (column_keep.astype(F32) + swap(column_send).astype(F32)).astype(BF)
-    ahead = [
-        lax.ppermute(column[d * 512 : (d + 1) * 512], "y", [(i, (i + d) % 4) for i in range(4)])
-        for d in (1, 2, 3)
-    ]
+        limit=60,
+    )
+
+    both = (keep.astype(F32) + swap(send).astype(F32)).astype(BF)
+    both, act = lax.optimization_barrier((both, act))
+    shares = exchange(both.reshape(16, grad_rows // 16, 128), PLANE)
     share = jnp.sum(shares.astype(F32), axis=0).astype(BF)
-    bev = column[:512].astype(F32)
-    for part in ahead:
-        bev = bev + part.astype(F32)
-    bev = bev.astype(BF)
-    share, bev = lax.optimization_barrier((share, bev))
-    mine = exchange(
-        jnp.broadcast_to(share[None], (64,) + share.shape), ("x", "z", "y")
-    ).reshape(36, 128, 128)
-    bev_low = chain(bev[448:], ALL, 1)
-    bev_high = chain(bev[:64], ALL, -1)
-    head_out = call(
+    shares = exchange(jnp.broadcast_to(share[None], (4,) + share.shape), "y")
+    share = jnp.sum(shares.astype(F32), axis=0).astype(BF)
+    head_keep, head_send = call(
         head_kernel,
-        shape((512, 128), BF),
-        (bev_low, bev, bev_high, head_weight),
-        scratch=[pltpu.VMEM((3, 640, 256), BF)],
-        flops=1 << 30,
-    )
-
+        [shape((4 * EDGED, 128), BF), shape((4 * EDGED, 128), BF)],
+        (core, bev_cell.reshape(1, voxels), act, head_weight),
+        specs=[SMEM, VMEM, VMEM, VMEM],
+        scratch=[pltpu.VMEM((3, 256, 384), BF), pltpu.VMEM((66 * 64, 128), F32)],
+        flops=4 << 30,
+    )
+    head = (head_keep.astype(F32) + swap(head_send).astype(F32)).astype(BF)
+    mine = exchange(jnp.broadcast_to(share[None], (16,) + share.shape), PLANE).reshape(36, 128, 128)
+    total = head[:EDGED].astype(F32)
+    for d in (1, 2, 3):
+        sent = head[d * EDGED : (d + 1) * EDGED]
+        total = total + lax.ppermute(sent, "y", [(i, (i + d) % 4) for i in range(4)]).astype(F32)
+    tiles = lax.axis_size(PLANE)
+    ends = [(t * layers - 1, t * layers) for t in range(1, tiles)]
+    beyond = lax.ppermute(total[512:].astype(BF), ALL, ends + [(j, i) for i, j in ends]).astype(F32)
+    layer = lax.axis_index(HEIGHT)
+    head_out = jnp.concatenate(
+        [
+            total[:64] + jnp.where(layer == 0, beyond, 0.0),
+            total[64:448],
+            total[448:512] + jnp.where(layer == layers - 1, beyond, 0.0),
+        ]
+    ).astype(BF)
     mine, head_out = lax.optimization_barrier((mine, head_out))
     conv_grad, head_grad = join(mine, swap(mine), core)
     return (head_out.reshape(8, 64, 128), conv_grad, head_grad)

time: 168 us -> 153 us (0.911)
  starting transfers between devices: 55.9 us -> 43.8 us
  waiting for transfers between devices: 51.2 us -> 39.9 us
  blocking collectives: 0 us -> 10.6 us
  local copies, waits for them, and re-layouts: 10.1 us -> 7.23 us
    all_to_all x3, waiting for transfers between devices: 32.2 us -> 8.17 us  [exchange(): return lax.all_to_all(block, axes, split_axis=0, concat_axis=0, tiled=True)]
    all_to_all x0 -> x1, blocking collectives: none -> 10.6 us  [exchange(): return lax.all_to_all(block, axes, split_axis=0, concat_axis=0, tiled=True)]
    ppermute x6 -> x4, starting transfers between devices: 21 us -> 13.2 us  [chain(): lax.ppermute(block, axes, [(i, i + by) for i in range(count) if 0 <= i +...]
    ppermute x3 -> x4, waiting for transfers between devices: 7.3 us -> 14 us  [the longest x1 7.32 us: local(): lax.ppermute(total[512:].astype(BF), ALL, ends + [(j, i) for i, j in ends])]
    all_to_all x3, starting transfers between devices: 27.9 us -> 21.8 us  [exchange(): return lax.all_to_all(block, axes, split_axis=0, concat_axis=0, tiled=True)]
    ppermute x4, waiting for transfers between devices: 2.85 us -> 5.9 us  [swap(): return lax.ppermute(block, 'c', [(0, 1), (1, 0)])]
    ppermute x6 -> x4, waiting for transfers between devices: 8.84 us -> 11.8 us  [chain(): lax.ppermute(block, axes, [(i, i + by) for i in range(count) if 0 <= i +...]
    unnamed x38 -> x26, local copies, waits for them, and re-layouts: 5.91 us -> 3.67 us
  transfers between devices with their start and end apart: 17 -> 16, of which waited for: 7 -> 10; matrix products, arithmetic and copies ran while one was open for 3% -> 4% of each run, Pallas kernels for 13% -> 10%
where the time goes in v4:
time: 153 us; the launch traced here: 152 us
  Pallas kernels  44.8 us (29%)
  starting transfers between devices  43.8 us (29%)
  waiting for transfers between devices  39.9 us (26%)
  blocking collectives  10.6 us (7%)
  local copies, waits for them, and re-layouts  7.23 us (5%)
  other arithmetic  4.31 us (3%)
    pallas_call x5, Pallas kernels, call(): pl.pallas_call(kernel, out_shape=outs, in_specs=[VMEM] * len(args) if spe...  42 us
    all_to_all x3, starting transfers between devices, exchange(): return lax.all_to_all(block, axes, split_axis=0, concat_axis=0, tiled=True)  21.8 us
    ppermute x4, starting transfers between devices, chain(): lax.ppermute(block, axes, [(i, i + by) for i in range(count) if 0 <= i +...  13.2 us
    ppermute x4, waiting for transfers between devices, chain(): lax.ppermute(block, axes, [(i, i + by) for i in range(count) if 0 <= i +...  11.8 us
    all_to_all x1, blocking collectives, exchange(): return lax.all_to_all(block, axes, split_axis=0, concat_axis=0, tiled=True)  10.6 us
    all_to_all x3, waiting for transfers between devices, exchange(): return lax.all_to_all(block, axes, split_axis=0, concat_axis=0, tiled=True)  8.17 us
    ppermute x1, waiting for transfers between devices, local(): lax.ppermute(total[512:].astype(BF), ALL, ends + [(j, i) for i, j in ends])  7.32 us
    ppermute x3, waiting for transfers between devices, local(): lax.ppermute(sent, 'y', [(i, (i + d) % 4) for i in range(4)]).astype(F32)  6.64 us
  transfers between devices with their start and end apart: 16, of which 10 were waited for; matrix products, arithmetic and copies ran while one was open for 4% of the time, Pallas kernels for 10%

profile of v4, /device:TPU:2, one launch (start us, length us, event | category | flops | bytes accessed | tf_op | source)
XLA Modules:
  0.0 151.7 jit_solution(4639632382377947959)
XLA Ops:
  0.6 7.4 %shard_map.121 = bf16[128,40,128]{2,1,0:T(8,128)(2,1)} custom-call(s32[1,2048]{1,0:T(1,128)} %bitcast.34, s32[1,2048]{1,0:T(1,128)} %bitcast.35, bf16[2048,128]{1,0:T(8,128)(2,1)} %points_ref.1), custom_call_target="tpu_custom_call" | custom-call | flops 3221225472 | bytes 4194304 | tf_op jit(solution)/shard_map/pallas_call | solution.py:46
  8.0 10.5 %all-to-all-start = ((bf16[128,40,128]{2,1,0:T(8,128)(2,1)}), bf16[128,40,128]{2,1,0:T(8,128)(2,1)S(1)}, u32[]{:S(2)}, u32[]{:S(2)}) async-start(bf16[128,40,128]{2,1,0:T(8,128)(2,1)} %shard_map.121), calls=%async_computation | async-start | bytes 2621440 | tf_op jit(solution)/shard_map/all_to_all | solution.py:300
  19.3 5.2 %collective-permute-start.1 = (bf16[64,128]{1,0:T(8,128)(2,1)S(1)}, bf16[64,128]{1,0:T(8,128)(2,1)S(1)}, u32[]{:S(2)}, u32[]{:S(2)}) collective-permute-start(bf16[64,128]{1,0:T(8,128)(2,1)S(1)} %get-tuple-element.41), channel_id=1, source_target_pairs={{8,0},{16,8},{24,16},{32,24},{40,32},{48,40},{56,48},{64,56},{72,6... | collective-permute-start | bytes 49160 | tf_op jit(solution)/shard_map/ppermute | solution.py:290
  27.3 6.7 %collective-permute-done.1.high_ref = bf16[64,128]{1,0:T(8,128)(2,1)S(1)} collective-permute-done((bf16[64,128]{1,0:T(8,128)(2,1)S(1)}, bf16[64,128]{1,0:T(8,128)(2,1)S(1)}, u32[]{:S(2)}, u32[]{:S(2)}) %collective-permute-start.1) | collective-permute-done | bytes 16416 | tf_op jit(solution)/shard_map/ppermute | solution.py:290
  34.0 3.3 %collective-permute-done.low_ref = bf16[64,128]{1,0:T(8,128)(2,1)S(1)} collective-permute-done((bf16[64,128]{1,0:T(8,128)(2,1)S(1)}, bf16[64,128]{1,0:T(8,128)(2,1)S(1)}, u32[]{:S(2)}, u32[]{:S(2)}) %collective-permute-start) | collective-permute-done | bytes 16416 | tf_op jit(solution)/shard_map/ppermute | solution.py:290
  37.9 7.2 %shard_map.122 = (bf16[1024,1152]{1,0:T(8,128)(2,1)}, bf16[1024,256]{1,0:T(8,128)(2,1)}) custom-call(s32[1024]{0:T(1024)} %bitcast.36, bf16[64,128]{1,0:T(8,128)(2,1)} %copy-done.8, bf16[4096,128]{1,0:T(8,128)(2,1)} %bitcast.32, bf16[64,128]{1,0:T(8,128)(2,1)} %copy-done.6, bf16[9,256,128]{2,1,0:T(8,128)(2,1)} %weight_ref.3), custom_call_target="tpu_custom_call" | custom-call | flops 1073741824 | bytes 4194304 | tf_op jit(solution)/shard_map/pallas_call | solution.py:46
  46.1 4.6 %shard_map.123 = (bf16[1024,128]{1,0:T(8,128)(2,1)}, bf16[256,128]{1,0:T(8,128)(2,1)}) custom-call(bf16[128,40,128]{2,1,0:T(8,128)(2,1)} %copy-done.1, s32[256,1]{1,0:T(8,128)} %reshape.97.rim_ref), custom_call_target="tpu_custom_call" | custom-call | flops 2147483648 | bytes 4194304 | tf_op jit(solution)/shard_map/pallas_call | solution.py:46
  52.2 2.9 %collective-permute-start.4 = (bf16[64,128]{1,0:T(8,128)(2,1)S(1)}, bf16[64,128]{1,0:T(8,128)(2,1)S(1)}, u32[]{:S(2)}, u32[]{:S(2)}) collective-permute-start(bf16[64,128]{1,0:T(8,128)(2,1)S(1)} %get-tuple-element.49), channel_id=1, source_target_pairs={{0,1},{1,0},{2,3},{3,2},{4,5},{5,4},{6,7},{7,6},{8,9},{9,8},{10,11... | collective-permute-start | bytes 49160 | tf_op jit(solution)/shard_map/ppermute | solution.py:296
  55.1 2.2 %collective-permute-start.3 = (bf16[64,128]{1,0:T(8,128)(2,1)S(1)}, bf16[64,128]{1,0:T(8,128)(2,1)S(1)}, u32[]{:S(2)}, u32[]{:S(2)}) collective-permute-start(bf16[64,128]{1,0:T(8,128)(2,1)S(1)} %get-tuple-element.50), channel_id=1, source_target_pairs={{8,0},{16,8},{24,16},{32,24},{40,32},{48,40},{56,48},{64,56},{72,6... | collective-permute-start | bytes 49160 | tf_op jit(solution)/shard_map/ppermute | solution.py:290
  57.3 3.8 %collective-permute-start.2 = (bf16[64,128]{1,0:T(8,128)(2,1)S(1)}, bf16[64,128]{1,0:T(8,128)(2,1)S(1)}, u32[]{:S(2)}, u32[]{:S(2)}) collective-permute-start(bf16[64,128]{1,0:T(8,128)(2,1)S(1)} %get-tuple-element.51), channel_id=1, source_target_pairs={{0,8},{8,16},{16,24},{24,32},{32,40},{40,48},{48,56},{56,64},{64,7... | collective-permute-start | bytes 49160 | tf_op jit(solution)/shard_map/ppermute | solution.py:290
  65.6 14.1 %shard_map.124 = (bf16[1024,256]{1,0:T(8,128)(2,1)}, bf16[4608,128]{1,0:T(8,128)(2,1)}, bf16[4608,128]{1,0:T(8,128)(2,1)}) custom-call(s32[2]{0:T(128)} %pad_add_fusion.1.core_ref, bf16[1024,128]{1,0:T(8,128)(2,1)} %get-tuple-element.24.pooled_ref, bf16[64,128]{1,0:T(8,128)(2,1)} %copy-done.11, bf16[64,128]{1,0:T(8,128)(2,1)} %copy-done.10, ...), custom_call_target="tpu_custom_call" | custom-call | flops 8589934592 | bytes 4194304 | tf_op jit(solution)/shard_map/pallas_call | solution.py:46
  79.8 3.0 %collective-permute-done.6 = bf16[4608,128]{1,0:T(8,128)(2,1)S(1)} collective-permute-done((bf16[4608,128]{1,0:T(8,128)(2,1)}, bf16[4608,128]{1,0:T(8,128)(2,1)S(1)}, u32[]{:S(2)}, u32[]{:S(2)}) %collective-permute-start.6) | collective-permute-done | bytes 1179680 | tf_op jit(solution)/shard_map/ppermute | solution.py:296
  82.8 2.6 %add_convert_fusion = bf16[4608,128]{1,0:T(8,128)(2,1)} fusion(bf16[4608,128]{1,0:T(8,128)(2,1)S(1)} %collective-permute-done.6, bf16[4608,128]{1,0:T(8,128)(2,1)} %get-tuple-element.28), kind=kLoop, calls=%fused_computation | loop fusion | flops 2359296 | bytes 3538944 | tf_op jit(solution)/shard_map/convert_element_type | solution.py:399
  85.4 4.7 %all-to-all-start.1 = ((bf16[16,288,128]{2,1,0:T(8,128)(2,1)}), bf16[16,288,128]{2,1,0:T(8,128)(2,1)S(1)}, u32[]{:S(2)}, u32[]{:S(2)}) async-start(bf16[16,288,128]{2,1,0:T(8,128)(2,1)} %bitcast.14), calls=%async_computation.1 | async-start | bytes 2359296 | tf_op jit(solution)/shard_map/all_to_all | solution.py:300
  90.1 8.7 %shard_map.125 = (bf16[2304,128]{1,0:T(8,128)(2,1)}, bf16[2304,128]{1,0:T(8,128)(2,1)}) custom-call(s32[2]{0:T(128)} %pad_add_fusion.1.core_ref, s32[1,1024]{1,0:T(1,128)} %bitcast.37, bf16[1024,256]{1,0:T(8,128)(2,1)} %get-tuple-element.32.act_ref, bf16[9,256,128]{2,1,0:T(8,128)(2,1)} %weight_ref.3), custom_call_target="tpu_custom_call" | custom-call | flops 4294967296 | bytes 4194304 | tf_op jit(solution)/shard_map/pallas_call | solution.py:46
  98.8 8.2 %all-to-all-done.1 = bf16[16,288,128]{2,1,0:T(8,128)(2,1)S(1)} async-done(((bf16[16,288,128]{2,1,0:T(8,128)(2,1)}), bf16[16,288,128]{2,1,0:T(8,128)(2,1)S(1)}, u32[]{:S(2)}, u32[]{:S(2)}) %all-to-all-start.1) | async-done | bytes 1179680 | tf_op jit(solution)/shard_map/all_to_all | solution.py:300
  107.2 10.6 %all_to_all.20 = bf16[4,288,128]{2,1,0:T(8,128)(2,1)S(1)} all-to-all(bf16[4,288,128]{2,1,0:T(8,128)(2,1)S(1)} %broadcast_in_dim.8), channel_id=1, replica_groups=mesh['x'=4,'z'=4,'y'=4,'c'=2] {'y'}, dimensions={0} | all-to-all | bytes 589824 | tf_op jit(solution)/shard_map/all_to_all | solution.py:300
  119.1 6.5 %all-to-all-start.3 = ((bf16[16,288,128]{2,1,0:T(8,128)(2,1)}), bf16[16,288,128]{2,1,0:T(8,128)(2,1)S(1)}, u32[]{:S(2)}, u32[]{:S(2)}) async-start(bf16[16,288,128]{2,1,0:T(8,128)(2,1)} %broadcast_in_dim.18), calls=%async_computation.3 | async-start | bytes 2359296 | tf_op jit(solution)/shard_map/all_to_all | solution.py:300
  126.4 2.7 %collective-permute-start.10 = (bf16[576,128]{1,0:T(8,128)(2,1)S(1)}, bf16[576,128]{1,0:T(8,128)(2,1)S(1)}, u32[]{:S(2)}, u32[]{:S(2)}) collective-permute-start(bf16[576,128]{1,0:T(8,128)(2,1)S(1)} %get-tuple-element.44), channel_id=1, source_target_pairs={{0,6},{2,0},{4,2},{6,4},{1,7},{3,1},{5,3},{7,5},{8,14},{10,8},{12,... | collective-permute-start | bytes 442376 | tf_op jit(solution)/shard_map/ppermute | solution.py:418
  129.1 3.7 %collective-permute-done.8 = bf16[576,128]{1,0:T(8,128)(2,1)S(1)} collective-permute-done((bf16[576,128]{1,0:T(8,128)(2,1)S(1)}, bf16[576,128]{1,0:T(8,128)(2,1)S(1)}, u32[]{:S(2)}, u32[]{:S(2)}) %collective-permute-start.8) | collective-permute-done | bytes 147488 | tf_op jit(solution)/shard_map/ppermute | solution.py:418
  133.4 2.4 %collective-permute-done.9 = bf16[576,128]{1,0:T(8,128)(2,1)S(1)} collective-permute-done((bf16[576,128]{1,0:T(8,128)(2,1)S(1)}, bf16[576,128]{1,0:T(8,128)(2,1)S(1)}, u32[]{:S(2)}, u32[]{:S(2)}) %collective-permute-start.9) | collective-permute-done | bytes 147488 | tf_op jit(solution)/shard_map/ppermute | solution.py:418
  137.8 7.3 %collective-permute-done.11 = bf16[64,128]{1,0:T(8,128)(2,1)S(1)} collective-permute-done((bf16[64,128]{1,0:T(8,128)(2,1)S(1)}, bf16[64,128]{1,0:T(8,128)(2,1)S(1)}, u32[]{:S(2)}, u32[]{:S(2)}) %collective-permute-start.11) | collective-permute-done | bytes 16416 | tf_op jit(solution)/shard_map/ppermute | solution.py:421
  145.8 2.8 %collective-permute-done.12.theirs_ref = bf16[36,128,128]{2,1,0:T(8,128)(2,1)S(1)} collective-permute-done((bf16[36,128,128]{2,1,0:T(8,128)(2,1)S(1)}, bf16[36,128,128]{2,1,0:T(8,128)(2,1)S(1)}, u32[]{:S(2)}, u32[]{:S(2)}) %collective-permute-start.12) | collective-permute-done | bytes 1179680 | tf_op jit(solution)/shard_map/ppermute | solution.py:296
  148.7 2.9 %shard_map.126 = (f32[27,128,256]{2,1,0:T(8,128)}, f32[9,256,128]{2,1,0:T(8,128)}) custom-call(bf16[36,128,128]{2,1,0:T(8,128)(2,1)S(1)} %bitcast.28, bf16[36,128,128]{2,1,0:T(8,128)(2,1)S(1)} %collective-permute-done.12.theirs_ref, s32[2]{0:T(128)S(1)} %copy-done), custom_call_target="tpu_custom_call" | custom-call | tf_op jit(solution)/shard_map/pallas_call | solution.py:278
  (60 shorter events, 16.7 us)
Async XLA Ops:
  8.0 18.5 %copy-start.5 = (s32[1,1,4,64]{3,2,1,0:T(4,128)S(1)}, s32[1,1,4,64]{3,2,1,0:T(4,128)}, u32[]{:S(2)}) copy-start(s32[1,1,4,64]{3,2,1,0:T(4,128)} %param.13) | copy-start | bytes 3076
  8.0 37.0 %all-to-all-start = ((bf16[128,40,128]{2,1,0:T(8,128)(2,1)}), bf16[128,40,128]{2,1,0:T(8,128)(2,1)S(1)}, u32[]{:S(2)}, u32[]{:S(2)}) async-start(bf16[128,40,128]{2,1,0:T(8,128)(2,1)} %shard_map.121), calls=%async_computation | async-start | bytes 2621440 | tf_op jit(solution)/shard_map/all_to_all | solution.py:300
  19.3 14.7 %collective-permute-start.1 = (bf16[64,128]{1,0:T(8,128)(2,1)S(1)}, bf16[64,128]{1,0:T(8,128)(2,1)S(1)}, u32[]{:S(2)}, u32[]{:S(2)}) collective-permute-start(bf16[64,128]{1,0:T(8,128)(2,1)S(1)} %get-tuple-element.41), channel_id=1, source_target_pairs={{8,0},{16,8},{24,16},{32,24},{40,32},{48,40},{56,48},{64,56},{72,6... | collective-permute-start | bytes 49160 | tf_op jit(solution)/shard_map/ppermute | solution.py:290
  24.6 12.7 %collective-permute-start = (bf16[64,128]{1,0:T(8,128)(2,1)S(1)}, bf16[64,128]{1,0:T(8,128)(2,1)S(1)}, u32[]{:S(2)}, u32[]{:S(2)}) collective-permute-start(bf16[64,128]{1,0:T(8,128)(2,1)S(1)} %get-tuple-element.42), channel_id=1, source_target_pairs={{0,8},{8,16},{16,24},{24,32},{32,40},{40,48},{48,56},{56,64},{64,7... | collective-permute-start | bytes 49160 | tf_op jit(solution)/shard_map/ppermute | solution.py:290
  34.0 3.3 %copy-start.6 = (bf16[64,128]{1,0:T(8,128)(2,1)}, bf16[64,128]{1,0:T(8,128)(2,1)S(1)}, u32[]{:S(2)}) copy-start(bf16[64,128]{1,0:T(8,128)(2,1)S(1)} %collective-permute-done.1.high_ref) | copy-start | bytes 49156
  46.1 15.6 %copy-start.4 = (s32[1,1,26,256]{3,1,2,0:T(1,128)S(1)}, s32[1,1,26,256]{3,1,2,0:T(1,128)}, u32[]{:S(2)}) copy-start(s32[1,1,26,256]{3,1,2,0:T(1,128)} %param.15) | copy-start | bytes 79876
  46.1 16.2 %copy-start.3 = (s32[1,1,26,256]{3,1,2,0:T(1,128)S(1)}, s32[1,1,26,256]{3,1,2,0:T(1,128)}, u32[]{:S(2)}) copy-start(s32[1,1,26,256]{3,1,2,0:T(1,128)} %param.14) | copy-start | bytes 79876
  51.5 11.5 %collective-permute-start.5 = (bf16[64,128]{1,0:T(8,128)(2,1)S(1)}, bf16[64,128]{1,0:T(8,128)(2,1)S(1)}, u32[]{:S(2)}, u32[]{:S(2)}) collective-permute-start(bf16[64,128]{1,0:T(8,128)(2,1)S(1)} %get-tuple-element.48), channel_id=1, source_target_pairs={{1,2},{3,4},{5,6},{2,1},{4,3},{6,5},{9,10},{11,12},{13,14},{10,9},... | collective-permute-start | bytes 49160 | tf_op jit(solution)/shard_map/ppermute | solution.py:360
  52.2 10.9 %collective-permute-start.4 = (bf16[64,128]{1,0:T(8,128)(2,1)S(1)}, bf16[64,128]{1,0:T(8,128)(2,1)S(1)}, u32[]{:S(2)}, u32[]{:S(2)}) collective-permute-start(bf16[64,128]{1,0:T(8,128)(2,1)S(1)} %get-tuple-element.49), channel_id=1, source_target_pairs={{0,1},{1,0},{2,3},{3,2},{4,5},{5,4},{6,7},{7,6},{8,9},{9,8},{10,11... | collective-permute-start | bytes 49160 | tf_op jit(solution)/shard_map/ppermute | solution.py:296
  55.1 8.0 %collective-permute-start.3 = (bf16[64,128]{1,0:T(8,128)(2,1)S(1)}, bf16[64,128]{1,0:T(8,128)(2,1)S(1)}, u32[]{:S(2)}, u32[]{:S(2)}) collective-permute-start(bf16[64,128]{1,0:T(8,128)(2,1)S(1)} %get-tuple-element.50), channel_id=1, source_target_pairs={{8,0},{16,8},{24,16},{32,24},{40,32},{48,40},{56,48},{64,56},{72,6... | collective-permute-start | bytes 49160 | tf_op jit(solution)/shard_map/ppermute | solution.py:290
  57.3 7.7 %collective-permute-start.2 = (bf16[64,128]{1,0:T(8,128)(2,1)S(1)}, bf16[64,128]{1,0:T(8,128)(2,1)S(1)}, u32[]{:S(2)}, u32[]{:S(2)}) collective-permute-start(bf16[64,128]{1,0:T(8,128)(2,1)S(1)} %get-tuple-element.51), channel_id=1, source_target_pairs={{0,8},{8,16},{16,24},{24,32},{32,40},{40,48},{48,56},{56,64},{64,7... | collective-permute-start | bytes 49160 | tf_op jit(solution)/shard_map/ppermute | solution.py:290
  63.1 2.0 %copy-start.7 = (bf16[64,128]{1,0:T(8,128)(2,1)}, bf16[64,128]{1,0:T(8,128)(2,1)S(1)}, u32[]{:S(2)}) copy-start(bf16[64,128]{1,0:T(8,128)(2,1)S(1)} %collective-permute-done.5.paired_ref) | copy-start | bytes 49156
  63.1 2.0 %copy-start.9 = (bf16[64,128]{1,0:T(8,128)(2,1)}, bf16[64,128]{1,0:T(8,128)(2,1)S(1)}, u32[]{:S(2)}) copy-start(bf16[64,128]{1,0:T(8,128)(2,1)S(1)} %collective-permute-done.4.swapped_ref) | copy-start | bytes 49156
  79.7 3.1 %collective-permute-start.6 = (bf16[4608,128]{1,0:T(8,128)(2,1)}, bf16[4608,128]{1,0:T(8,128)(2,1)S(1)}, u32[]{:S(2)}, u32[]{:S(2)}) collective-permute-start(bf16[4608,128]{1,0:T(8,128)(2,1)} %get-tuple-element.29), channel_id=1, source_target_pairs={{0,1},{1,0},{2,3},{3,2},{4,5},{5,4},{6,7},{7,6},{8,9},{9,8},{10,11... | collective-permute-start | bytes 3538952 | tf_op jit(solution)/shard_map/ppermute | solution.py:296
  85.4 21.6 %all-to-all-start.1 = ((bf16[16,288,128]{2,1,0:T(8,128)(2,1)}), bf16[16,288,128]{2,1,0:T(8,128)(2,1)S(1)}, u32[]{:S(2)}, u32[]{:S(2)}) async-start(bf16[16,288,128]{2,1,0:T(8,128)(2,1)} %bitcast.14), calls=%async_computation.1 | async-start | bytes 2359296 | tf_op jit(solution)/shard_map/all_to_all | solution.py:300
  98.8 26.7 %collective-permute-start.7 = (bf16[2304,128]{1,0:T(8,128)(2,1)}, bf16[2304,128]{1,0:T(8,128)(2,1)S(1)}, u32[]{:S(2)}, u32[]{:S(2)}) collective-permute-start(bf16[2304,128]{1,0:T(8,128)(2,1)} %get-tuple-element.34), channel_id=1, source_target_pairs={{0,1},{1,0},{2,3},{3,2},{4,5},{5,4},{6,7},{7,6},{8,9},{9,8},{10,11... | collective-permute-start | bytes 1769480 | tf_op jit(solution)/shard_map/ppermute | solution.py:296
  119.1 6.5 %copy-start.2 = (bf16[2304,128]{1,0:T(8,128)(2,1)S(1)}, bf16[2304,128]{1,0:T(8,128)(2,1)}, u32[]{:S(2)}) copy-start(bf16[2304,128]{1,0:T(8,128)(2,1)} %get-tuple-element.33) | copy-start | bytes 1769476
  119.1 26.8 %all-to-all-start.3 = ((bf16[16,288,128]{2,1,0:T(8,128)(2,1)}), bf16[16,288,128]{2,1,0:T(8,128)(2,1)S(1)}, u32[]{:S(2)}, u32[]{:S(2)}) async-start(bf16[16,288,128]{2,1,0:T(8,128)(2,1)} %broadcast_in_dim.18), calls=%async_computation.3 | async-start | bytes 2359296 | tf_op jit(solution)/shard_map/all_to_all | solution.py:300
  125.8 22.9 %copy-start = (s32[2]{0:T(128)S(1)}, s32[2]{0:T(128)}, u32[]{:S(2)}) copy-start(s32[2]{0:T(128)} %pad_add_fusion.1.core_ref) | copy-start | bytes 28
  125.8 7.0 %collective-permute-start.8 = (bf16[576,128]{1,0:T(8,128)(2,1)S(1)}, bf16[576,128]{1,0:T(8,128)(2,1)S(1)}, u32[]{:S(2)}, u32[]{:S(2)}) collective-permute-start(bf16[576,128]{1,0:T(8,128)(2,1)S(1)} %get-tuple-element.43), channel_id=1, source_target_pairs={{0,2},{2,4},{4,6},{6,0},{1,3},{3,5},{5,7},{7,1},{8,10},{10,12},{12... | collective-permute-start | bytes 442376 | tf_op jit(solution)/shard_map/ppermute | solution.py:418
  126.4 6.9 %collective-permute-start.10 = (bf16[576,128]{1,0:T(8,128)(2,1)S(1)}, bf16[576,128]{1,0:T(8,128)(2,1)S(1)}, u32[]{:S(2)}, u32[]{:S(2)}) collective-permute-start(bf16[576,128]{1,0:T(8,128)(2,1)S(1)} %get-tuple-element.44), channel_id=1, source_target_pairs={{0,6},{2,0},{4,2},{6,4},{1,7},{3,1},{5,3},{7,5},{8,14},{10,8},{12,... | collective-permute-start | bytes 442376 | tf_op jit(solution)/shard_map/ppermute | solution.py:418
  129.1 6.6 %collective-permute-start.9 = (bf16[576,128]{1,0:T(8,128)(2,1)S(1)}, bf16[576,128]{1,0:T(8,128)(2,1)S(1)}, u32[]{:S(2)}, u32[]{:S(2)}) collective-permute-start(bf16[576,128]{1,0:T(8,128)(2,1)S(1)} %get-tuple-element.45), channel_id=1, source_target_pairs={{0,4},{2,6},{4,0},{6,2},{1,5},{3,7},{5,1},{7,3},{8,12},{10,14},{12... | collective-permute-start | bytes 442376 | tf_op jit(solution)/shard_map/ppermute | solution.py:418
  135.9 9.3 %collective-permute-start.11 = (bf16[64,128]{1,0:T(8,128)(2,1)S(1)}, bf16[64,128]{1,0:T(8,128)(2,1)S(1)}, u32[]{:S(2)}, u32[]{:S(2)}) collective-permute-start(bf16[64,128]{1,0:T(8,128)(2,1)S(1)} %slice.91), channel_id=1, source_target_pairs={{7,8},{15,16},{23,24},{31,32},{39,40},{47,48},{55,56},{63,64},{71,... | collective-permute-start | bytes 49160 | tf_op jit(solution)/shard_map/ppermute | solution.py:421
  145.8 2.8 %collective-permute-start.12 = (bf16[36,128,128]{2,1,0:T(8,128)(2,1)S(1)}, bf16[36,128,128]{2,1,0:T(8,128)(2,1)S(1)}, u32[]{:S(2)}, u32[]{:S(2)}) collective-permute-start(bf16[36,128,128]{2,1,0:T(8,128)(2,1)S(1)} %bitcast.27), channel_id=1, source_target_pairs={{0,1},{1,0},{2,3},{3,2},{4,5},{5,4},{6,7},{7,6},{8,9},{9,8},{10,11... | collective-permute-start | bytes 3538952 | tf_op jit(solution)/shard_map/ppermute | solution.py:296
  (4 other events, 4.2 us)

commit v5 on v4

--- a/solution.py
+++ b/solution.py
@@ -102,6 +102,15 @@
     rows_ref[...] = dot(hot(rim_ref[...] == iota((256, voxels), 1)), pooled).astype(BF)
 
 
+def shifts(rows):
+    total = rows.shape[0]
+    y = iota(rows.shape, 0)
+    wide = rows.astype(F32)
+    lower = jnp.where(y == 0, 0.0, pltpu.roll(wide, 1, 0))
+    upper = jnp.where(y == total - 1, 0.0, pltpu.roll(wide, total - 1, 0))
+    return [lower.astype(BF), rows, upper.astype(BF)]
+
+
 def conv_kernel(
     core_ref,
     pooled_ref,
@@ -111,6 +120,10 @@
     paired_ref,
     src_ref,
     dst_ref,
+    low_ref,
+    high_ref,
+    cell_ref,
+    head_ref,
     weight_any,
     upstream_any,
     window_any,
@@ -127,6 +140,7 @@
     act_ref,
     keep_ref,
     send_ref,
+    edge_ref,
     sems,
 ):
     voxels = pooled_ref.shape[0]
@@ -158,14 +172,34 @@
         place = hot(dst_ref[k : k + 1, :] == iota((voxels, 256), 0))
         table_ref[:, k * 128 : (k + 1) * 128] = dot(place, rows_ref[k * 256 : (k + 1) * 256, :]).astype(BF)
     table_ref[:, OFFS * 128 :] = pooled_ref[...]
+    edge_ref[...] = jnp.zeros_like(edge_ref)
+    lows, highs = shifts(low_ref[...]), shifts(high_ref[...])
+    reach = jnp.zeros((128, 256), F32)
+    for b in range(3):
+        edge_ref[64:128, b * 128 : (b + 1) * 128] = highs[2 - b]
+        edge_ref[0:64, (3 + b) * 128 : (4 + b) * 128] = lows[2 - b]
+    for a in range(2):
+        for b in range(3):
+            k = 3 * a + b
+            reach = reach + dot_lanes(edge_ref[:, k * 128 : (k + 1) * 128], head_ref[6 * a + b])
+    edge_row = iota((128, voxels), 0)
+    at_edge = hot(cell_ref[...] == jnp.where(edge_row < 64, edge_row, edge_row + (63 * 64 - 64)))
+    coarse = reach.astype(BF)
+    fine = (reach - coarse.astype(F32)).astype(BF)
     loads[0].wait()
     loads[1].wait()
+    upstream_ref[...] += dot_rows(at_edge, coarse) + dot_rows(at_edge, fine)
+    loads[2].wait()
+    beside = dot_rows(at_edge, edge_ref[...])
+    for a in range(2):
+        span = slice(a * 768, a * 768 + 384)
+        window_ref[:, span] = (window_ref[:, span].astype(F32) + beside[:, a * 384 : (a + 1) * 384]).astype(BF)
     for m in range(0, voxels, 512):
         pre = dot(table_ref[m : m + 512, :], weight_ref[...])
         sigma = 1.0 / (1.0 + jnp.exp(-pre))
         act_ref[m : m + 512, :] = (pre * sigma).astype(BF)
         slope = sigma * (1.0 + pre * (1.0 - sigma))
-        grad = upstream_ref[m : m + 512, :].astype(F32) * slope
+        grad = upstream_ref[m : m + 512, :].astype(BF).astype(F32) * slope
         grad_ref[:, m : m + 512] = grad.T.astype(BF)
     stores = [pltpu.make_async_copy(act_ref, act_any, sems.at[3])]
     stores[0].start()
@@ -177,7 +211,6 @@
             to = step * wide + at
             keep_ref[to : to + 128, :] = jnp.where(first, lo, hi).T.astype(BF)
             send_ref[to : to + 128, :] = jnp.where(first, hi, lo).T.astype(BF)
-    loads[2].wait()
     base = (OFFS + 1) * 128
     stores += [
         pltpu.make_async_copy(send_ref.at[0:base], send_any.at[0:base], sems.at[4]),
@@ -226,13 +259,13 @@
             out_ref[d * EDGED + 512 : (d + 1) * EDGED, :] = beyond.astype(BF)
 
 
-def window_kernel(cell_ref, low_ref, cot_ref, high_ref, weight_ref, window_ref, up_ref, pad_ref, rows_ref):
+def window_kernel(cell_ref, cot_ref, weight_ref, window_ref, up_ref, pad_ref, rows_ref):
     voxels = window_ref.shape[0]
     pad_ref[:, 0:8, :] = jnp.zeros((66, 8, 128), F32)
     pad_ref[:, 72:80, :] = jnp.zeros((66, 8, 128), F32)
-    pad_ref[0, 8:72, :] = low_ref[...].astype(F32)
+    pad_ref[0, 8:72, :] = jnp.zeros((64, 128), F32)
     pad_ref[1:65, 8:72, :] = cot_ref[...].reshape(64, 64, 128).astype(F32)
-    pad_ref[65, 8:72, :] = high_ref[...].astype(F32)
+    pad_ref[65, 8:72, :] = jnp.zeros((64, 128), F32)
 
     def step_window(v, carry):
         cell = cell_ref[v]
@@ -250,7 +283,7 @@
             rows = rows_ref[a, pl.ds(2 - b, voxels, stride=4), :].astype(BF)
             window_ref[:, k * 128 : (k + 1) * 128] = rows
             up = up + dot_lanes(rows, weight_ref[k])
-    up_ref[...] = up.astype(BF)
+    up_ref[...] = up
 
 
 def final_kernel(mine_ref, theirs_ref, core_ref, conv_any, head_any, conv_ref, head_ref, sems):
@@ -332,9 +365,9 @@
 
     window, upstream = call(
         window_kernel,
-        [shape((voxels, 9 * 128), BF), shape((voxels, 256), BF)],
-        (bev_cell.reshape(voxels), cot_low, cot, cot_high, head_weight),
-        specs=[SMEM] + [VMEM] * 4,
+        [shape((voxels, 9 * 128), BF), shape((voxels, 256), F32)],
+        (bev_cell.reshape(voxels), cot, head_weight),
+        specs=[SMEM] + [VMEM] * 2,
         scratch=[pltpu.VMEM((66, 80, 128), F32), pltpu.VMEM((3, 4 * voxels, 128), F32)],
         flops=1 << 30,
     )
@@ -373,11 +406,15 @@
             paired,
             jnp.transpose(pair_in[0, 0]),
             pair_out[0, 0],
+            cot_low,
+            cot_high,
+            bev_cell.reshape(1, voxels),
+            head_weight,
             conv_weight.reshape(table_width, 256),
             upstream,
             window,
         ),
-        specs=[SMEM] + [VMEM] * 7 + [ANY] * 3,
+        specs=[SMEM] + [VMEM] * 11 + [ANY] * 3,
         out=ANY,
         scratch=[
             pltpu.VMEM((256, 5 * 128), BF),
@@ -385,11 +422,12 @@
             pltpu.VMEM((voxels, table_width), BF),
             pltpu.VMEM((256, voxels), BF),
             pltpu.VMEM((table_width, 256), BF),
-            pltpu.VMEM((voxels, 256), BF),
+            pltpu.VMEM((voxels, 256), F32),
             pltpu.VMEM((voxels, 9 * 128), BF),
             pltpu.VMEM((voxels, 256), BF),
             pltpu.VMEM((grad_rows, 128), BF),
             pltpu.VMEM((grad_rows, 128), BF),
+            pltpu.VMEM((128, 6 * 128), BF),
             pltpu.SemaphoreType.DMA((8,)),
         ],
         flops=8 << 30,

time: 153 us -> 148 us (0.967)
  waiting for transfers between devices: 39.9 us -> 37 us
  starting transfers between devices: 43.8 us -> 41.1 us
  Pallas kernels: 44.8 us -> 46.6 us
    ppermute x4, waiting for transfers between devices: 11.8 us -> 3.44 us  [chain(): lax.ppermute(block, axes, [(i, i + by) for i in range(count) if 0 <= i +...]
    all_to_all x3, waiting for transfers between devices: 8.17 us -> 13.7 us  [exchange(): return lax.all_to_all(block, axes, split_axis=0, concat_axis=0, tiled=True)]
    ppermute x4, starting transfers between devices: 3 us -> 1.06 us  [swap(): return lax.ppermute(block, 'c', [(0, 1), (1, 0)])]
    pallas_call x5, Pallas kernels: 42 us -> 43.8 us  [call(): pl.pallas_call(kernel, out_shape=outs, in_specs=[VMEM] * len(args) if spe...]
  transfers between devices with their start and end apart: 16 -> 16, of which waited for: 10 -> 9; matrix products, arithmetic and copies ran while one was open for 4% -> 5% of each run, Pallas kernels for 10% -> 14%
where the time goes in v5:
time: 148 us; the launch traced here: 147 us
  Pallas kernels  46.6 us (31%)
  starting transfers between devices  41.1 us (28%)
  waiting for transfers between devices  37 us (25%)
  blocking collectives  10.4 us (7%)
  local copies, waits for them, and re-layouts  6.63 us (4%)
  other arithmetic  4.33 us (3%)
    pallas_call x5, Pallas kernels, call(): pl.pallas_call(kernel, out_shape=outs, in_specs=[VMEM] * len(args) if spe...  43.8 us
    all_to_all x3, starting transfers between devices, exchange(): return lax.all_to_all(block, axes, split_axis=0, concat_axis=0, tiled=True)  21 us
    all_to_all x3, waiting for transfers between devices, exchange(): return lax.all_to_all(block, axes, split_axis=0, concat_axis=0, tiled=True)  13.7 us
    ppermute x4, starting transfers between devices, chain(): lax.ppermute(block, axes, [(i, i + by) for i in range(count) if 0 <= i +...  13.2 us
    all_to_all x1, blocking collectives, exchange(): return lax.all_to_all(block, axes, split_axis=0, concat_axis=0, tiled=True)  10.4 us
    ppermute x1, waiting for transfers between devices, local(): lax.ppermute(total[512:].astype(BF), ALL, ends + [(j, i) for i, j in ends])  7.32 us
    ppermute x3, waiting for transfers between devices, local(): lax.ppermute(sent, 'y', [(i, (i + d) % 4) for i in range(4)]).astype(F32)  6.64 us
    ppermute x4, waiting for transfers between devices, swap(): return lax.ppermute(block, 'c', [(0, 1), (1, 0)])  5.9 us
  transfers between devices with their start and end apart: 16, of which 9 were waited for; matrix products, arithmetic and copies ran while one was open for 5% of the time, Pallas kernels for 14%

profile of v5, /device:TPU:2, one launch (start us, length us, event | category | flops | bytes accessed | tf_op | source)
XLA Modules:
  0.0 147.2 jit_solution(1145087666046431137)
XLA Ops:
  0.6 7.4 %shard_map.121 = bf16[128,40,128]{2,1,0:T(8,128)(2,1)} custom-call(s32[1,2048]{1,0:T(1,128)} %bitcast.34, s32[1,2048]{1,0:T(1,128)} %bitcast.35, bf16[2048,128]{1,0:T(8,128)(2,1)} %points_ref.1), custom_call_target="tpu_custom_call" | custom-call | flops 3221225472 | bytes 4194304 | tf_op jit(solution)/shard_map/pallas_call | solution.py:46
  8.0 10.5 %all-to-all-start = ((bf16[128,40,128]{2,1,0:T(8,128)(2,1)}), bf16[128,40,128]{2,1,0:T(8,128)(2,1)S(1)}, u32[]{:S(2)}, u32[]{:S(2)}) async-start(bf16[128,40,128]{2,1,0:T(8,128)(2,1)} %shard_map.121), calls=%async_computation | async-start | bytes 2621440 | tf_op jit(solution)/shard_map/all_to_all | solution.py:333
  19.3 5.2 %collective-permute-start.5 = (bf16[64,128]{1,0:T(8,128)(2,1)S(1)}, bf16[64,128]{1,0:T(8,128)(2,1)S(1)}, u32[]{:S(2)}, u32[]{:S(2)}) collective-permute-start(bf16[64,128]{1,0:T(8,128)(2,1)S(1)} %get-tuple-element.41), channel_id=1, source_target_pairs={{8,0},{16,8},{24,16},{32,24},{40,32},{48,40},{56,48},{64,56},{72,6... | collective-permute-start | bytes 49160 | tf_op jit(solution)/shard_map/ppermute | solution.py:323
  24.5 1.9 %collective-permute-start.4 = (bf16[64,128]{1,0:T(8,128)(2,1)S(1)}, bf16[64,128]{1,0:T(8,128)(2,1)S(1)}, u32[]{:S(2)}, u32[]{:S(2)}) collective-permute-start(bf16[64,128]{1,0:T(8,128)(2,1)S(1)} %get-tuple-element.42), channel_id=1, source_target_pairs={{0,8},{8,16},{16,24},{24,32},{32,40},{40,48},{48,56},{56,64},{64,7... | collective-permute-start | bytes 49160 | tf_op jit(solution)/shard_map/ppermute | solution.py:323
  27.3 7.3 %shard_map.122 = (bf16[1024,1152]{1,0:T(8,128)(2,1)}, f32[1024,256]{1,0:T(8,128)}) custom-call(s32[1024]{0:T(1024)} %bitcast.36, bf16[4096,128]{1,0:T(8,128)(2,1)} %bitcast.32, bf16[9,256,128]{2,1,0:T(8,128)(2,1)} %weight_ref.3), custom_call_target="tpu_custom_call" | custom-call | flops 1073741824 | bytes 4194304 | tf_op jit(solution)/shard_map/pallas_call | solution.py:46
  34.6 5.5 %all-to-all-done.got_ref = bf16[128,40,128]{2,1,0:T(8,128)(2,1)S(1)} async-done(((bf16[128,40,128]{2,1,0:T(8,128)(2,1)}), bf16[128,40,128]{2,1,0:T(8,128)(2,1)S(1)}, u32[]{:S(2)}, u32[]{:S(2)}) %all-to-all-start) | async-done | bytes 1310752 | tf_op jit(solution)/shard_map/all_to_all | solution.py:333
  41.3 4.6 %shard_map.123 = (bf16[1024,128]{1,0:T(8,128)(2,1)}, bf16[256,128]{1,0:T(8,128)(2,1)}) custom-call(bf16[128,40,128]{2,1,0:T(8,128)(2,1)} %copy-done.1, s32[256,1]{1,0:T(8,128)} %reshape.98.rim_ref), custom_call_target="tpu_custom_call" | custom-call | flops 2147483648 | bytes 4194304 | tf_op jit(solution)/shard_map/pallas_call | solution.py:46
  48.3 3.8 %collective-permute-start.1 = (bf16[64,128]{1,0:T(8,128)(2,1)S(1)}, bf16[64,128]{1,0:T(8,128)(2,1)S(1)}, u32[]{:S(2)}, u32[]{:S(2)}) collective-permute-start(bf16[64,128]{1,0:T(8,128)(2,1)S(1)} %get-tuple-element.50), channel_id=1, source_target_pairs={{8,0},{16,8},{24,16},{32,24},{40,32},{48,40},{56,48},{64,56},{72,6... | collective-permute-start | bytes 49160 | tf_op jit(solution)/shard_map/ppermute | solution.py:323
  52.1 2.3 %collective-permute-start = (bf16[64,128]{1,0:T(8,128)(2,1)S(1)}, bf16[64,128]{1,0:T(8,128)(2,1)S(1)}, u32[]{:S(2)}, u32[]{:S(2)}) collective-permute-start(bf16[64,128]{1,0:T(8,128)(2,1)S(1)} %get-tuple-element.51), channel_id=1, source_target_pairs={{0,8},{8,16},{16,24},{24,32},{32,40},{40,48},{48,56},{56,64},{64,7... | collective-permute-start | bytes 49160 | tf_op jit(solution)/shard_map/ppermute | solution.py:323
  56.4 3.4 %collective-permute-done.left_ref = bf16[64,128]{1,0:T(8,128)(2,1)S(1)} collective-permute-done((bf16[64,128]{1,0:T(8,128)(2,1)S(1)}, bf16[64,128]{1,0:T(8,128)(2,1)S(1)}, u32[]{:S(2)}, u32[]{:S(2)}) %collective-permute-start) | collective-permute-done | bytes 16416 | tf_op jit(solution)/shard_map/ppermute | solution.py:323
  60.4 15.7 %shard_map.124 = (bf16[1024,256]{1,0:T(8,128)(2,1)}, bf16[4608,128]{1,0:T(8,128)(2,1)}, bf16[4608,128]{1,0:T(8,128)(2,1)}) custom-call(s32[2]{0:T(128)} %pad_add_fusion.1.core_ref, bf16[1024,128]{1,0:T(8,128)(2,1)} %get-tuple-element.24.pooled_ref, bf16[64,128]{1,0:T(8,128)(2,1)} %copy-done.11, bf16[64,128]{1,0:T(8,128)(2,1)} %copy-done.10, ...), custom_call_target="tpu_custom_call" | custom-call | flops 8589934592 | bytes 4194304 | tf_op jit(solution)/shard_map/pallas_call | solution.py:46
  76.2 3.0 %collective-permute-done.6 = bf16[4608,128]{1,0:T(8,128)(2,1)S(1)} collective-permute-done((bf16[4608,128]{1,0:T(8,128)(2,1)}, bf16[4608,128]{1,0:T(8,128)(2,1)S(1)}, u32[]{:S(2)}, u32[]{:S(2)}) %collective-permute-start.6) | collective-permute-done | bytes 1179680 | tf_op jit(solution)/shard_map/ppermute | solution.py:329
  79.3 2.6 %add_convert_fusion = bf16[4608,128]{1,0:T(8,128)(2,1)} fusion(bf16[4608,128]{1,0:T(8,128)(2,1)S(1)} %collective-permute-done.6, bf16[4608,128]{1,0:T(8,128)(2,1)} %get-tuple-element.28), kind=kLoop, calls=%fused_computation | loop fusion | flops 2359296 | bytes 3538944 | tf_op jit(solution)/shard_map/convert_element_type | solution.py:437
  81.9 4.0 %all-to-all-start.1 = ((bf16[16,288,128]{2,1,0:T(8,128)(2,1)}), bf16[16,288,128]{2,1,0:T(8,128)(2,1)S(1)}, u32[]{:S(2)}, u32[]{:S(2)}) async-start(bf16[16,288,128]{2,1,0:T(8,128)(2,1)} %bitcast.15), calls=%async_computation.1 | async-start | bytes 2359296 | tf_op jit(solution)/shard_map/all_to_all | solution.py:333
  85.8 8.7 %shard_map.125 = (bf16[2304,128]{1,0:T(8,128)(2,1)}, bf16[2304,128]{1,0:T(8,128)(2,1)}) custom-call(s32[2]{0:T(128)} %pad_add_fusion.1.core_ref, s32[1,1024]{1,0:T(1,128)} %bitcast.38, bf16[1024,256]{1,0:T(8,128)(2,1)} %get-tuple-element.32.act_ref, bf16[9,256,128]{2,1,0:T(8,128)(2,1)} %weight_ref.3), custom_call_target="tpu_custom_call" | custom-call | flops 4294967296 | bytes 4194304 | tf_op jit(solution)/shard_map/pallas_call | solution.py:46
  94.5 8.2 %all-to-all-done.1 = bf16[16,288,128]{2,1,0:T(8,128)(2,1)S(1)} async-done(((bf16[16,288,128]{2,1,0:T(8,128)(2,1)}), bf16[16,288,128]{2,1,0:T(8,128)(2,1)S(1)}, u32[]{:S(2)}, u32[]{:S(2)}) %all-to-all-start.1) | async-done | bytes 1179680 | tf_op jit(solution)/shard_map/all_to_all | solution.py:333
  102.9 10.4 %all_to_all.20 = bf16[4,288,128]{2,1,0:T(8,128)(2,1)S(1)} all-to-all(bf16[4,288,128]{2,1,0:T(8,128)(2,1)S(1)} %broadcast_in_dim.8), channel_id=1, replica_groups=mesh['x'=4,'z'=4,'y'=4,'c'=2] {'y'}, dimensions={0} | all-to-all | bytes 589824 | tf_op jit(solution)/shard_map/all_to_all | solution.py:333
  114.5 6.5 %all-to-all-start.3 = ((bf16[16,288,128]{2,1,0:T(8,128)(2,1)}), bf16[16,288,128]{2,1,0:T(8,128)(2,1)S(1)}, u32[]{:S(2)}, u32[]{:S(2)}) async-start(bf16[16,288,128]{2,1,0:T(8,128)(2,1)} %broadcast_in_dim.18), calls=%async_computation.3 | async-start | bytes 2359296 | tf_op jit(solution)/shard_map/all_to_all | solution.py:333
  121.9 2.7 %collective-permute-start.10 = (bf16[576,128]{1,0:T(8,128)(2,1)S(1)}, bf16[576,128]{1,0:T(8,128)(2,1)S(1)}, u32[]{:S(2)}, u32[]{:S(2)}) collective-permute-start(bf16[576,128]{1,0:T(8,128)(2,1)S(1)} %get-tuple-element.44), channel_id=1, source_target_pairs={{0,6},{2,0},{4,2},{6,4},{1,7},{3,1},{5,3},{7,5},{8,14},{10,8},{12,... | collective-permute-start | bytes 442376 | tf_op jit(solution)/shard_map/ppermute | solution.py:456
  124.6 3.7 %collective-permute-done.8 = bf16[576,128]{1,0:T(8,128)(2,1)S(1)} collective-permute-done((bf16[576,128]{1,0:T(8,128)(2,1)S(1)}, bf16[576,128]{1,0:T(8,128)(2,1)S(1)}, u32[]{:S(2)}, u32[]{:S(2)}) %collective-permute-start.8) | collective-permute-done | bytes 147488 | tf_op jit(solution)/shard_map/ppermute | solution.py:456
  128.8 2.4 %collective-permute-done.9 = bf16[576,128]{1,0:T(8,128)(2,1)S(1)} collective-permute-done((bf16[576,128]{1,0:T(8,128)(2,1)S(1)}, bf16[576,128]{1,0:T(8,128)(2,1)S(1)}, u32[]{:S(2)}, u32[]{:S(2)}) %collective-permute-start.9) | collective-permute-done | bytes 147488 | tf_op jit(solution)/shard_map/ppermute | solution.py:456
  133.3 7.3 %collective-permute-done.11 = bf16[64,128]{1,0:T(8,128)(2,1)S(1)} collective-permute-done((bf16[64,128]{1,0:T(8,128)(2,1)S(1)}, bf16[64,128]{1,0:T(8,128)(2,1)S(1)}, u32[]{:S(2)}, u32[]{:S(2)}) %collective-permute-start.11) | collective-permute-done | bytes 16416 | tf_op jit(solution)/shard_map/ppermute | solution.py:459
  141.3 2.8 %collective-permute-done.12.theirs_ref = bf16[36,128,128]{2,1,0:T(8,128)(2,1)S(1)} collective-permute-done((bf16[36,128,128]{2,1,0:T(8,128)(2,1)S(1)}, bf16[36,128,128]{2,1,0:T(8,128)(2,1)S(1)}, u32[]{:S(2)}, u32[]{:S(2)}) %collective-permute-start.12) | collective-permute-done | bytes 1179680 | tf_op jit(solution)/shard_map/ppermute | solution.py:329
  144.1 2.9 %shard_map.126 = (f32[27,128,256]{2,1,0:T(8,128)}, f32[9,256,128]{2,1,0:T(8,128)}) custom-call(bf16[36,128,128]{2,1,0:T(8,128)(2,1)S(1)} %bitcast.28, bf16[36,128,128]{2,1,0:T(8,128)(2,1)S(1)} %collective-permute-done.12.theirs_ref, s32[2]{0:T(128)S(1)} %copy-done), custom_call_target="tpu_custom_call" | custom-call | tf_op jit(solution)/shard_map/pallas_call | solution.py:311
  (60 shorter events, 13.3 us)
Async XLA Ops:
  8.0 18.5 %copy-start.5 = (s32[1,1,4,64]{3,2,1,0:T(4,128)S(1)}, s32[1,1,4,64]{3,2,1,0:T(4,128)}, u32[]{:S(2)}) copy-start(s32[1,1,4,64]{3,2,1,0:T(4,128)} %param.13) | copy-start | bytes 3076
  8.0 32.1 %all-to-all-start = ((bf16[128,40,128]{2,1,0:T(8,128)(2,1)}), bf16[128,40,128]{2,1,0:T(8,128)(2,1)S(1)}, u32[]{:S(2)}, u32[]{:S(2)}) async-start(bf16[128,40,128]{2,1,0:T(8,128)(2,1)} %shard_map.121), calls=%async_computation | async-start | bytes 2621440 | tf_op jit(solution)/shard_map/all_to_all | solution.py:333
  19.3 32.7 %collective-permute-start.5 = (bf16[64,128]{1,0:T(8,128)(2,1)S(1)}, bf16[64,128]{1,0:T(8,128)(2,1)S(1)}, u32[]{:S(2)}, u32[]{:S(2)}) collective-permute-start(bf16[64,128]{1,0:T(8,128)(2,1)S(1)} %get-tuple-element.41), channel_id=1, source_target_pairs={{8,0},{16,8},{24,16},{32,24},{40,32},{48,40},{56,48},{64,56},{72,6... | collective-permute-start | bytes 49160 | tf_op jit(solution)/shard_map/ppermute | solution.py:323
  24.5 31.8 %collective-permute-start.4 = (bf16[64,128]{1,0:T(8,128)(2,1)S(1)}, bf16[64,128]{1,0:T(8,128)(2,1)S(1)}, u32[]{:S(2)}, u32[]{:S(2)}) collective-permute-start(bf16[64,128]{1,0:T(8,128)(2,1)S(1)} %get-tuple-element.42), channel_id=1, source_target_pairs={{0,8},{8,16},{16,24},{24,32},{32,40},{40,48},{48,56},{56,64},{64,7... | collective-permute-start | bytes 49160 | tf_op jit(solution)/shard_map/ppermute | solution.py:323
  41.3 13.7 %copy-start.4 = (s32[1,1,26,256]{3,1,2,0:T(1,128)S(1)}, s32[1,1,26,256]{3,1,2,0:T(1,128)}, u32[]{:S(2)}) copy-start(s32[1,1,26,256]{3,1,2,0:T(1,128)} %param.15) | copy-start | bytes 79876
  41.3 14.3 %copy-start.3 = (s32[1,1,26,256]{3,1,2,0:T(1,128)S(1)}, s32[1,1,26,256]{3,1,2,0:T(1,128)}, u32[]{:S(2)}) copy-start(s32[1,1,26,256]{3,1,2,0:T(1,128)} %param.14) | copy-start | bytes 79876
  46.7 9.7 %collective-permute-start.3 = (bf16[64,128]{1,0:T(8,128)(2,1)S(1)}, bf16[64,128]{1,0:T(8,128)(2,1)S(1)}, u32[]{:S(2)}, u32[]{:S(2)}) collective-permute-start(bf16[64,128]{1,0:T(8,128)(2,1)S(1)} %get-tuple-element.48), channel_id=1, source_target_pairs={{1,2},{3,4},{5,6},{2,1},{4,3},{6,5},{9,10},{11,12},{13,14},{10,9},... | collective-permute-start | bytes 49160 | tf_op jit(solution)/shard_map/ppermute | solution.py:393
  47.3 9.0 %collective-permute-start.2 = (bf16[64,128]{1,0:T(8,128)(2,1)S(1)}, bf16[64,128]{1,0:T(8,128)(2,1)S(1)}, u32[]{:S(2)}, u32[]{:S(2)}) collective-permute-start(bf16[64,128]{1,0:T(8,128)(2,1)S(1)} %get-tuple-element.49), channel_id=1, source_target_pairs={{0,1},{1,0},{2,3},{3,2},{4,5},{5,4},{6,7},{7,6},{8,9},{9,8},{10,11... | collective-permute-start | bytes 49160 | tf_op jit(solution)/shard_map/ppermute | solution.py:329
  48.3 8.1 %collective-permute-start.1 = (bf16[64,128]{1,0:T(8,128)(2,1)S(1)}, bf16[64,128]{1,0:T(8,128)(2,1)S(1)}, u32[]{:S(2)}, u32[]{:S(2)}) collective-permute-start(bf16[64,128]{1,0:T(8,128)(2,1)S(1)} %get-tuple-element.50), channel_id=1, source_target_pairs={{8,0},{16,8},{24,16},{32,24},{40,32},{48,40},{56,48},{64,56},{72,6... | collective-permute-start | bytes 49160 | tf_op jit(solution)/shard_map/ppermute | solution.py:323
  52.1 7.8 %copy-start.6 = (bf16[64,128]{1,0:T(8,128)(2,1)}, bf16[64,128]{1,0:T(8,128)(2,1)S(1)}, u32[]{:S(2)}) copy-start(bf16[64,128]{1,0:T(8,128)(2,1)S(1)} %collective-permute-done.5.high_ref) | copy-start | bytes 49156
  52.1 7.7 %collective-permute-start = (bf16[64,128]{1,0:T(8,128)(2,1)S(1)}, bf16[64,128]{1,0:T(8,128)(2,1)S(1)}, u32[]{:S(2)}, u32[]{:S(2)}) collective-permute-start(bf16[64,128]{1,0:T(8,128)(2,1)S(1)} %get-tuple-element.51), channel_id=1, source_target_pairs={{0,8},{8,16},{16,24},{24,32},{32,40},{40,48},{48,56},{56,64},{64,7... | collective-permute-start | bytes 49160 | tf_op jit(solution)/shard_map/ppermute | solution.py:323
  56.3 3.5 %copy-start.7 = (bf16[64,128]{1,0:T(8,128)(2,1)}, bf16[64,128]{1,0:T(8,128)(2,1)S(1)}, u32[]{:S(2)}) copy-start(bf16[64,128]{1,0:T(8,128)(2,1)S(1)} %collective-permute-done.4.low_ref) | copy-start | bytes 49156
  56.3 3.5 %copy-start.8 = (bf16[64,128]{1,0:T(8,128)(2,1)}, bf16[64,128]{1,0:T(8,128)(2,1)S(1)}, u32[]{:S(2)}) copy-start(bf16[64,128]{1,0:T(8,128)(2,1)S(1)} %collective-permute-done.3.paired_ref) | copy-start | bytes 49156
  76.2 3.1 %collective-permute-start.6 = (bf16[4608,128]{1,0:T(8,128)(2,1)}, bf16[4608,128]{1,0:T(8,128)(2,1)S(1)}, u32[]{:S(2)}, u32[]{:S(2)}) collective-permute-start(bf16[4608,128]{1,0:T(8,128)(2,1)} %get-tuple-element.29), channel_id=1, source_target_pairs={{0,1},{1,0},{2,3},{3,2},{4,5},{5,4},{6,7},{7,6},{8,9},{9,8},{10,11... | collective-permute-start | bytes 3538952 | tf_op jit(solution)/shard_map/ppermute | solution.py:329
  81.9 20.8 %all-to-all-start.1 = ((bf16[16,288,128]{2,1,0:T(8,128)(2,1)}), bf16[16,288,128]{2,1,0:T(8,128)(2,1)S(1)}, u32[]{:S(2)}, u32[]{:S(2)}) async-start(bf16[16,288,128]{2,1,0:T(8,128)(2,1)} %bitcast.15), calls=%async_computation.1 | async-start | bytes 2359296 | tf_op jit(solution)/shard_map/all_to_all | solution.py:333
  94.5 26.5 %collective-permute-start.7 = (bf16[2304,128]{1,0:T(8,128)(2,1)}, bf16[2304,128]{1,0:T(8,128)(2,1)S(1)}, u32[]{:S(2)}, u32[]{:S(2)}) collective-permute-start(bf16[2304,128]{1,0:T(8,128)(2,1)} %get-tuple-element.34), channel_id=1, source_target_pairs={{0,1},{1,0},{2,3},{3,2},{4,5},{5,4},{6,7},{7,6},{8,9},{9,8},{10,11... | collective-permute-start | bytes 1769480 | tf_op jit(solution)/shard_map/ppermute | solution.py:329
  114.5 6.5 %copy-start.2 = (bf16[2304,128]{1,0:T(8,128)(2,1)S(1)}, bf16[2304,128]{1,0:T(8,128)(2,1)}, u32[]{:S(2)}) copy-start(bf16[2304,128]{1,0:T(8,128)(2,1)} %get-tuple-element.33) | copy-start | bytes 1769476
  114.5 26.8 %all-to-all-start.3 = ((bf16[16,288,128]{2,1,0:T(8,128)(2,1)}), bf16[16,288,128]{2,1,0:T(8,128)(2,1)S(1)}, u32[]{:S(2)}, u32[]{:S(2)}) async-start(bf16[16,288,128]{2,1,0:T(8,128)(2,1)} %broadcast_in_dim.18), calls=%async_computation.3 | async-start | bytes 2359296 | tf_op jit(solution)/shard_map/all_to_all | solution.py:333
  121.2 22.9 %copy-start = (s32[2]{0:T(128)S(1)}, s32[2]{0:T(128)}, u32[]{:S(2)}) copy-start(s32[2]{0:T(128)} %pad_add_fusion.1.core_ref) | copy-start | bytes 28
  121.3 7.0 %collective-permute-start.8 = (bf16[576,128]{1,0:T(8,128)(2,1)S(1)}, bf16[576,128]{1,0:T(8,128)(2,1)S(1)}, u32[]{:S(2)}, u32[]{:S(2)}) collective-permute-start(bf16[576,128]{1,0:T(8,128)(2,1)S(1)} %get-tuple-element.43), channel_id=1, source_target_pairs={{0,2},{2,4},{4,6},{6,0},{1,3},{3,5},{5,7},{7,1},{8,10},{10,12},{12... | collective-permute-start | bytes 442376 | tf_op jit(solution)/shard_map/ppermute | solution.py:456
  121.9 6.9 %collective-permute-start.10 = (bf16[576,128]{1,0:T(8,128)(2,1)S(1)}, bf16[576,128]{1,0:T(8,128)(2,1)S(1)}, u32[]{:S(2)}, u32[]{:S(2)}) collective-permute-start(bf16[576,128]{1,0:T(8,128)(2,1)S(1)} %get-tuple-element.44), channel_id=1, source_target_pairs={{0,6},{2,0},{4,2},{6,4},{1,7},{3,1},{5,3},{7,5},{8,14},{10,8},{12,... | collective-permute-start | bytes 442376 | tf_op jit(solution)/shard_map/ppermute | solution.py:456
  124.6 6.6 %collective-permute-start.9 = (bf16[576,128]{1,0:T(8,128)(2,1)S(1)}, bf16[576,128]{1,0:T(8,128)(2,1)S(1)}, u32[]{:S(2)}, u32[]{:S(2)}) collective-permute-start(bf16[576,128]{1,0:T(8,128)(2,1)S(1)} %get-tuple-element.45), channel_id=1, source_target_pairs={{0,4},{2,6},{4,0},{6,2},{1,5},{3,7},{5,1},{7,3},{8,12},{10,14},{12... | collective-permute-start | bytes 442376 | tf_op jit(solution)/shard_map/ppermute | solution.py:456
  131.3 9.3 %collective-permute-start.11 = (bf16[64,128]{1,0:T(8,128)(2,1)S(1)}, bf16[64,128]{1,0:T(8,128)(2,1)S(1)}, u32[]{:S(2)}, u32[]{:S(2)}) collective-permute-start(bf16[64,128]{1,0:T(8,128)(2,1)S(1)} %slice.91), channel_id=1, source_target_pairs={{7,8},{15,16},{23,24},{31,32},{39,40},{47,48},{55,56},{63,64},{71,... | collective-permute-start | bytes 49160 | tf_op jit(solution)/shard_map/ppermute | solution.py:459
  141.3 2.8 %collective-permute-start.12 = (bf16[36,128,128]{2,1,0:T(8,128)(2,1)S(1)}, bf16[36,128,128]{2,1,0:T(8,128)(2,1)S(1)}, u32[]{:S(2)}, u32[]{:S(2)}) collective-permute-start(bf16[36,128,128]{2,1,0:T(8,128)(2,1)S(1)} %bitcast.27), channel_id=1, source_target_pairs={{0,1},{1,0},{2,3},{3,2},{4,5},{5,4},{6,7},{7,6},{8,9},{9,8},{10,11... | collective-permute-start | bytes 3538952 | tf_op jit(solution)/shard_map/ppermute | solution.py:329
  (4 other events, 8.6 us)

commit v6 on v5

--- a/solution.py
+++ b/solution.py
@@ -86,7 +86,7 @@
         out_ref[m // CAP : (m + 512) // CAP, 0:CAP, :] = rows.reshape(512 // CAP, CAP, 128)
 
 
-def pool_kernel(got_ref, rim_ref, pooled_ref, rows_ref, acc_ref):
+def pool_kernel(got_ref, rim_ref, pooled_ref, right_ref, left_ref, swap_ref, pair_ref, acc_ref):
     voxels = pooled_ref.shape[0]
     own = (iota((8, 256), 1) >> 5) == iota((8, 256), 0)
     for i in range(16):
@@ -99,7 +99,9 @@
         acc_ref[...] = part if i == 0 else acc_ref[...] + part
     pooled = acc_ref[...].astype(BF)
     pooled_ref[...] = pooled
-    rows_ref[...] = dot(hot(rim_ref[...] == iota((256, voxels), 1)), pooled).astype(BF)
+    rows = dot(hot(rim_ref[...] == iota((256, voxels), 1)), pooled).astype(BF)
+    for side, ref in enumerate((right_ref, left_ref, swap_ref, pair_ref)):
+        ref[...] = rows[side * 64 : (side + 1) * 64]
 
 
 def shifts(rows):
@@ -372,26 +374,29 @@
         flops=1 << 30,
     )
 
-    got, window, upstream = lax.optimization_barrier((got, window, upstream))
+    sources, targets = jnp.transpose(pair_in[0, 0]), pair_out[0, 0]
+    got, window, upstream, sources, targets, core = lax.optimization_barrier(
+        (got, window, upstream, sources, targets, core)
+    )
 
     sides = send_rows[0, 0]
     even = core[0] == 0
     sides = jnp.concatenate(
         [sides[:2], jnp.where(even, sides[3:], sides[2:3]), jnp.where(even, sides[2:3], sides[3:])]
     )
-    pooled, outgoing = call(
+    pooled, to_right, to_left, to_swap, to_pair = call(
         pool_kernel,
-        [shape((voxels, 128), BF), shape((256, 128), BF)],
+        [shape((voxels, 128), BF)] + [shape((64, 128), BF)] * 4,
         (got, sides.reshape(256, 1)),
         scratch=[pltpu.VMEM((voxels, 128), F32)],
         flops=2 << 30,
     )
     layers = lax.axis_size(HEIGHT)
     pairs = [(i, i + 1) for i in range(1, layers - 1, 2)]
-    from_left = chain(outgoing[64:128], PLANE, 1)
-    from_right = chain(outgoing[0:64], PLANE, -1)
-    paired = lax.ppermute(outgoing[192:256], HEIGHT, pairs + [(j, i) for i, j in pairs])
-    swapped = swap(outgoing[128:192])
+    from_left = chain(to_left, PLANE, 1)
+    from_right = chain(to_right, PLANE, -1)
+    paired = lax.ppermute(to_pair, HEIGHT, pairs + [(j, i) for i, j in pairs])
+    swapped = swap(to_swap)
     table_width = (OFFS + 1) * 128
     grad_rows = table_width + 9 * 128
     act, keep, send = call(
@@ -404,8 +409,8 @@
             from_right,
             swapped,
             paired,
-            jnp.transpose(pair_in[0, 0]),
-            pair_out[0, 0],
+            sources,
+            targets,
             cot_low,
             cot_high,
             bev_cell.reshape(1, voxels),

time: 148 us -> 147 us (level)
  starting transfers between devices: 41.1 us -> 46.4 us
  waiting for transfers between devices: 37 us -> 33.5 us
  local copies, waits for them, and re-layouts: 6.63 us -> 5.02 us
    ppermute x4, starting transfers between devices: 1.06 us -> 4.44 us  [swap(): return lax.ppermute(block, 'c', [(0, 1), (1, 0)])]
    ppermute x4, waiting for transfers between devices: 3.44 us -> 0.63 us  [chain(): lax.ppermute(block, axes, [(i, i + by) for i in range(count) if 0 <= i +...]
    ppermute x4, starting transfers between devices: 13.2 us -> 15.1 us  [chain(): lax.ppermute(block, axes, [(i, i + by) for i in range(count) if 0 <= i +...]
    unnamed x26 -> x28, local copies, waits for them, and re-layouts: 3.07 us -> 2.02 us
  transfers between devices with their start and end apart: 16 -> 16, of which waited for: 9 -> 9; matrix products, arithmetic and copies ran while one was open for 5% -> 4% of each run, Pallas kernels for 14% -> 14%
where the time goes in v6:
time: 147 us; the launch traced here: 146 us
  Pallas kernels  46.6 us (32%)
  starting transfers between devices  46.4 us (32%)
  waiting for transfers between devices  33.5 us (23%)
  blocking collectives  9.22 us (6%)
  local copies, waits for them, and re-layouts  5.02 us (3%)
  other arithmetic  3.81 us (3%)
    pallas_call x5, Pallas kernels, call(): pl.pallas_call(kernel, out_shape=outs, in_specs=[VMEM] * len(args) if spe...  43.7 us
    all_to_all x3, starting transfers between devices, exchange(): return lax.all_to_all(block, axes, split_axis=0, concat_axis=0, tiled=True)  20.8 us
    ppermute x4, starting transfers between devices, chain(): lax.ppermute(block, axes, [(i, i + by) for i in range(count) if 0 <= i +...  15.1 us
    all_to_all x3, waiting for transfers between devices, exchange(): return lax.all_to_all(block, axes, split_axis=0, concat_axis=0, tiled=True)  13.3 us
    all_to_all x1, blocking collectives, exchange(): return lax.all_to_all(block, axes, split_axis=0, concat_axis=0, tiled=True)  9.22 us
    ppermute x1, waiting for transfers between devices, local(): lax.ppermute(total[512:].astype(BF), ALL, ends + [(j, i) for i, j in ends])  7.32 us
    ppermute x3, waiting for transfers between devices, local(): lax.ppermute(sent, 'y', [(i, (i + d) % 4) for i in range(4)]).astype(F32)  6.64 us
    ppermute x4, waiting for transfers between devices, swap(): return lax.ppermute(block, 'c', [(0, 1), (1, 0)])  5.54 us
  transfers between devices with their start and end apart: 16, of which 9 were waited for; matrix products, arithmetic and copies ran while one was open for 4% of the time, Pallas kernels for 14%

profile of v6, /device:TPU:2, one launch (start us, length us, event | category | flops | bytes accessed | tf_op | source)
XLA Modules:
  0.0 145.7 jit_solution(14358332406983484580)
XLA Ops:
  0.6 7.4 %shard_map.121 = bf16[128,40,128]{2,1,0:T(8,128)(2,1)} custom-call(s32[1,2048]{1,0:T(1,128)} %bitcast.37, s32[1,2048]{1,0:T(1,128)} %bitcast.38, bf16[2048,128]{1,0:T(8,128)(2,1)} %points_ref.1), custom_call_target="tpu_custom_call" | custom-call | flops 3221225472 | bytes 4194304 | tf_op jit(solution)/shard_map/pallas_call | solution.py:46
  8.0 10.5 %all-to-all-start = ((bf16[128,40,128]{2,1,0:T(8,128)(2,1)}), bf16[128,40,128]{2,1,0:T(8,128)(2,1)S(1)}, u32[]{:S(2)}, u32[]{:S(2)}) async-start(bf16[128,40,128]{2,1,0:T(8,128)(2,1)} %shard_map.121), calls=%async_computation | async-start | bytes 2621440 | tf_op jit(solution)/shard_map/all_to_all | solution.py:335
  19.3 5.2 %collective-permute-start.5 = (bf16[64,128]{1,0:T(8,128)(2,1)S(1)}, bf16[64,128]{1,0:T(8,128)(2,1)S(1)}, u32[]{:S(2)}, u32[]{:S(2)}) collective-permute-start(bf16[64,128]{1,0:T(8,128)(2,1)S(1)} %get-tuple-element.53), channel_id=1, source_target_pairs={{8,0},{16,8},{24,16},{32,24},{40,32},{48,40},{56,48},{64,56},{72,6... | collective-permute-start | bytes 49160 | tf_op jit(solution)/shard_map/ppermute | solution.py:325
  24.5 1.9 %collective-permute-start.4 = (bf16[64,128]{1,0:T(8,128)(2,1)S(1)}, bf16[64,128]{1,0:T(8,128)(2,1)S(1)}, u32[]{:S(2)}, u32[]{:S(2)}) collective-permute-start(bf16[64,128]{1,0:T(8,128)(2,1)S(1)} %get-tuple-element.54), channel_id=1, source_target_pairs={{0,8},{8,16},{16,24},{24,32},{32,40},{40,48},{48,56},{56,64},{64,7... | collective-permute-start | bytes 49160 | tf_op jit(solution)/shard_map/ppermute | solution.py:325
  27.9 7.3 %shard_map.122 = (bf16[1024,1152]{1,0:T(8,128)(2,1)}, f32[1024,256]{1,0:T(8,128)}) custom-call(s32[1024]{0:T(1024)} %bitcast.39, bf16[4096,128]{1,0:T(8,128)(2,1)} %bitcast.35, bf16[9,256,128]{2,1,0:T(8,128)(2,1)} %weight_ref.3), custom_call_target="tpu_custom_call" | custom-call | flops 1073741824 | bytes 4194304 | tf_op jit(solution)/shard_map/pallas_call | solution.py:46
  35.3 4.9 %all-to-all-done.got_ref = bf16[128,40,128]{2,1,0:T(8,128)(2,1)S(1)} async-done(((bf16[128,40,128]{2,1,0:T(8,128)(2,1)}), bf16[128,40,128]{2,1,0:T(8,128)(2,1)S(1)}, u32[]{:S(2)}, u32[]{:S(2)}) %all-to-all-start) | async-done | bytes 1310752 | tf_op jit(solution)/shard_map/all_to_all | solution.py:335
  41.3 4.6 %shard_map.123 = (bf16[1024,128]{1,0:T(8,128)(2,1)}, bf16[64,128]{1,0:T(8,128)(2,1)}, bf16[64,128]{1,0:T(8,128)(2,1)}, bf16[64,128]{1,0:T(8,128)(2,1)}, bf16[64,128]{1,0:T(8,128)(2,1)}) custom-call(bf16[128,40,128]{2,1,0:T(8,128)(2,1)} %copy-done.2, s32[256,1]{1,0:T(8,128)} %reshape.100.rim_ref), custom_call_target="tpu_custom_call" | custom-call | flops 2147483648 | bytes 4194304 | tf_op jit(solution)/shard_map/pallas_call | solution.py:46
  45.9 2.7 %collective-permute-start = (bf16[64,128]{1,0:T(8,128)(2,1)}, bf16[64,128]{1,0:T(8,128)(2,1)S(1)}, u32[]{:S(2)}, u32[]{:S(2)}) collective-permute-start(bf16[64,128]{1,0:T(8,128)(2,1)} %get-tuple-element.32), channel_id=1, source_target_pairs={{0,8},{8,16},{16,24},{24,32},{32,40},{40,48},{48,56},{56,64},{64,7... | collective-permute-start | bytes 49160 | tf_op jit(solution)/shard_map/ppermute | solution.py:325
  48.6 5.2 %collective-permute-start.1 = (bf16[64,128]{1,0:T(8,128)(2,1)}, bf16[64,128]{1,0:T(8,128)(2,1)S(1)}, u32[]{:S(2)}, u32[]{:S(2)}) collective-permute-start(bf16[64,128]{1,0:T(8,128)(2,1)} %get-tuple-element.33), channel_id=1, source_target_pairs={{8,0},{16,8},{24,16},{32,24},{40,32},{48,40},{56,48},{64,56},{72,6... | collective-permute-start | bytes 49160 | tf_op jit(solution)/shard_map/ppermute | solution.py:325
  56.1 15.7 %shard_map.124 = (bf16[1024,256]{1,0:T(8,128)(2,1)}, bf16[4608,128]{1,0:T(8,128)(2,1)}, bf16[4608,128]{1,0:T(8,128)(2,1)}) custom-call(s32[2]{0:T(128)} %copy-done, bf16[1024,128]{1,0:T(8,128)(2,1)} %get-tuple-element.31.pooled_ref, bf16[64,128]{1,0:T(8,128)(2,1)} %copy-done.9, bf16[64,128]{1,0:T(8,128)(2,1)} %copy-done.10, bf16[64,128]{1,0:T(8,128)(2,1)} %copy-done.11, ...), custom_call_target="tpu_custom_call" | custom-call | flops 8589934592 | bytes 4194304 | tf_op jit(solution)/shard_map/pallas_call | solution.py:46
  71.8 4.3 %collective-permute-start.6 = (bf16[4608,128]{1,0:T(8,128)(2,1)}, bf16[4608,128]{1,0:T(8,128)(2,1)S(1)}, u32[]{:S(2)}, u32[]{:S(2)}) collective-permute-start(bf16[4608,128]{1,0:T(8,128)(2,1)} %get-tuple-element.41), channel_id=1, source_target_pairs={{0,1},{1,0},{2,3},{3,2},{4,5},{5,4},{6,7},{7,6},{8,9},{9,8},{10,11... | collective-permute-start | bytes 3538952 | tf_op jit(solution)/shard_map/ppermute | solution.py:331
  76.1 2.7 %collective-permute-done.6 = bf16[4608,128]{1,0:T(8,128)(2,1)S(1)} collective-permute-done((bf16[4608,128]{1,0:T(8,128)(2,1)}, bf16[4608,128]{1,0:T(8,128)(2,1)S(1)}, u32[]{:S(2)}, u32[]{:S(2)}) %collective-permute-start.6) | collective-permute-done | bytes 1179680 | tf_op jit(solution)/shard_map/ppermute | solution.py:331
  78.8 2.6 %add_convert_fusion = bf16[4608,128]{1,0:T(8,128)(2,1)} fusion(bf16[4608,128]{1,0:T(8,128)(2,1)S(1)} %collective-permute-done.6, bf16[4608,128]{1,0:T(8,128)(2,1)} %get-tuple-element.40), kind=kLoop, calls=%fused_computation | loop fusion | flops 2359296 | bytes 3538944 | tf_op jit(solution)/shard_map/convert_element_type | solution.py:442
  81.4 3.9 %all-to-all-start.1 = ((bf16[16,288,128]{2,1,0:T(8,128)(2,1)}), bf16[16,288,128]{2,1,0:T(8,128)(2,1)S(1)}, u32[]{:S(2)}, u32[]{:S(2)}) async-start(bf16[16,288,128]{2,1,0:T(8,128)(2,1)} %bitcast.16), calls=%async_computation.1 | async-start | bytes 2359296 | tf_op jit(solution)/shard_map/all_to_all | solution.py:335
  85.3 8.7 %shard_map.125 = (bf16[2304,128]{1,0:T(8,128)(2,1)}, bf16[2304,128]{1,0:T(8,128)(2,1)}) custom-call(s32[2]{0:T(128)} %copy-done, s32[1,1024]{1,0:T(1,128)} %bitcast.41, bf16[1024,256]{1,0:T(8,128)(2,1)} %get-tuple-element.44.act_ref, bf16[9,256,128]{2,1,0:T(8,128)(2,1)} %weight_ref.3), custom_call_target="tpu_custom_call" | custom-call | flops 4294967296 | bytes 4194304 | tf_op jit(solution)/shard_map/pallas_call | solution.py:46
  94.1 8.4 %all-to-all-done.1 = bf16[16,288,128]{2,1,0:T(8,128)(2,1)S(1)} async-done(((bf16[16,288,128]{2,1,0:T(8,128)(2,1)}), bf16[16,288,128]{2,1,0:T(8,128)(2,1)S(1)}, u32[]{:S(2)}, u32[]{:S(2)}) %all-to-all-start.1) | async-done | bytes 1179680 | tf_op jit(solution)/shard_map/all_to_all | solution.py:335
  102.7 9.2 %all_to_all.20 = bf16[4,288,128]{2,1,0:T(8,128)(2,1)S(1)} all-to-all(bf16[4,288,128]{2,1,0:T(8,128)(2,1)S(1)} %broadcast_in_dim.8), channel_id=1, replica_groups=mesh['x'=4,'z'=4,'y'=4,'c'=2] {'y'}, dimensions={0} | all-to-all | bytes 589824 | tf_op jit(solution)/shard_map/all_to_all | solution.py:335
  113.1 6.4 %all-to-all-start.3 = ((bf16[16,288,128]{2,1,0:T(8,128)(2,1)}), bf16[16,288,128]{2,1,0:T(8,128)(2,1)S(1)}, u32[]{:S(2)}, u32[]{:S(2)}) async-start(bf16[16,288,128]{2,1,0:T(8,128)(2,1)} %broadcast_in_dim.18), calls=%async_computation.3 | async-start | bytes 2359296 | tf_op jit(solution)/shard_map/all_to_all | solution.py:335
  120.4 2.7 %collective-permute-start.10 = (bf16[576,128]{1,0:T(8,128)(2,1)S(1)}, bf16[576,128]{1,0:T(8,128)(2,1)S(1)}, u32[]{:S(2)}, u32[]{:S(2)}) collective-permute-start(bf16[576,128]{1,0:T(8,128)(2,1)S(1)} %get-tuple-element.56), channel_id=1, source_target_pairs={{0,6},{2,0},{4,2},{6,4},{1,7},{3,1},{5,3},{7,5},{8,14},{10,8},{12,... | collective-permute-start | bytes 442376 | tf_op jit(solution)/shard_map/ppermute | solution.py:461
  123.1 4.1 %collective-permute-done.8 = bf16[576,128]{1,0:T(8,128)(2,1)S(1)} collective-permute-done((bf16[576,128]{1,0:T(8,128)(2,1)S(1)}, bf16[576,128]{1,0:T(8,128)(2,1)S(1)}, u32[]{:S(2)}, u32[]{:S(2)}) %collective-permute-start.8) | collective-permute-done | bytes 147488 | tf_op jit(solution)/shard_map/ppermute | solution.py:461
  127.3 2.4 %collective-permute-done.9 = bf16[576,128]{1,0:T(8,128)(2,1)S(1)} collective-permute-done((bf16[576,128]{1,0:T(8,128)(2,1)S(1)}, bf16[576,128]{1,0:T(8,128)(2,1)S(1)}, u32[]{:S(2)}, u32[]{:S(2)}) %collective-permute-start.9) | collective-permute-done | bytes 147488 | tf_op jit(solution)/shard_map/ppermute | solution.py:461
  131.8 7.3 %collective-permute-done.11 = bf16[64,128]{1,0:T(8,128)(2,1)S(1)} collective-permute-done((bf16[64,128]{1,0:T(8,128)(2,1)S(1)}, bf16[64,128]{1,0:T(8,128)(2,1)S(1)}, u32[]{:S(2)}, u32[]{:S(2)}) %collective-permute-start.11) | collective-permute-done | bytes 16416 | tf_op jit(solution)/shard_map/ppermute | solution.py:464
  139.8 2.8 %collective-permute-done.12.theirs_ref = bf16[36,128,128]{2,1,0:T(8,128)(2,1)S(1)} collective-permute-done((bf16[36,128,128]{2,1,0:T(8,128)(2,1)S(1)}, bf16[36,128,128]{2,1,0:T(8,128)(2,1)S(1)}, u32[]{:S(2)}, u32[]{:S(2)}) %collective-permute-start.12) | collective-permute-done | bytes 1179680 | tf_op jit(solution)/shard_map/ppermute | solution.py:331
  142.6 2.9 %shard_map.126 = (f32[27,128,256]{2,1,0:T(8,128)}, f32[9,256,128]{2,1,0:T(8,128)}) custom-call(bf16[36,128,128]{2,1,0:T(8,128)(2,1)S(1)} %bitcast.30, bf16[36,128,128]{2,1,0:T(8,128)(2,1)S(1)} %collective-permute-done.12.theirs_ref, s32[2]{0:T(128)S(1)} %copy-done.1), custom_call_target="tpu_custom_call" | custom-call | tf_op jit(solution)/shard_map/pallas_call | solution.py:313
  (61 shorter events, 10.6 us)
Async XLA Ops:
  8.0 18.5 %copy-start.5 = (s32[1,1,26,256]{3,1,2,0:T(1,128)S(1)}, s32[1,1,26,256]{3,1,2,0:T(1,128)}, u32[]{:S(2)}) copy-start(s32[1,1,26,256]{3,1,2,0:T(1,128)} %param.15) | copy-start | bytes 79876
  8.0 19.1 %copy-start.4 = (s32[1,1,26,256]{3,1,2,0:T(1,128)S(1)}, s32[1,1,26,256]{3,1,2,0:T(1,128)}, u32[]{:S(2)}) copy-start(s32[1,1,26,256]{3,1,2,0:T(1,128)} %param.14) | copy-start | bytes 79876
  8.0 32.1 %all-to-all-start = ((bf16[128,40,128]{2,1,0:T(8,128)(2,1)}), bf16[128,40,128]{2,1,0:T(8,128)(2,1)S(1)}, u32[]{:S(2)}, u32[]{:S(2)}) async-start(bf16[128,40,128]{2,1,0:T(8,128)(2,1)} %shard_map.121), calls=%async_computation | async-start | bytes 2621440 | tf_op jit(solution)/shard_map/all_to_all | solution.py:335
  19.3 34.6 %collective-permute-start.5 = (bf16[64,128]{1,0:T(8,128)(2,1)S(1)}, bf16[64,128]{1,0:T(8,128)(2,1)S(1)}, u32[]{:S(2)}, u32[]{:S(2)}) collective-permute-start(bf16[64,128]{1,0:T(8,128)(2,1)S(1)} %get-tuple-element.53), channel_id=1, source_target_pairs={{8,0},{16,8},{24,16},{32,24},{40,32},{48,40},{56,48},{64,56},{72,6... | collective-permute-start | bytes 49160 | tf_op jit(solution)/shard_map/ppermute | solution.py:325
  24.5 30.3 %collective-permute-start.4 = (bf16[64,128]{1,0:T(8,128)(2,1)S(1)}, bf16[64,128]{1,0:T(8,128)(2,1)S(1)}, u32[]{:S(2)}, u32[]{:S(2)}) collective-permute-start(bf16[64,128]{1,0:T(8,128)(2,1)S(1)} %get-tuple-element.54), channel_id=1, source_target_pairs={{0,8},{8,16},{16,24},{24,32},{32,40},{40,48},{48,56},{56,64},{64,7... | collective-permute-start | bytes 49160 | tf_op jit(solution)/shard_map/ppermute | solution.py:325
  27.9 7.4 %copy-start.6 = (s32[1,1,4,64]{3,2,1,0:T(4,128)S(1)}, s32[1,1,4,64]{3,2,1,0:T(4,128)}, u32[]{:S(2)}) copy-start(s32[1,1,4,64]{3,2,1,0:T(4,128)} %param.13) | copy-start | bytes 3076
  35.3 10.6 %copy-start = (s32[2]{0:T(128)}, s32[2]{0:T(128)S(1)}, u32[]{:S(2)}) copy-start(s32[2]{0:T(128)S(1)} %pad_add_fusion.1.core_ref) | copy-start | bytes 28
  40.2 1.1 copy-start.2
  45.9 8.9 %collective-permute-start = (bf16[64,128]{1,0:T(8,128)(2,1)}, bf16[64,128]{1,0:T(8,128)(2,1)S(1)}, u32[]{:S(2)}, u32[]{:S(2)}) collective-permute-start(bf16[64,128]{1,0:T(8,128)(2,1)} %get-tuple-element.32), channel_id=1, source_target_pairs={{0,8},{8,16},{16,24},{24,32},{32,40},{40,48},{48,56},{56,64},{64,7... | collective-permute-start | bytes 49160 | tf_op jit(solution)/shard_map/ppermute | solution.py:325
  48.6 6.8 %collective-permute-start.1 = (bf16[64,128]{1,0:T(8,128)(2,1)}, bf16[64,128]{1,0:T(8,128)(2,1)S(1)}, u32[]{:S(2)}, u32[]{:S(2)}) collective-permute-start(bf16[64,128]{1,0:T(8,128)(2,1)} %get-tuple-element.33), channel_id=1, source_target_pairs={{8,0},{16,8},{24,16},{32,24},{40,32},{48,40},{56,48},{64,56},{72,6... | collective-permute-start | bytes 49160 | tf_op jit(solution)/shard_map/ppermute | solution.py:325
  53.8 1.6 %collective-permute-start.2 = (bf16[64,128]{1,0:T(8,128)(2,1)}, bf16[64,128]{1,0:T(8,128)(2,1)S(1)}, u32[]{:S(2)}, u32[]{:S(2)}) collective-permute-start(bf16[64,128]{1,0:T(8,128)(2,1)} %get-tuple-element.34), channel_id=1, source_target_pairs={{0,1},{1,0},{2,3},{3,2},{4,5},{5,4},{6,7},{7,6},{8,9},{9,8},{10,11... | collective-permute-start | bytes 49160 | tf_op jit(solution)/shard_map/ppermute | solution.py:331
  53.9 1.6 %copy-start.7 = (bf16[64,128]{1,0:T(8,128)(2,1)}, bf16[64,128]{1,0:T(8,128)(2,1)S(1)}, u32[]{:S(2)}) copy-start(bf16[64,128]{1,0:T(8,128)(2,1)S(1)} %collective-permute-done.5.high_ref) | copy-start | bytes 49156
  53.9 1.5 %collective-permute-start.3 = (bf16[64,128]{1,0:T(8,128)(2,1)}, bf16[64,128]{1,0:T(8,128)(2,1)S(1)}, u32[]{:S(2)}, u32[]{:S(2)}) collective-permute-start(bf16[64,128]{1,0:T(8,128)(2,1)} %get-tuple-element.35), channel_id=1, source_target_pairs={{1,2},{3,4},{5,6},{2,1},{4,3},{6,5},{9,10},{11,12},{13,14},{10,9},... | collective-permute-start | bytes 49160 | tf_op jit(solution)/shard_map/ppermute | solution.py:398
  71.8 7.0 %collective-permute-start.6 = (bf16[4608,128]{1,0:T(8,128)(2,1)}, bf16[4608,128]{1,0:T(8,128)(2,1)S(1)}, u32[]{:S(2)}, u32[]{:S(2)}) collective-permute-start(bf16[4608,128]{1,0:T(8,128)(2,1)} %get-tuple-element.41), channel_id=1, source_target_pairs={{0,1},{1,0},{2,3},{3,2},{4,5},{5,4},{6,7},{7,6},{8,9},{9,8},{10,11... | collective-permute-start | bytes 3538952 | tf_op jit(solution)/shard_map/ppermute | solution.py:331
  81.4 21.1 %all-to-all-start.1 = ((bf16[16,288,128]{2,1,0:T(8,128)(2,1)}), bf16[16,288,128]{2,1,0:T(8,128)(2,1)S(1)}, u32[]{:S(2)}, u32[]{:S(2)}) async-start(bf16[16,288,128]{2,1,0:T(8,128)(2,1)} %bitcast.16), calls=%async_computation.1 | async-start | bytes 2359296 | tf_op jit(solution)/shard_map/all_to_all | solution.py:335
  94.0 25.6 %collective-permute-start.7 = (bf16[2304,128]{1,0:T(8,128)(2,1)}, bf16[2304,128]{1,0:T(8,128)(2,1)S(1)}, u32[]{:S(2)}, u32[]{:S(2)}) collective-permute-start(bf16[2304,128]{1,0:T(8,128)(2,1)} %get-tuple-element.46), channel_id=1, source_target_pairs={{0,1},{1,0},{2,3},{3,2},{4,5},{5,4},{6,7},{7,6},{8,9},{9,8},{10,11... | collective-permute-start | bytes 1769480 | tf_op jit(solution)/shard_map/ppermute | solution.py:331
  113.1 6.4 %copy-start.3 = (bf16[2304,128]{1,0:T(8,128)(2,1)S(1)}, bf16[2304,128]{1,0:T(8,128)(2,1)}, u32[]{:S(2)}) copy-start(bf16[2304,128]{1,0:T(8,128)(2,1)} %get-tuple-element.45) | copy-start | bytes 1769476
  113.1 26.6 %all-to-all-start.3 = ((bf16[16,288,128]{2,1,0:T(8,128)(2,1)}), bf16[16,288,128]{2,1,0:T(8,128)(2,1)S(1)}, u32[]{:S(2)}, u32[]{:S(2)}) async-start(bf16[16,288,128]{2,1,0:T(8,128)(2,1)} %broadcast_in_dim.18), calls=%async_computation.3 | async-start | bytes 2359296 | tf_op jit(solution)/shard_map/all_to_all | solution.py:335
  119.7 22.9 %copy-start.1 = (s32[2]{0:T(128)S(1)}, s32[2]{0:T(128)}, u32[]{:S(2)}) copy-start(s32[2]{0:T(128)} %copy-done) | copy-start | bytes 28
  119.7 7.4 %collective-permute-start.8 = (bf16[576,128]{1,0:T(8,128)(2,1)S(1)}, bf16[576,128]{1,0:T(8,128)(2,1)S(1)}, u32[]{:S(2)}, u32[]{:S(2)}) collective-permute-start(bf16[576,128]{1,0:T(8,128)(2,1)S(1)} %get-tuple-element.55), channel_id=1, source_target_pairs={{0,2},{2,4},{4,6},{6,0},{1,3},{3,5},{5,7},{7,1},{8,10},{10,12},{12... | collective-permute-start | bytes 442376 | tf_op jit(solution)/shard_map/ppermute | solution.py:461
  120.4 6.9 %collective-permute-start.10 = (bf16[576,128]{1,0:T(8,128)(2,1)S(1)}, bf16[576,128]{1,0:T(8,128)(2,1)S(1)}, u32[]{:S(2)}, u32[]{:S(2)}) collective-permute-start(bf16[576,128]{1,0:T(8,128)(2,1)S(1)} %get-tuple-element.56), channel_id=1, source_target_pairs={{0,6},{2,0},{4,2},{6,4},{1,7},{3,1},{5,3},{7,5},{8,14},{10,8},{12,... | collective-permute-start | bytes 442376 | tf_op jit(solution)/shard_map/ppermute | solution.py:461
  123.1 6.6 %collective-permute-start.9 = (bf16[576,128]{1,0:T(8,128)(2,1)S(1)}, bf16[576,128]{1,0:T(8,128)(2,1)S(1)}, u32[]{:S(2)}, u32[]{:S(2)}) collective-permute-start(bf16[576,128]{1,0:T(8,128)(2,1)S(1)} %get-tuple-element.57), channel_id=1, source_target_pairs={{0,4},{2,6},{4,0},{6,2},{1,5},{3,7},{5,1},{7,3},{8,12},{10,14},{12... | collective-permute-start | bytes 442376 | tf_op jit(solution)/shard_map/ppermute | solution.py:461
  129.8 9.3 %collective-permute-start.11 = (bf16[64,128]{1,0:T(8,128)(2,1)S(1)}, bf16[64,128]{1,0:T(8,128)(2,1)S(1)}, u32[]{:S(2)}, u32[]{:S(2)}) collective-permute-start(bf16[64,128]{1,0:T(8,128)(2,1)S(1)} %slice.79), channel_id=1, source_target_pairs={{7,8},{15,16},{23,24},{31,32},{39,40},{47,48},{55,56},{63,64},{71,... | collective-permute-start | bytes 49160 | tf_op jit(solution)/shard_map/ppermute | solution.py:464
  139.8 2.8 %collective-permute-start.12 = (bf16[36,128,128]{2,1,0:T(8,128)(2,1)S(1)}, bf16[36,128,128]{2,1,0:T(8,128)(2,1)S(1)}, u32[]{:S(2)}, u32[]{:S(2)}) collective-permute-start(bf16[36,128,128]{2,1,0:T(8,128)(2,1)S(1)} %bitcast.29), channel_id=1, source_target_pairs={{0,1},{1,0},{2,3},{3,2},{4,5},{5,4},{6,7},{7,6},{8,9},{9,8},{10,11... | collective-permute-start | bytes 3538952 | tf_op jit(solution)/shard_map/ppermute | solution.py:331
  (5 other events, 3.2 us)
